TPU v7x, 32 devices: a whole 2x2x4 slice. The times are simulated.
32 devices in a mesh: row: 4 (over y, x), col: 8 (over z, core).
Axes of the slice: x: 2, y: 2, z: 4, core: 2. Of those that a mesh axis runs over, the one named last changes fastest.
Arguments:
- latent: bfloat16 [8192, 1408], P(('row', 'col')), may hold values from -6 to 6
- skips: bfloat16 [2, 8192, 1408], P(None, ('row', 'col')), may hold values from -6 to 6
- cond: bfloat16 [8, 1408], P('row'), may hold values from -6 to 6
- text: bfloat16 [8, 333, 1024], P('row', None, 'col'), may hold values from -6 to 6
- skip_gain: float32 [2, 2816], replicated, may hold values from 0.1 to 1.9
- attn_gain: float32 [2, 2, 1408], replicated, may hold values from 0.1 to 1.9
- ffn_gain: float32 [2, 1408], replicated, may hold values from 0.1 to 1.9
- skip_w: bfloat16 [2, 2816, 1408], P(None, 'row', 'col'), may hold values from -0.109375 to 0.109375
- mod_w: bfloat16 [2, 1408, 1408], P(None, 'row', 'col'), may hold values from -0.15625 to 0.15625
- qkv_w: bfloat16 [2, 3, 1408, 1408], P(None, None, 'row', 'col'), may hold values from -0.15625 to 0.15625
- out_w: bfloat16 [2, 1408, 1408], P(None, 'col', 'row'), may hold values from -2.5 to 2.5
- cq_w: bfloat16 [2, 1408, 1408], P(None, 'row', 'col'), may hold values from -0.15625 to 0.15625
- ckv_w: bfloat16 [2, 2, 1024, 1408], P(None, None, 'row', 'col'), may hold values from -0.1875 to 0.1875
- cout_w: bfloat16 [2, 1408, 1408], P(None, 'col', 'row'), may hold values from -1.75 to 1.75
- fc1_w: bfloat16 [2, 1408, 6144], P(None, 'row', 'col'), may hold values from -0.15625 to 0.15625
- fc2_w: bfloat16 [2, 6144, 1408], P(None, 'col', 'row'), may hold values from -0.078125 to 0.078125
- cotangent: bfloat16 [8192, 1408], P(('row', 'col')), may hold values from -6 to 6
Outputs:
- mixed: float32 [8192, 1408], P(('row', 'col'))
- latent_grad: float32 [8192, 1408], P(('row', 'col'))
- skip_grad: float32 [2, 8192, 1408], P(None, ('row', 'col'))
- text_grad: float32 [8, 333, 1024], P('row', None, 'col')
- skip_gain_grad: float32 [2, 2816], replicated
- attn_gain_grad: float32 [2, 2, 1408], replicated
- ffn_gain_grad: float32 [2, 1408], replicated
- skip_w_grad: float32 [2, 2816, 1408], P(None, 'row', 'col')
- mod_w_grad: float32 [2, 1408, 1408], P(None, 'row', 'col')
- qkv_w_grad: float32 [2, 3, 1408, 1408], P(None, None, 'row', 'col')
- out_w_grad: float32 [2, 1408, 1408], P(None, 'col', 'row')
- cq_w_grad: float32 [2, 1408, 1408], P(None, 'row', 'col')
- ckv_w_grad: float32 [2, 2, 1024, 1408], P(None, None, 'row', 'col')
- cout_w_grad: float32 [2, 1408, 1408], P(None, 'col', 'row')
- fc1_w_grad: float32 [2, 1408, 6144], P(None, 'row', 'col')
- fc2_w_grad: float32 [2, 6144, 1408], P(None, 'col', 'row')
All inputs are finite; a program needn't handle non-finite values.
Results may differ from a plain program's by a relative error of at most 0.025.
Values may be sent and summed in bfloat16 or wider, within the bound.
A program may use at most 384 MiB of HBM per device.

v0:
```python
import jax
import jax.numpy as jnp
from jax import lax
from jax.sharding import PartitionSpec as P

HD = 88
SIDE = 32
SEQ = 1024


HIGHEST = lax.Precision.HIGHEST
EPSILON = 1e-06


def norm_rows(value):
    center = value - jnp.mean(value, axis=-1, keepdims=True)
    spread = jnp.mean(center * center, axis=-1, keepdims=True)
    return center * lax.rsqrt(spread + EPSILON)


def gained_norm(value, gain):
    return norm_rows(value) * gain


def silu(value):
    return value * jax.nn.sigmoid(value)


def gelu_tanh(value):
    inner = 0.7978845608028654 * (value + 0.044715 * value * value * value)
    return 0.5 * value * (1.0 + jnp.tanh(inner))


def rotary_tables():
    place = jnp.arange(SEQ, dtype=jnp.int32)
    grid_row = (place // SIDE).astype(jnp.float32)
    grid_col = (place % SIDE).astype(jnp.float32)
    pair = jnp.arange(HD // 2, dtype=jnp.int32)
    quarter = HD // 4
    power = (pair % quarter).astype(jnp.float32) * (4.0 / HD)
    freq = jnp.exp(-power * jnp.log(10000.0))
    coordinate = jnp.where(pair[None, :] < quarter, grid_row[:, None], grid_col[:, None])
    angle = coordinate * freq[None, :]
    return (jnp.cos(angle), jnp.sin(angle))


def rotate(value, cos_table, sin_table):
    pairs = value.reshape(value.shape[:-1] + (value.shape[-1] // 2, 2))
    even = pairs[..., 0]
    odd = pairs[..., 1]
    cosine = cos_table[:, None, :]
    sine = sin_table[:, None, :]
    turned = jnp.stack([even * cosine - odd * sine, even * sine + odd * cosine], axis=-1)
    return turned.reshape(value.shape)


def contract_rows(left, right):
    return lax.dot_general(
        left, right, (((0,), (0,)), ((), ())), preferred_element_type=jnp.float32
    )


def times_transposed(left, right):
    return lax.dot_general(
        left, right, (((1,), (1,)), ((), ())), preferred_element_type=jnp.float32
    )


def attend_forward(inputs):
    query, keys, values = inputs
    scores = jnp.einsum("qhe,khe->hqk", query, keys, preferred_element_type=jnp.float32) * HD ** (
        -0.5
    )
    highest = jnp.max(scores, axis=-1, keepdims=True)
    expo = jnp.exp(scores - highest)
    total = jnp.sum(expo, axis=-1, keepdims=True)
    probs_low = (expo / total).astype(jnp.bfloat16)
    result = jnp.einsum("hqk,khe->qhe", probs_low, values, preferred_element_type=jnp.float32)
    return (result, (highest + jnp.log(total))[..., 0])


def attend_backward(inputs):
    query, keys, values, logsum, grad_low = inputs
    scores = jnp.einsum("qhe,khe->hqk", query, keys, preferred_element_type=jnp.float32) * HD ** (
        -0.5
    )
    probs = jnp.exp(scores - logsum[..., None])
    probs_low = probs.astype(jnp.bfloat16)
    values_grad = jnp.einsum(
        "hqk,qhe->khe", probs_low, grad_low, preferred_element_type=jnp.float32
    )
    probs_grad = jnp.einsum("qhe,khe->hqk", grad_low, values, preferred_element_type=jnp.float32)
    scores_grad = probs * (probs_grad - jnp.sum(probs * probs_grad, axis=-1, keepdims=True))
    scores_low = scores_grad.astype(jnp.bfloat16)
    query_grad = jnp.einsum(
        "hqk,khe->qhe", scores_low, keys, preferred_element_type=jnp.float32
    ) * HD ** (-0.5)
    keys_grad = jnp.einsum(
        "hqk,qhe->khe", scores_low, query, preferred_element_type=jnp.float32
    ) * HD ** (-0.5)
    return (query_grad, keys_grad, values_grad)


def on_device(
    latent,
    skips,
    cond,
    text,
    skip_gain,
    attn_gain,
    ffn_gain,
    skip_w,
    mod_w,
    qkv_w,
    out_w,
    cq_w,
    ckv_w,
    cout_w,
    fc1_w,
    fc2_w,
    cotangent,
):
    col_count = lax.axis_size("col")
    tok_dev = latent.shape[0]
    row_tokens = tok_dev * col_count
    seq_count = cond.shape[0]
    width = latent.shape[1]
    local_width = qkv_w.shape[3]
    local_heads = local_width // HD
    layer_count = skip_w.shape[0]
    cos_table, sin_table = rotary_tables()
    position = lax.axis_index("col") * tok_dev + jnp.arange(tok_dev, dtype=jnp.int32)
    member = (position[:, None] // SEQ == jnp.arange(seq_count, dtype=jnp.int32)[None, :]).astype(
        jnp.float32
    )
    cond_low = silu(cond.astype(jnp.float32)).astype(jnp.bfloat16)
    text_full = lax.all_gather(text, "col", axis=2, tiled=True)
    heads_shape = (seq_count, SEQ, local_heads, HD)
    text_shape = (seq_count, text_full.shape[1], local_heads, HD)
    flat_shape = (row_tokens, local_width)

    def self_prep(query, keys):
        return (
            rotate(norm_rows(query), cos_table, sin_table),
            rotate(norm_rows(keys), cos_table, sin_table),
        )

    def cross_prep(query, keys):
        return (rotate(norm_rows(query), cos_table, sin_table), norm_rows(keys))

    def first_fn(resid, gain, shift):
        return norm_rows(resid) * gain + jnp.dot(member, shift, precision=HIGHEST)

    def gather_weights(layer_idx):
        return (
            lax.all_gather(skip_w[layer_idx], "row", axis=0, tiled=True),
            lax.all_gather(mod_w[layer_idx], "row", axis=0, tiled=True),
            lax.all_gather(qkv_w[layer_idx], "row", axis=1, tiled=True),
            lax.all_gather(out_w[layer_idx], "row", axis=1, tiled=True),
            lax.all_gather(cq_w[layer_idx], "row", axis=0, tiled=True),
            lax.all_gather(ckv_w[layer_idx], "row", axis=1, tiled=True),
            lax.all_gather(cout_w[layer_idx], "row", axis=1, tiled=True),
            lax.all_gather(fc1_w[layer_idx], "row", axis=0, tiled=True),
            lax.all_gather(fc2_w[layer_idx], "row", axis=1, tiled=True),
        )

    def spread_rows(value, product):
        return product(lax.all_gather(value, "col", axis=0, tiled=True), jnp.int32(0))

    def sum_rows(term):
        return lax.psum_scatter(
            term(jnp.int32(0), tok_dev * lax.axis_size("col")).astype(jnp.bfloat16),
            "col",
            scatter_dimension=0,
            tiled=True,
        ).astype(jnp.float32)

    def fold_grads(value, fold, init):
        return fold(init, lax.all_gather(value, "col", axis=0, tiled=True), jnp.int32(0))

    def fold_inputs(value, fold, init):
        return fold(init, lax.all_gather(value, "col", axis=0, tiled=True), jnp.int32(0))

    def sum_grads(term):
        return lax.psum_scatter(
            term(jnp.int32(0), tok_dev * lax.axis_size("col")).astype(jnp.bfloat16),
            "col",
            scatter_dimension=0,
            tiled=True,
        ).astype(jnp.float32)

    def row_product(weight):

        def product(piece, start):
            return jnp.dot(piece, weight, preferred_element_type=jnp.float32)

        return product

    def row_term(left_low, weight):

        def term(start, count):
            return jnp.dot(left_low, weight, preferred_element_type=jnp.float32)

        return term

    def back_term(grad_low, weight):

        def term(start, count):
            return times_transposed(grad_low, weight)

        return term

    def input_fold(grad_low):

        def fold(carry, piece, start):
            return contract_rows(piece, grad_low)

        return fold

    def out_fold(left_low, weight):

        def fold(carry, piece, start):
            weight_grad = contract_rows(left_low, piece)
            left_grad = times_transposed(piece, weight)
            return (weight_grad, left_grad)

        return fold

    def forward_layer(layer_idx, resid_in, weights):
        w_skip, w_mod, w_qkv, w_out, w_query, w_text, w_cross, w_up, w_down = weights
        joined = jnp.concatenate([resid_in, skips[layer_idx].astype(jnp.float32)], axis=1)
        skip_low = gained_norm(joined, skip_gain[layer_idx]).astype(jnp.bfloat16)
        skip_proj = spread_rows(skip_low, row_product(w_skip))
        resid_one = lax.all_to_all(
            skip_proj.astype(jnp.bfloat16), "col", split_axis=0, concat_axis=1, tiled=True
        ).astype(skip_proj.dtype)
        shift = lax.all_gather(
            jnp.dot(cond_low, w_mod, preferred_element_type=jnp.float32), "col", axis=1, tiled=True
        )
        first_low = first_fn(resid_one, attn_gain[layer_idx, 0], shift).astype(jnp.bfloat16)

        def qkv_product(piece, start):
            return jnp.einsum("td,kdc->tkc", piece, w_qkv, preferred_element_type=jnp.float32)

        projected = spread_rows(first_low, qkv_product)
        query_raw = projected[:, 0].reshape(heads_shape)
        keys_raw = projected[:, 1].reshape(heads_shape)
        values_raw = projected[:, 2].reshape(heads_shape)
        query_rot, keys_rot = self_prep(query_raw, keys_raw)
        self_out, self_lse = lax.map(
            attend_forward,
            (
                query_rot.astype(jnp.bfloat16),
                keys_rot.astype(jnp.bfloat16),
                values_raw.astype(jnp.bfloat16),
            ),
        )
        self_low = self_out.reshape(flat_shape).astype(jnp.bfloat16)
        resid_two = resid_one + sum_rows(row_term(self_low, w_out))
        third_low = gained_norm(resid_two, attn_gain[layer_idx, 1]).astype(jnp.bfloat16)
        cross_query = spread_rows(third_low, row_product(w_query)).reshape(heads_shape)
        text_proj = jnp.einsum(
            "snt,ktc->sknc", text_full, w_text, preferred_element_type=jnp.float32
        )
        cross_keys = text_proj[:, 0].reshape(text_shape)
        cross_values = text_proj[:, 1].reshape(text_shape)
        cross_rot, cross_norm = cross_prep(cross_query, cross_keys)
        cross_out, cross_lse = lax.map(
            attend_forward,
            (
                cross_rot.astype(jnp.bfloat16),
                cross_norm.astype(jnp.bfloat16),
                cross_values.astype(jnp.bfloat16),
            ),
        )
        cross_low = cross_out.reshape(flat_shape).astype(jnp.bfloat16)
        resid_three = resid_two + sum_rows(row_term(cross_low, w_cross))
        second_low = gained_norm(resid_three, ffn_gain[layer_idx]).astype(jnp.bfloat16)
        hidden = spread_rows(second_low, row_product(w_up))
        act_low = gelu_tanh(hidden).astype(jnp.bfloat16)
        resid_out = resid_three + sum_rows(row_term(act_low, w_down))
        saved = (
            resid_in,
            resid_one,
            resid_two,
            resid_three,
            shift,
            query_raw,
            keys_raw,
            values_raw,
            self_low,
            self_lse,
            cross_query,
            cross_keys,
            cross_values,
            cross_low,
            cross_lse,
            hidden,
        )
        return (resid_out, saved)

    resid = latent.astype(jnp.float32)
    layer_inputs = []
    kept = []
    for layer_idx in range(layer_count):
        layer_inputs.append(resid)
        weights = gather_weights(layer_idx)
        resid, saved = forward_layer(layer_idx, resid, weights)
        kept.append((weights, saved))
    grad = cotangent.astype(jnp.float32)
    text_grad = jnp.zeros(text_full.shape, jnp.float32)
    weight_store = [None] * layer_count
    gain_store = [None] * layer_count
    skip_store = [None] * layer_count
    for layer_idx in range(layer_count - 1, -1, -1):
        weights = gather_weights(layer_idx)
        unused, saved = forward_layer(layer_idx, layer_inputs[layer_idx], weights)
        backward_text_grad = text_grad
        (
            backward_w_skip,
            backward_w_mod,
            backward_w_qkv,
            backward_w_out,
            backward_w_query,
            backward_w_text,
            backward_w_cross,
            backward_w_up,
            backward_w_down,
        ) = weights
        (
            backward_resid_in,
            backward_resid_one,
            backward_resid_two,
            backward_resid_three,
            backward_shift,
            backward_query_raw,
            backward_keys_raw,
            backward_values_raw,
            backward_self_low,
            backward_self_lse,
            backward_cross_query,
            backward_cross_keys,
            backward_cross_values,
            backward_cross_low,
            backward_cross_lse,
            backward_hidden,
        ) = saved
        second, second_pull = jax.vjp(gained_norm, backward_resid_three, ffn_gain[layer_idx])
        activation, act_pull = jax.vjp(gelu_tanh, backward_hidden)
        backward_act_low = activation.astype(jnp.bfloat16)
        down_grad, act_grad = fold_grads(
            grad.astype(jnp.bfloat16),
            out_fold(backward_act_low, backward_w_down),
            (
                jnp.zeros(backward_w_down.shape, jnp.float32),
                jnp.zeros(backward_hidden.shape, jnp.float32),
            ),
        )
        hidden_grad = act_pull(act_grad)[0].astype(jnp.bfloat16)
        up_grad = fold_inputs(
            second.astype(jnp.bfloat16),
            input_fold(hidden_grad),
            jnp.zeros(backward_w_up.shape, jnp.float32),
        )
        norm_part, gain_ffn = second_pull(sum_grads(back_term(hidden_grad, backward_w_up)))
        grad_three = grad + norm_part
        cross_w_grad, cross_out_grad = fold_grads(
            grad_three.astype(jnp.bfloat16),
            out_fold(backward_cross_low, backward_w_cross),
            (jnp.zeros(backward_w_cross.shape, jnp.float32), jnp.zeros(flat_shape, jnp.float32)),
        )
        (backward_cross_rot, backward_cross_norm), cross_pull = jax.vjp(
            cross_prep, backward_cross_query, backward_cross_keys
        )
        rot_grad, norm_grad, value_grad = lax.map(
            attend_backward,
            (
                backward_cross_rot.astype(jnp.bfloat16),
                backward_cross_norm.astype(jnp.bfloat16),
                backward_cross_values.astype(jnp.bfloat16),
                backward_cross_lse,
                cross_out_grad.astype(jnp.bfloat16).reshape(heads_shape),
            ),
        )
        query_grad, keys_grad = cross_pull((rot_grad, norm_grad))
        query_low_grad = query_grad.reshape(flat_shape).astype(jnp.bfloat16)
        text_low_grad = jnp.stack(
            [
                keys_grad.reshape(seq_count, -1, local_width),
                value_grad.reshape(seq_count, -1, local_width),
            ],
            axis=1,
        ).astype(jnp.bfloat16)
        third, third_pull = jax.vjp(gained_norm, backward_resid_two, attn_gain[layer_idx, 1])
        query_w_grad = fold_inputs(
            third.astype(jnp.bfloat16),
            input_fold(query_low_grad),
            jnp.zeros(backward_w_query.shape, jnp.float32),
        )
        text_w_grad = jnp.einsum(
            "snt,sknc->ktc", text_full, text_low_grad, preferred_element_type=jnp.float32
        )
        backward_text_grad = backward_text_grad + jnp.einsum(
            "sknc,ktc->snt", text_low_grad, backward_w_text, preferred_element_type=jnp.float32
        )
        norm_part, gain_cross = third_pull(sum_grads(back_term(query_low_grad, backward_w_query)))
        grad_two = grad_three + norm_part
        self_w_grad, self_out_grad = fold_grads(
            grad_two.astype(jnp.bfloat16),
            out_fold(backward_self_low, backward_w_out),
            (jnp.zeros(backward_w_out.shape, jnp.float32), jnp.zeros(flat_shape, jnp.float32)),
        )
        (backward_query_rot, backward_keys_rot), self_pull = jax.vjp(
            self_prep, backward_query_raw, backward_keys_raw
        )
        rot_query_grad, rot_keys_grad, value_grad = lax.map(
            attend_backward,
            (
                backward_query_rot.astype(jnp.bfloat16),
                backward_keys_rot.astype(jnp.bfloat16),
                backward_values_raw.astype(jnp.bfloat16),
                backward_self_lse,
                self_out_grad.astype(jnp.bfloat16).reshape(heads_shape),
            ),
        )
        query_grad, keys_grad = self_pull((rot_query_grad, rot_keys_grad))
        qkv_low_grad = jnp.stack(
            [
                query_grad.reshape(flat_shape),
                keys_grad.reshape(flat_shape),
                value_grad.reshape(flat_shape),
            ],
            axis=1,
        ).astype(jnp.bfloat16)
        first, first_pull = jax.vjp(
            first_fn, backward_resid_one, attn_gain[layer_idx, 0], backward_shift
        )

        def qkv_fold(carry, piece, start):
            return jnp.einsum(
                "td,tkc->kdc", piece, qkv_low_grad, preferred_element_type=jnp.float32
            )

        def qkv_term(start, count):
            return jnp.einsum(
                "tkc,kdc->td", qkv_low_grad, backward_w_qkv, preferred_element_type=jnp.float32
            )

        qkv_w_grad = fold_inputs(
            first.astype(jnp.bfloat16), qkv_fold, jnp.zeros(backward_w_qkv.shape, jnp.float32)
        )
        norm_part, gain_self, shift_part = first_pull(sum_grads(qkv_term))
        shift_grad = lax.psum_scatter(shift_part, "col", scatter_dimension=1, tiled=True)
        mod_w_grad = contract_rows(cond_low, shift_grad.astype(jnp.bfloat16))
        grad_one = grad_two + norm_part
        skip_proj_grad = lax.all_to_all(
            grad_one.astype(jnp.bfloat16), "col", split_axis=1, concat_axis=0, tiled=True
        )
        backward_joined = jnp.concatenate(
            [backward_resid_in, skips[layer_idx].astype(jnp.float32)], axis=1
        )
        skip_norm, skip_pull = jax.vjp(gained_norm, backward_joined, skip_gain[layer_idx])
        skip_w_grad = fold_inputs(
            skip_norm.astype(jnp.bfloat16),
            input_fold(skip_proj_grad),
            jnp.zeros(backward_w_skip.shape, jnp.float32),
        )
        joined_part, gain_skip = skip_pull(sum_grads(back_term(skip_proj_grad, backward_w_skip)))
        weight_grads = (
            skip_w_grad,
            mod_w_grad,
            qkv_w_grad,
            self_w_grad,
            query_w_grad,
            text_w_grad,
            cross_w_grad,
            up_grad,
            down_grad,
        )
        gain_grads = (gain_skip, jnp.stack([gain_self, gain_cross]), gain_ffn)
        grad = joined_part[:, :width]
        skip_part = joined_part[:, width:]
        text_grad = backward_text_grad
        weight_store[layer_idx] = weight_grads
        gain_store[layer_idx] = gain_grads
        skip_store[layer_idx] = skip_part
    weight_full = tuple(
        (
            jnp.stack([weight_store[level][slot] for level in range(layer_count)])
            for slot in range(9)
        )
    )
    weight_shards = (
        lax.psum_scatter(
            weight_full[0].astype(jnp.bfloat16), "row", scatter_dimension=1, tiled=True
        ).astype(jnp.float32),
        lax.psum_scatter(
            weight_full[1].astype(jnp.bfloat16), "row", scatter_dimension=1, tiled=True
        ).astype(jnp.float32),
        lax.psum_scatter(
            weight_full[2].astype(jnp.bfloat16), "row", scatter_dimension=2, tiled=True
        ).astype(jnp.float32),
        lax.psum_scatter(
            weight_full[3].astype(jnp.bfloat16), "row", scatter_dimension=2, tiled=True
        ).astype(jnp.float32),
        lax.psum_scatter(
            weight_full[4].astype(jnp.bfloat16), "row", scatter_dimension=1, tiled=True
        ).astype(jnp.float32),
        lax.psum_scatter(
            weight_full[5].astype(jnp.bfloat16), "row", scatter_dimension=2, tiled=True
        ).astype(jnp.float32),
        lax.psum_scatter(
            weight_full[6].astype(jnp.bfloat16), "row", scatter_dimension=2, tiled=True
        ).astype(jnp.float32),
        lax.psum_scatter(
            weight_full[7].astype(jnp.bfloat16), "row", scatter_dimension=1, tiled=True
        ).astype(jnp.float32),
        lax.psum_scatter(
            weight_full[8].astype(jnp.bfloat16), "row", scatter_dimension=2, tiled=True
        ).astype(jnp.float32),
    )
    skip_gain_part = jnp.stack([gain_store[level][0] for level in range(layer_count)])
    attn_gain_part = jnp.stack([gain_store[level][1] for level in range(layer_count)])
    ffn_gain_part = jnp.stack([gain_store[level][2] for level in range(layer_count)])
    gain_totals = lax.psum((skip_gain_part, attn_gain_part, ffn_gain_part), ("row", "col"))
    text_shard = lax.psum_scatter(
        text_grad.astype(jnp.bfloat16), "col", scatter_dimension=2, tiled=True
    ).astype(jnp.float32)
    skip_grad = jnp.stack(skip_store)
    return (
        resid,
        grad,
        skip_grad,
        text_shard,
        gain_totals[0],
        gain_totals[1],
        gain_totals[2],
        weight_shards[0],
        weight_shards[1],
        weight_shards[2],
        weight_shards[3],
        weight_shards[4],
        weight_shards[5],
        weight_shards[6],
        weight_shards[7],
        weight_shards[8],
    )


def solution(mesh):
    return jax.shard_map(
        on_device,
        mesh=mesh,
        in_specs=(
            P(("row", "col"), None),
            P(None, ("row", "col"), None),
            P("row", None),
            P("row", None, "col"),
            P(),
            P(),
            P(),
            P(None, "row", "col"),
            P(None, "row", "col"),
            P(None, None, "row", "col"),
            P(None, "col", "row"),
            P(None, "row", "col"),
            P(None, None, "row", "col"),
            P(None, "col", "row"),
            P(None, "row", "col"),
            P(None, "col", "row"),
            P(("row", "col"), None),
        ),
        out_specs=(
            P(("row", "col"), None),
            P(("row", "col"), None),
            P(None, ("row", "col"), None),
            P("row", None, "col"),
            P(),
            P(),
            P(),
            P(None, "row", "col"),
            P(None, "row", "col"),
            P(None, None, "row", "col"),
            P(None, "col", "row"),
            P(None, "row", "col"),
            P(None, None, "row", "col"),
            P(None, "col", "row"),
            P(None, "row", "col"),
            P(None, "col", "row"),
        ),
        check_vma=False,
    )
```

profile of v0, /device:TPU:0, one launch (start us, length us, event | category | flops | bytes accessed | tf_op | source)
XLA Modules:
  0.0 3878.2 jit_solution(18075194317293776969)
XLA Ops:
  20.2 30.9 all-gather
  57.2 70.4 %all-gather.46.cloned.1.call-done = bf16[2048,2816]{1,0:T(8,128)(2,1)} async-done(((bf16[256,2816]{1,0:T(8,128)(2,1)}), bf16[2048,2816]{1,0:T(8,128)(2,1)}) %all-gather.46.cloned.1.call-update) | async-done | bytes 11534352 | tf_op jit(solution)/shard_map/all_gather | solution.py:168
  144.1 25.4 all-gather.1
  192.2 18.1 all-gather.3
  218.6 36.6 all-gather.48.cloned.1.call-done
  292.0 18.9 while.144
  333.7 57.2 %reduce-scatter.48.cloned.1.call-done = bf16[256,1408]{1,0:T(8,128)(2,1)} async-done(((bf16[2048,1408]{1,0:T(8,128)(2,1)}), bf16[256,1408]{1,0:T(8,128)(2,1)}) %reduce-scatter.48.cloned.1.call-update) | async-done | bytes 720912 | tf_op jit(solution)/shard_map/reduce_scatter | solution.py:171
  392.3 63.7 %reduce-scatter.72.cloned.1.call-done = bf16[256,1408]{1,0:T(8,128)(2,1)} async-done(((bf16[2048,1408]{1,0:T(8,128)(2,1)}), bf16[256,1408]{1,0:T(8,128)(2,1)}) %reduce-scatter.72.cloned.1.call-update) | async-done | bytes 720912 | tf_op jit(solution)/shard_map/reduce_scatter | solution.py:171
  462.5 15.6 all-gather.5
  482.8 15.5 all-gather.6
  532.4 48.1 %all-gather.76.cloned.1.call-done = bf16[2048,1408]{1,0:T(8,128)(2,1)} async-done(((bf16[256,1408]{1,0:T(8,128)(2,1)}), bf16[2048,1408]{1,0:T(8,128)(2,1)}) %all-gather.76.cloned.1.call-update) | async-done | bytes 5767184 | tf_op jit(solution)/shard_map/all_gather | solution.py:168
  644.9 44.5 %reduce-scatter.50.cloned.1.call-done = bf16[256,1408]{1,0:T(8,128)(2,1)} async-done(((bf16[2048,1408]{1,0:T(8,128)(2,1)}), bf16[256,1408]{1,0:T(8,128)(2,1)}) %reduce-scatter.50.cloned.1.call-update) | async-done | bytes 720912 | tf_op jit(solution)/shard_map/reduce_scatter | solution.py:171
  691.4 63.5 %reduce-scatter.74.cloned.1.call-done = bf16[256,1408]{1,0:T(8,128)(2,1)} async-done(((bf16[2048,1408]{1,0:T(8,128)(2,1)}), bf16[256,1408]{1,0:T(8,128)(2,1)}) %reduce-scatter.74.cloned.1.call-update) | async-done | bytes 720912 | tf_op jit(solution)/shard_map/reduce_scatter | solution.py:171
  759.4 32.0 all-gather.86.cloned.1.call-done
  791.4 62.4 %all-gather.54.cloned.1.call-done = bf16[2048,1408]{1,0:T(8,128)(2,1)} async-done(((bf16[256,1408]{1,0:T(8,128)(2,1)}), bf16[2048,1408]{1,0:T(8,128)(2,1)}) %all-gather.54.cloned.1.call-update) | async-done | bytes 5767184 | tf_op jit(solution)/shard_map/all_gather | solution.py:168
  863.1 27.4 all-gather.88.cloned.1.call-done
  900.4 64.9 %reduce-scatter.52.cloned.1.call-done = bf16[256,1408]{1,0:T(8,128)(2,1)} async-done(((bf16[2048,1408]{1,0:T(8,128)(2,1)}), bf16[256,1408]{1,0:T(8,128)(2,1)}) %reduce-scatter.52.cloned.1.call-update) | async-done | bytes 720912 | tf_op jit(solution)/shard_map/reduce_scatter | solution.py:171
  972.0 25.7 all-gather.9
  1003.7 72.3 %all-gather.56.cloned.1.call-done = bf16[2048,2816]{1,0:T(8,128)(2,1)} async-done(((bf16[256,2816]{1,0:T(8,128)(2,1)}), bf16[2048,2816]{1,0:T(8,128)(2,1)}) %all-gather.56.cloned.1.call-update) | async-done | bytes 11534352 | tf_op jit(solution)/shard_map/all_gather | solution.py:168
  1091.1 24.1 all-gather.10
  1136.8 19.0 all-gather.12
  1163.0 39.2 %all-gather.58.cloned.1.call-done = bf16[2048,1408]{1,0:T(8,128)(2,1)} async-done(((bf16[256,1408]{1,0:T(8,128)(2,1)}), bf16[2048,1408]{1,0:T(8,128)(2,1)}) %all-gather.58.cloned.1.call-update) | async-done | bytes 5767184 | tf_op jit(solution)/shard_map/all_gather | solution.py:168
  1264.5 63.3 %reduce-scatter.60.cloned.1.call-done = bf16[256,1408]{1,0:T(8,128)(2,1)} async-done(((bf16[2048,1408]{1,0:T(8,128)(2,1)}), bf16[256,1408]{1,0:T(8,128)(2,1)}) %reduce-scatter.60.cloned.1.call-update) | async-done | bytes 720912 | tf_op jit(solution)/shard_map/reduce_scatter | solution.py:171
  1332.2 15.8 all-gather.14
  1352.2 15.2 all-gather.15
  1425.8 64.0 %reduce-scatter.62.cloned.1.call-done = bf16[256,1408]{1,0:T(8,128)(2,1)} async-done(((bf16[2048,1408]{1,0:T(8,128)(2,1)}), bf16[256,1408]{1,0:T(8,128)(2,1)}) %reduce-scatter.62.cloned.1.call-update) | async-done | bytes 720912 | tf_op jit(solution)/shard_map/reduce_scatter | solution.py:171
  1494.5 31.7 all-gather.92.cloned.1.call-done
  1526.2 62.5 %all-gather.68.cloned.1.call-done = bf16[2048,1408]{1,0:T(8,128)(2,1)} async-done(((bf16[256,1408]{1,0:T(8,128)(2,1)}), bf16[2048,1408]{1,0:T(8,128)(2,1)}) %all-gather.68.cloned.1.call-update) | async-done | bytes 5767184 | tf_op jit(solution)/shard_map/all_gather | solution.py:168
  1598.3 27.3 all-gather.94.cloned.1.call-done
  1625.6 62.0 %all-gather.64.cloned.1.call-done = bf16[2048,1408]{1,0:T(8,128)(2,1)} async-done(((bf16[256,1408]{1,0:T(8,128)(2,1)}), bf16[2048,1408]{1,0:T(8,128)(2,1)}) %all-gather.64.cloned.1.call-update) | async-done | bytes 5767184 | tf_op jit(solution)/shard_map/all_gather | solution.py:179
  1708.6 63.7 %reduce-scatter.64.cloned.1.call-done = bf16[256,1408]{1,0:T(8,128)(2,1)} async-done(((bf16[2048,1408]{1,0:T(8,128)(2,1)}), bf16[256,1408]{1,0:T(8,128)(2,1)}) %reduce-scatter.64.cloned.1.call-update) | async-done | bytes 720912 | tf_op jit(solution)/shard_map/reduce_scatter | solution.py:185
  1782.7 53.1 %all-gather.70.cloned.1.call-done = bf16[2048,1408]{1,0:T(8,128)(2,1)} async-done(((bf16[256,1408]{1,0:T(8,128)(2,1)}), bf16[2048,1408]{1,0:T(8,128)(2,1)}) %all-gather.70.cloned.1.call-update) | async-done | bytes 5767184 | tf_op jit(solution)/shard_map/all_gather | solution.py:179
  1844.4 47.6 %while.150 = (s32[]{:T(128)}, f32[2,1024,2,88]{1,0,3,2:T(2,128)}, f32[2,333,2,88]{1,3,2,0:T(8,128)}, bf16[2,333,2,88]{1,3,2,0:T(8,128)(2,1)}, bf16[2,333,2,88]{1...) while((s32[]{:T(128)}, f32[2,1024,2,88]{1,0,3,2:T(2,128)}, ...), condition=%wide.region_77.78_spmd, body=%wide.region_75.77_spmd.sunk | while | flops 605838592 | bytes 35741892 | solution.py:375
  1849.9 13.3 dynamic_update_slice.127
  1873.7 13.3 dynamic_update_slice.127
  1907.5 63.6 %reduce-scatter.66.cloned.1.call-done = bf16[256,1408]{1,0:T(8,128)(2,1)} async-done(((bf16[2048,1408]{1,0:T(8,128)(2,1)}), bf16[256,1408]{1,0:T(8,128)(2,1)}) %reduce-scatter.66.cloned.1.call-update) | async-done | bytes 720912 | tf_op jit(solution)/shard_map/reduce_scatter | solution.py:185
  1977.6 18.9 while.146
  2023.6 19.2 all-gather.72.cloned.1.call-done
  2052.1 91.8 %while.151 = (s32[]{:T(128)}, f32[2,1024,2,88]{1,0,3,2:T(2,128)}, f32[2,1024,2,88]{1,0,3,2:T(2,128)}, bf16[2,1024,2,88]{1,3,2,0:T(8,128)(2,1)}, bf16[2,1024,2,88...) while((s32[]{:T(128)}, f32[2,1024,2,88]{1,0,3,2:T(2,128)}, ...), condition=%wide.region_85.86_spmd, body=%wide.region_83.85_spmd.sunk | while | flops 1871017984 | bytes 123759784 | solution.py:416
  2079.2 13.3 dynamic_update_slice.129
  2125.0 13.3 dynamic_update_slice.129
  2192.9 63.8 %reduce-scatter.68.cloned.1.call-done = bf16[256,1408]{1,0:T(8,128)(2,1)} async-done(((bf16[2048,1408]{1,0:T(8,128)(2,1)}), bf16[256,1408]{1,0:T(8,128)(2,1)}) %reduce-scatter.68.cloned.1.call-update) | async-done | bytes 720912 | tf_op jit(solution)/shard_map/reduce_scatter | solution.py:185
  2262.4 22.1 all_to_all.74
  2292.2 164.1 %reduce-scatter.70.cloned.1.call-done = bf16[256,2816]{1,0:T(8,128)(2,1)} async-done(((bf16[2048,2816]{1,0:T(8,128)(2,1)}), bf16[256,2816]{1,0:T(8,128)(2,1)}) %reduce-scatter.70.cloned.1.call-update) | async-done | bytes 1441808 | tf_op jit(solution)/shard_map/reduce_scatter | solution.py:185
  2474.1 48.2 %all-gather.74.cloned.1.call-done = bf16[2048,1408]{1,0:T(8,128)(2,1)} async-done(((bf16[256,1408]{1,0:T(8,128)(2,1)}), bf16[2048,1408]{1,0:T(8,128)(2,1)}) %all-gather.74.cloned.1.call-update) | async-done | bytes 5767184 | tf_op jit(solution)/shard_map/all_gather | solution.py:179
  2543.4 63.4 %reduce-scatter.76.cloned.1.call-done = bf16[256,1408]{1,0:T(8,128)(2,1)} async-done(((bf16[2048,1408]{1,0:T(8,128)(2,1)}), bf16[256,1408]{1,0:T(8,128)(2,1)}) %reduce-scatter.76.cloned.1.call-update) | async-done | bytes 720912 | tf_op jit(solution)/shard_map/reduce_scatter | solution.py:185
  2617.6 54.5 %all-gather.80.cloned.1.call-done = bf16[2048,1408]{1,0:T(8,128)(2,1)} async-done(((bf16[256,1408]{1,0:T(8,128)(2,1)}), bf16[2048,1408]{1,0:T(8,128)(2,1)}) %all-gather.80.cloned.1.call-update) | async-done | bytes 5767184 | tf_op jit(solution)/shard_map/all_gather | solution.py:179
  2680.7 47.3 %while.154 = (s32[]{:T(128)}, f32[2,1024,2,88]{1,0,3,2:T(2,128)}, f32[2,333,2,88]{1,3,2,0:T(8,128)}, bf16[2,333,2,88]{1,3,2,0:T(8,128)(2,1)}, bf16[2,333,2,88]{1...) while((s32[]{:T(128)}, f32[2,1024,2,88]{1,0,3,2:T(2,128)}, ...), condition=%wide.region_117.118_spmd, body=%wide.region_115.117_spmd.sunk | while | flops 605838592 | bytes 34804144 | solution.py:375
  2686.1 13.3 dynamic_update_slice.137
  2709.8 13.3 dynamic_update_slice.137
  2744.0 109.8 %reduce-scatter.78.cloned.1.call-done = bf16[256,1408]{1,0:T(8,128)(2,1)} async-done(((bf16[2048,1408]{1,0:T(8,128)(2,1)}), bf16[256,1408]{1,0:T(8,128)(2,1)}) %reduce-scatter.78.cloned.1.call-update) | async-done | bytes 720912 | tf_op jit(solution)/shard_map/reduce_scatter | solution.py:185
  2871.8 45.7 %all-gather.82.cloned.1.call-done = bf16[2048,1408]{1,0:T(8,128)(2,1)} async-done(((bf16[256,1408]{1,0:T(8,128)(2,1)}), bf16[2048,1408]{1,0:T(8,128)(2,1)}) %all-gather.82.cloned.1.call-update) | async-done | bytes 5767184 | tf_op jit(solution)/shard_map/all_gather | solution.py:179
  2926.8 92.0 %while.155 = (s32[]{:T(128)}, f32[2,1024,2,88]{1,0,3,2:T(2,128)}, f32[2,1024,2,88]{1,0,3,2:T(2,128)}, bf16[2,1024,2,88]{1,3,2,0:T(8,128)(2,1)}, bf16[2,1024,2,88...) while((s32[]{:T(128)}, f32[2,1024,2,88]{1,0,3,2:T(2,128)}, ...), condition=%wide.region_125.126_spmd, body=%wide.region_123.125_spmd.sunk | while | flops 1871017984 | bytes 123759784 | solution.py:416
  3107.2 63.5 %reduce-scatter.80.cloned.1.call-done = bf16[256,1408]{1,0:T(8,128)(2,1)} async-done(((bf16[2048,1408]{1,0:T(8,128)(2,1)}), bf16[256,1408]{1,0:T(8,128)(2,1)}) %reduce-scatter.80.cloned.1.call-update) | async-done | bytes 720912 | tf_op jit(solution)/shard_map/reduce_scatter | solution.py:185
  3393.4 23.6 reduce-scatter.102.cloned.1.call-done
  3419.7 34.1 reduce-scatter.88.cloned.1.call-done
  3456.0 29.6 reduce-scatter.84.cloned.1.call-done
  3487.5 29.1 reduce-scatter.100.cloned.1.call-done
  3519.3 45.3 %reduce-scatter.98.cloned.1.call-done = bf16[352,1056]{1,0:T(8,128)(2,1)} async-done(((bf16[1408,1056]{1,0:T(8,128)(2,1)}), bf16[352,1056]{1,0:T(8,128)(2,1)}) %reduce-scatter.98.cloned.1.call-update) | async-done | bytes 743440
  3572.0 24.3 reduce-scatter.96.cloned.1.call-done
  3599.0 37.0 reduce-scatter.90.cloned.1.call-done
  3640.7 62.5 %reduce-scatter.58.cloned.1.call-done = bf16[256,1408]{1,0:T(8,128)(2,1)} async-done(((bf16[2048,1408]{1,0:T(8,128)(2,1)}), bf16[256,1408]{1,0:T(8,128)(2,1)}) %reduce-scatter.58.cloned.1.call-update) | async-done | bytes 720912 | tf_op jit(solution)/shard_map/reduce_scatter | solution.py:171
  3705.9 117.4 %reduce-scatter.82.cloned.1.call-done = bf16[256,2816]{1,0:T(8,128)(2,1)} async-done(((bf16[2048,2816]{1,0:T(8,128)(2,1)}), bf16[256,2816]{1,0:T(8,128)(2,1)}) %reduce-scatter.82.cloned.1.call-update) | async-done | bytes 1441808 | tf_op jit(solution)/shard_map/reduce_scatter | solution.py:185
  3831.3 39.2 %all-reduce.13 = (f32[2,2816]{1,0:T(2,128)}, f32[2,2,1408]{2,1,0:T(2,128)}, f32[2,1408]{1,0:T(2,128)}) all-reduce(f32[2,2816]{1,0:T(2,128)S(1)} %pad_maximum_fusion.30, f32[2,2,1408]{2,1,0:T(2,128)S(1)} %pad_maximum_fusion.31, f32[2,1408]{1,0:T(2,128)S(1)} %pad_maximum_fusion.32), channel_id=1, replica_groups=mesh['row'=4,'col'=8] {'row','col'}, use_global_device_ids=true, to_apply=%region_143.144 | all-reduce | flops 14080 | bytes 112640 | tf_op jit(solution)/shard_map/psum | solution.py:525
  (1526 shorter events, 1353.3 us)
Async XLA Ops:
  8.0 119.6 %all-gather.46.cloned.1.call-start = ((), (), s32[]{:S(2)}) async-start(), calls=%async_computation.33 | async-start | bytes 12976128 | tf_op jit(solution)/shard_map/all_gather | solution.py:168
  136.9 48.1 %all-to-all-start = ((bf16[8,256,176]{1,2,0:T(8,128)(2,1)}), bf16[8,256,176]{1,2,0:T(8,128)(2,1)S(1)}, u32[]{:S(2)}, u32[]{:S(2)}) async-start(bf16[8,256,176]{1,2,0:T(8,128)(2,1)} %bitcast.903), calls=%async_computation | async-start | bytes 1441792 | tf_op jit(solution)/shard_map/all_to_all | solution.py:234
  140.4 73.7 %all-gather.84.cloned.1.call-start = ((), (), s32[]{:S(2)}) async-start(), calls=%async_computation.72 | async-start | bytes 3604480 | tf_op jit(solution)/shard_map/all_gather | solution.py:158
  142.7 112.6 %all-gather.48.cloned.1.call-start = ((), (), s32[]{:S(2)}) async-start(), calls=%async_computation.34 | async-start | bytes 6488064 | tf_op jit(solution)/shard_map/all_gather | solution.py:168
  190.8 200.1 %reduce-scatter.48.cloned.1.call-start = ((), (), s32[]{:S(2)}) async-start(), calls=%async_computation.35 | async-start | bytes 6488064 | tf_op jit(solution)/shard_map/reduce_scatter | solution.py:171
  316.3 139.7 %reduce-scatter.72.cloned.1.call-start = ((), (), s32[]{:S(2)}) async-start(), calls=%async_computation.60 | async-start | bytes 6488064 | tf_op jit(solution)/shard_map/reduce_scatter | solution.py:171
  332.1 183.8 %all-gather.50.cloned.1.call-start = ((), (), s32[]{:S(2)}) async-start(), calls=%async_computation.36 | async-start | bytes 1548288 | tf_op jit(solution)/shard_map/all_gather | solution.py:137
  333.7 186.3 %all-gather.52.cloned.1.call-start = ((), (), s32[]{:S(2)}) async-start(), calls=%async_computation.37 | async-start | bytes 6488064 | tf_op jit(solution)/shard_map/all_gather | solution.py:168
  460.2 120.3 %all-gather.76.cloned.1.call-start = ((), (), s32[]{:S(2)}) async-start(), calls=%async_computation.61 | async-start | bytes 6488064 | tf_op jit(solution)/shard_map/all_gather | solution.py:168
  460.8 228.7 %reduce-scatter.50.cloned.1.call-start = ((), (), s32[]{:S(2)}) async-start(), calls=%async_computation.38 | async-start | bytes 6488064 | tf_op jit(solution)/shard_map/reduce_scatter | solution.py:171
  626.0 128.9 %reduce-scatter.74.cloned.1.call-start = ((), (), s32[]{:S(2)}) async-start(), calls=%async_computation.62 | async-start | bytes 6488064 | tf_op jit(solution)/shard_map/reduce_scatter | solution.py:171
  641.8 149.6 %all-gather.86.cloned.1.call-start = ((), (), s32[]{:S(2)}) async-start(), calls=%async_computation.73 | async-start | bytes 2703360 | tf_op jit(solution)/shard_map/all_gather | solution.py:163
  644.1 209.7 %all-gather.54.cloned.1.call-start = ((), (), s32[]{:S(2)}) async-start(), calls=%async_computation.39 | async-start | bytes 6488064 | tf_op jit(solution)/shard_map/all_gather | solution.py:168
  758.2 132.2 %all-gather.88.cloned.1.call-start = ((), (), s32[]{:S(2)}) async-start(), calls=%async_computation.74 | async-start | bytes 2703360 | tf_op jit(solution)/shard_map/all_gather | solution.py:164
  759.3 205.9 %reduce-scatter.52.cloned.1.call-start = ((), (), s32[]{:S(2)}) async-start(), calls=%async_computation.40 | async-start | bytes 6488064 | tf_op jit(solution)/shard_map/reduce_scatter | solution.py:171
  900.3 175.7 %all-gather.56.cloned.1.call-start = ((), (), s32[]{:S(2)}) async-start(), calls=%async_computation.41 | async-start | bytes 12976128 | tf_op jit(solution)/shard_map/all_gather | solution.py:168
  1085.2 44.8 %all-to-all-start.1 = ((bf16[8,256,176]{1,2,0:T(8,128)(2,1)}), bf16[8,256,176]{1,2,0:T(8,128)(2,1)S(1)}, u32[]{:S(2)}, u32[]{:S(2)}) async-start(bf16[8,256,176]{1,2,0:T(8,128)(2,1)} %bitcast.902), calls=%async_computation.4 | async-start | bytes 1441792 | tf_op jit(solution)/shard_map/all_to_all | solution.py:234
  1088.9 69.8 %all-gather.90.cloned.1.call-start = ((), (), s32[]{:S(2)}) async-start(), calls=%async_computation.75 | async-start | bytes 3604480 | tf_op jit(solution)/shard_map/all_gather | solution.py:158
  1090.3 111.9 %all-gather.58.cloned.1.call-start = ((), (), s32[]{:S(2)}) async-start(), calls=%async_computation.42 | async-start | bytes 6488064 | tf_op jit(solution)/shard_map/all_gather | solution.py:168
  1133.0 194.7 %copy-start.9 = (f32[256,1408]{1,0:T(8,128)}, f32[256,1408]{1,0:T(8,128)S(1)}, u32[]{:S(2)}) copy-start(f32[256,1408]{1,0:T(8,128)S(1)} %copy.281) | copy-start | bytes 4325380
  1135.5 192.2 %reduce-scatter.60.cloned.1.call-start = ((), (), s32[]{:S(2)}) async-start(), calls=%async_computation.49 | async-start | bytes 6488064 | tf_op jit(solution)/shard_map/reduce_scatter | solution.py:171
  1264.0 125.8 %all-gather.66.cloned.1.call-start = ((), (), s32[]{:S(2)}) async-start(), calls=%async_computation.50 | async-start | bytes 6488064 | tf_op jit(solution)/shard_map/all_gather | solution.py:168
  1331.0 158.8 %reduce-scatter.62.cloned.1.call-start = ((), (), s32[]{:S(2)}) async-start(), calls=%async_computation.51 | async-start | bytes 6488064 | tf_op jit(solution)/shard_map/reduce_scatter | solution.py:171
  1425.2 101.0 %all-gather.92.cloned.1.call-start = ((), (), s32[]{:S(2)}) async-start(), calls=%async_computation.76 | async-start | bytes 2703360 | tf_op jit(solution)/shard_map/all_gather | solution.py:163
  1425.8 163.0 %all-gather.68.cloned.1.call-start = ((), (), s32[]{:S(2)}) async-start(), calls=%async_computation.52 | async-start | bytes 6488064 | tf_op jit(solution)/shard_map/all_gather | solution.py:168
  1493.0 132.6 %all-gather.94.cloned.1.call-start = ((), (), s32[]{:S(2)}) async-start(), calls=%async_computation.77 | async-start | bytes 2703360 | tf_op jit(solution)/shard_map/all_gather | solution.py:164
  1493.7 193.8 %all-gather.64.cloned.1.call-start = ((), (), s32[]{:S(2)}) async-start(), calls=%async_computation.48 | async-start | bytes 6488064 | tf_op jit(solution)/shard_map/all_gather | solution.py:179
  1494.5 277.8 %reduce-scatter.64.cloned.1.call-start = ((), (), s32[]{:S(2)}) async-start(), calls=%async_computation.53 | async-start | bytes 6488064 | tf_op jit(solution)/shard_map/reduce_scatter | solution.py:185
  1708.6 127.2 %all-gather.70.cloned.1.call-start = ((), (), s32[]{:S(2)}) async-start(), calls=%async_computation.54 | async-start | bytes 6488064 | tf_op jit(solution)/shard_map/all_gather | solution.py:179
  1776.9 194.2 %reduce-scatter.66.cloned.1.call-start = ((), (), s32[]{:S(2)}) async-start(), calls=%async_computation.55 | async-start | bytes 6488064 | tf_op jit(solution)/shard_map/reduce_scatter | solution.py:185
  1907.4 135.4 %all-gather.72.cloned.1.call-start = ((), (), s32[]{:S(2)}) async-start(), calls=%async_computation.56 | async-start | bytes 6488064 | tf_op jit(solution)/shard_map/all_gather | solution.py:179
  1976.3 216.6 %reduce-scatter.54.cloned.1.call-start = ((), (), s32[]{:S(2)}) async-start(), calls=%async_computation.43 | async-start | bytes 6488064 | tf_op jit(solution)/shard_map/reduce_scatter | solution.py:171
  2003.8 252.9 %reduce-scatter.68.cloned.1.call-start = ((), (), s32[]{:S(2)}) async-start(), calls=%async_computation.57 | async-start | bytes 6488064 | tf_op jit(solution)/shard_map/reduce_scatter | solution.py:185
  2192.6 263.6 %reduce-scatter.70.cloned.1.call-start = ((), (), s32[]{:S(2)}) async-start(), calls=%async_computation.58 | async-start | bytes 12976128 | tf_op jit(solution)/shard_map/reduce_scatter | solution.py:185
  2291.5 172.7 %all-gather.78.cloned.1.call-start = ((), (), s32[]{:S(2)}) async-start(), calls=%async_computation.63 | async-start | bytes 6488064 | tf_op jit(solution)/shard_map/all_gather | solution.py:168
  2292.1 166.2 %copy-start.314 = (f32[256]{0:T(256)S(1)}, f32[256]{0:T(256)}, u32[]{:S(2)}) copy-start(f32[256]{0:T(256)} %copy-done.313) | copy-start | bytes 3076
  2292.1 230.2 %all-gather.74.cloned.1.call-start = ((), (), s32[]{:S(2)}) async-start(), calls=%async_computation.59 | async-start | bytes 6488064 | tf_op jit(solution)/shard_map/all_gather | solution.py:179
  2463.7 143.1 %reduce-scatter.76.cloned.1.call-start = ((), (), s32[]{:S(2)}) async-start(), calls=%async_computation.64 | async-start | bytes 6488064 | tf_op jit(solution)/shard_map/reduce_scatter | solution.py:185
  2543.3 128.8 %all-gather.80.cloned.1.call-start = ((), (), s32[]{:S(2)}) async-start(), calls=%async_computation.65 | async-start | bytes 6488064 | tf_op jit(solution)/shard_map/all_gather | solution.py:179
  2613.3 240.5 %reduce-scatter.78.cloned.1.call-start = ((), (), s32[]{:S(2)}) async-start(), calls=%async_computation.66 | async-start | bytes 6488064 | tf_op jit(solution)/shard_map/reduce_scatter | solution.py:185
  2743.4 115.7 %all-gather.60.cloned.1.call-start = ((), (), s32[]{:S(2)}) async-start(), calls=%async_computation.44 | async-start | bytes 6488064 | tf_op jit(solution)/shard_map/all_gather | solution.py:168
  2744.0 173.5 %all-gather.82.cloned.1.call-start = ((), (), s32[]{:S(2)}) async-start(), calls=%async_computation.67 | async-start | bytes 6488064 | tf_op jit(solution)/shard_map/all_gather | solution.py:179
  2859.0 246.2 %reduce-scatter.56.cloned.1.call-start = ((), (), s32[]{:S(2)}) async-start(), calls=%async_computation.45 | async-start | bytes 6488064 | tf_op jit(solution)/shard_map/reduce_scatter | solution.py:171
  3041.5 129.1 %reduce-scatter.80.cloned.1.call-start = ((), (), s32[]{:S(2)}) async-start(), calls=%async_computation.68 | async-start | bytes 6488064 | tf_op jit(solution)/shard_map/reduce_scatter | solution.py:185
  3101.3 211.1 %reduce-scatter.94.cloned.1.call-start = ((), (), s32[]{:S(2)}) async-start(), calls=%async_computation.81 | async-start | bytes 811008
  3103.8 217.8 %reduce-scatter.92.cloned.1.call-start = ((), (), s32[]{:S(2)}) async-start(), calls=%async_computation.80 | async-start | bytes 811008
  3173.2 185.8 %all-gather.62.cloned.1.call-start = ((), (), s32[]{:S(2)}) async-start(), calls=%async_computation.46 | async-start | bytes 6488064 | tf_op jit(solution)/shard_map/all_gather | solution.py:168
  3174.4 210.0 %all-reduce.16.cloned.1.call-start = ((), (), s32[]{:S(2)}) async-start(), calls=%async_computation.87 | async-start | bytes 8650752
  3207.4 180.5 %reduce-scatter.86.cloned.1.call-start = ((), (), s32[]{:S(2)}) async-start(), calls=%async_computation.71 | async-start | bytes 5406720 | tf_op jit(solution)/shard_map/reduce_scatter | solution.py:515
  3226.8 163.9 %reduce-scatter.104.cloned.1.call-start = ((), (), s32[]{:S(2)}) async-start(), calls=%async_computation.86 | async-start | bytes 1351680
  3239.5 177.6 %reduce-scatter.102.cloned.1.call-start = ((), (), s32[]{:S(2)}) async-start(), calls=%async_computation.85 | async-start | bytes 1351680
  3252.5 201.3 %reduce-scatter.88.cloned.1.call-start = ((), (), s32[]{:S(2)}) async-start(), calls=%async_computation.78 | async-start | bytes 1769472
  3262.0 223.7 %reduce-scatter.84.cloned.1.call-start = ((), (), s32[]{:S(2)}) async-start(), calls=%async_computation.70 | async-start | bytes 1802240 | tf_op jit(solution)/shard_map/reduce_scatter | solution.py:509
  3266.3 250.3 %reduce-scatter.100.cloned.1.call-start = ((), (), s32[]{:S(2)}) async-start(), calls=%async_computation.84 | async-start | bytes 1351680
  3279.1 285.5 %reduce-scatter.98.cloned.1.call-start = ((), (), s32[]{:S(2)}) async-start(), calls=%async_computation.83 | async-start | bytes 4055040
  3317.6 23.0 all-to-all-start.3
  3321.2 275.2 %reduce-scatter.96.cloned.1.call-start = ((), (), s32[]{:S(2)}) async-start(), calls=%async_computation.82 | async-start | bytes 1351680
  3326.7 309.4 %reduce-scatter.90.cloned.1.call-start = ((), (), s32[]{:S(2)}) async-start(), calls=%async_computation.79 | async-start | bytes 2703360
  3358.9 344.3 %reduce-scatter.58.cloned.1.call-start = ((), (), s32[]{:S(2)}) async-start(), calls=%async_computation.47 | async-start | bytes 6488064 | tf_op jit(solution)/shard_map/reduce_scatter | solution.py:171
  3374.9 448.3 %reduce-scatter.82.cloned.1.call-start = ((), (), s32[]{:S(2)}) async-start(), calls=%async_computation.69 | async-start | bytes 12976128 | tf_op jit(solution)/shard_map/reduce_scatter | solution.py:185
  3640.7 182.6 %copy-start.25 = (f32[256,1408]{1,0:T(8,128)S(1)}, f32[256,1408]{1,0:T(8,128)}, u32[]{:S(2)}) copy-start(f32[256,1408]{1,0:T(8,128)} %copy-done.24) | copy-start | bytes 4325380
  3640.7 182.6 %copy-start.27 = (f32[256,1408]{1,0:T(8,128)S(1)}, f32[256,1408]{1,0:T(8,128)}, u32[]{:S(2)}) copy-start(f32[256,1408]{1,0:T(8,128)} %copy-done.26) | copy-start | bytes 4325380
  3640.7 182.6 %copy-start.215 = (f32[2816]{0:T(1024)S(1)}, f32[2816]{0:T(1024)}, u32[]{:S(2)}) copy-start(f32[2816]{0:T(1024)} %copy-done.214) | copy-start | bytes 33796
  3640.7 182.6 %copy-start.286 = (f32[256]{0:T(256)S(1)}, f32[256]{0:T(256)}, u32[]{:S(2)}) copy-start(f32[256]{0:T(256)} %copy-done.285) | copy-start | bytes 3076
  (359 other events, 5123.8 us)
Sparse Core Ops, SparseCore 0:
  16.8 110.7 all-gather.45
  335.1 43.6 all-gather.49
  460.3 58.8 all-gather.51
  521.3 59.0 all-gather.75
  900.4 64.8 reduce-scatter.51
  969.5 106.4 all-gather.55
  1264.2 63.5 reduce-scatter.59
  1331.1 58.7 all-gather.65
  1708.7 63.5 reduce-scatter.63
  1777.0 58.7 all-gather.69
  1907.5 63.5 reduce-scatter.65
  2003.9 84.9 reduce-scatter.53
  2192.7 63.9 reduce-scatter.67
  2294.3 106.7 all-gather.77
  2463.8 58.4 all-gather.73
  2743.5 110.2 reduce-scatter.77
  3041.7 63.5 reduce-scatter.55
  3107.4 63.2 reduce-scatter.79
  3173.5 70.1 reduce-scatter.93
  3245.8 29.2 reduce-scatter.91
  3278.2 75.7 reduce-scatter.85
  3356.9 29.2 reduce-scatter.103
  3389.0 27.9 reduce-scatter.101
  3419.8 33.9 reduce-scatter.87
  3457.3 28.2 reduce-scatter.83
  3488.6 27.9 reduce-scatter.99
  3519.8 44.7 reduce-scatter.97
  3568.4 27.9 reduce-scatter.95
  3600.2 35.7 reduce-scatter.89
  3638.3 64.8 reduce-scatter.57
  3705.6 117.6 reduce-scatter.81
Sparse Core Ops, SparseCore 1:
  143.3 49.5 all-gather.83
  194.9 60.2 all-gather.47
  316.3 74.5 reduce-scatter.47
  393.2 62.7 reduce-scatter.71
  626.1 63.3 reduce-scatter.49
  691.8 63.1 reduce-scatter.73
  757.2 34.1 all-gather.85
  793.5 60.2 all-gather.53
  856.0 34.3 all-gather.87
  1092.1 47.7 all-gather.89
  1142.0 60.2 all-gather.57
  1425.3 64.5 reduce-scatter.61
  1492.1 34.1 all-gather.91
  1528.5 60.2 all-gather.67
  1591.2 34.3 all-gather.93
  1627.3 60.2 all-gather.63
  1976.4 66.4 all-gather.71
  2291.6 164.6 reduce-scatter.69
  2543.4 63.3 reduce-scatter.75
  2613.4 58.7 all-gather.79
  2745.5 82.2 all-gather.59
  2859.1 58.3 all-gather.81
  3176.0 61.0 all-gather.61
  3240.7 126.5 all-reduce.15
where the time goes:
time: 3900 us; the launch traced here: 3880 us
  waiting for transfers between devices  2220 us (57%)
  local copies, waits for them, and re-layouts  579 us (15%)
  matrix products  498 us (13%)
  blocking collectives  319 us (8%)
  other arithmetic  219 us (6%)
    reduce_scatter x8, waiting for transfers between devices, sum_grads(): lax.psum_scatter(term(jnp.int32(0), tok_dev * lax.axis_size('col')).astyp...  709 us
    reduce_scatter x10, waiting for transfers between devices, sum_rows(): lax.psum_scatter(term(jnp.int32(0), tok_dev * lax.axis_size('col')).astyp...  485 us
    all_gather x12, waiting for transfers between devices, spread_rows(): lax.all_gather(value, 'col', axis=0, tiled=True)  394 us
    all_gather x6, waiting for transfers between devices, fold_grads(): lax.all_gather(value, 'col', axis=0, tiled=True)  283 us
    unnamed x65, waiting for transfers between devices  198 us
    dynamic_update_slice x24, local copies, waits for them, and re-layouts, forward_layer(): lax.map(attend_forward, (query_rot.astype(jnp.bfloat16), keys_rot.astype(...  169 us
    unnamed x729, local copies, waits for them, and re-layouts  154 us
    dot_general x12, matrix products, times_transposed(): lax.dot_general(left, right, (((1,), (1,)), ((), ())), preferred_element_...  78.1 us
  transfers between devices with their start and end apart: 58, of which 43 were waited for; matrix products, arithmetic and copies ran while one was open for 17% of the time, Pallas kernels for 0%

commit v1 on v0

v1 whole, which is shorter than its diff:
```python
import jax
import jax.numpy as jnp
from jax import lax
from jax.sharding import Mesh
from jax.sharding import PartitionSpec as P

HD = 88
SIDE = 32
SEQ = 1024
LATENTS = 2

HIGHEST = lax.Precision.HIGHEST
EPSILON = 1e-06
F32 = jnp.float32
B16 = jnp.bfloat16
SCALE = HD ** (-0.5)


def norm_stats(value):
    center = value - jnp.mean(value, axis=-1, keepdims=True)
    spread = jnp.mean(center * center, axis=-1, keepdims=True)
    rstd = lax.rsqrt(spread + EPSILON)
    return center * rstd, rstd


def norm_back(normed, rstd, grad):
    return rstd * (
        grad
        - jnp.mean(grad, axis=-1, keepdims=True)
        - normed * jnp.mean(grad * normed, axis=-1, keepdims=True)
    )


def silu(value):
    return value * jax.nn.sigmoid(value)


def gelu_tanh(value):
    inner = 0.7978845608028654 * (value + 0.044715 * value * value * value)
    return 0.5 * value * (1.0 + jnp.tanh(inner))


def gelu_grad(value):
    inner = 0.7978845608028654 * (value + 0.044715 * value * value * value)
    tanh = jnp.tanh(inner)
    slope = 0.7978845608028654 * (1.0 + 3.0 * 0.044715 * value * value)
    return 0.5 * (1.0 + tanh) + 0.5 * value * (1.0 - tanh * tanh) * slope


def rotary_tables():
    place = jnp.arange(SEQ, dtype=jnp.int32)
    grid_row = (place // SIDE).astype(F32)
    grid_col = (place % SIDE).astype(F32)
    feature = jnp.arange(HD, dtype=jnp.int32)
    pair = feature // 2
    quarter = HD // 4
    power = (pair % quarter).astype(F32) * (4.0 / HD)
    freq = jnp.exp(-power * jnp.log(10000.0))
    coordinate = jnp.where(pair[:, None] < quarter, grid_row[None, :], grid_col[None, :])
    angle = coordinate * freq[:, None]
    sign = jnp.where(feature % 2 == 0, -1.0, 1.0)[:, None]
    return (jnp.cos(angle), jnp.sin(angle) * sign)


def head_norm(value):
    center = value - jnp.mean(value, axis=1, keepdims=True)
    spread = jnp.mean(center * center, axis=1, keepdims=True)
    rstd = lax.rsqrt(spread + EPSILON)
    return center * rstd, rstd


def head_norm_back(normed, rstd, grad):
    return rstd * (
        grad
        - jnp.mean(grad, axis=1, keepdims=True)
        - normed * jnp.mean(grad * normed, axis=1, keepdims=True)
    )


def swapped(value):
    heads, _, tokens = value.shape
    pairs = value.reshape(heads, HD // 2, 2, tokens)
    return pairs[:, :, ::-1].reshape(value.shape)


def rotate(value, tables):
    return value * tables[0] + swapped(value) * tables[1]


def rotate_back(grad, tables):
    return grad * tables[0] - swapped(grad) * tables[1]


def attention(query, keys, values, tables, rotate_keys):
    query = query.reshape(-1, HD, query.shape[1])
    keys = keys.reshape(-1, HD, keys.shape[1])
    values_low = values.reshape(-1, HD, values.shape[1]).astype(B16)
    query_low = rotate(head_norm(query)[0], tables).astype(B16)
    keys_normed = head_norm(keys)[0]
    keys_low = (rotate(keys_normed, tables) if rotate_keys else keys_normed).astype(B16)
    scores = jnp.einsum("heq,hek->hqk", query_low, keys_low, preferred_element_type=F32) * SCALE
    highest = jnp.max(scores, axis=-1, keepdims=True)
    expo = jnp.exp(scores - highest)
    total = jnp.sum(expo, axis=-1, keepdims=True)
    probs_low = (expo / total).astype(B16)
    result = jnp.einsum("hqk,hek->heq", probs_low, values_low, preferred_element_type=F32)
    return result.astype(B16).reshape(-1, query.shape[2]), (highest + jnp.log(total))[..., 0]


def attention_back(query, keys, values, logsum, grad_low, tables, rotate_keys):
    query = query.reshape(-1, HD, query.shape[1])
    keys = keys.reshape(-1, HD, keys.shape[1])
    values_low = values.reshape(-1, HD, values.shape[1]).astype(B16)
    grad_low = grad_low.reshape(-1, HD, grad_low.shape[1])
    query_normed, query_rstd = head_norm(query)
    keys_normed, keys_rstd = head_norm(keys)
    query_low = rotate(query_normed, tables).astype(B16)
    keys_low = (rotate(keys_normed, tables) if rotate_keys else keys_normed).astype(B16)
    scores = jnp.einsum("heq,hek->hqk", query_low, keys_low, preferred_element_type=F32) * SCALE
    probs = jnp.exp(scores - logsum[..., None])
    probs_low = probs.astype(B16)
    values_grad = jnp.einsum("hqk,heq->hek", probs_low, grad_low, preferred_element_type=F32)
    probs_grad = jnp.einsum("heq,hek->hqk", grad_low, values_low, preferred_element_type=F32)
    scores_grad = probs * (probs_grad - jnp.sum(probs * probs_grad, axis=-1, keepdims=True))
    scores_low = scores_grad.astype(B16)
    query_grad = jnp.einsum("hqk,hek->heq", scores_low, keys_low, preferred_element_type=F32)
    keys_grad = jnp.einsum("hqk,heq->hek", scores_low, query_low, preferred_element_type=F32)
    query_grad = rotate_back(query_grad * SCALE, tables)
    keys_grad = keys_grad * SCALE
    if rotate_keys:
        keys_grad = rotate_back(keys_grad, tables)
    query_grad = head_norm_back(query_normed, query_rstd, query_grad)
    keys_grad = head_norm_back(keys_normed, keys_rstd, keys_grad)
    flat = lambda value: value.reshape(-1, value.shape[2]).astype(B16)
    return flat(query_grad), flat(keys_grad), flat(values_grad)


def dot(left, right, left_dim, right_dim):
    return lax.dot_general(
        left, right, (((left_dim,), (right_dim,)), ((), ())), preferred_element_type=F32
    )


def on_device(
    latent,
    skips,
    cond,
    text,
    skip_gain,
    attn_gain,
    ffn_gain,
    skip_w,
    mod_w,
    qkv_w,
    out_w,
    cq_w,
    ckv_w,
    cout_w,
    fc1_w,
    fc2_w,
    cotangent,
):
    rows = lax.axis_size("row")
    ranks = lax.axis_size("tp")
    row = lax.axis_index("row")
    lat = lax.axis_index("lat")
    rank = lax.axis_index("tp")
    width = latent.shape[1]
    depth = qkv_w.shape[2]
    local = qkv_w.shape[3]
    hidden_local = fc1_w.shape[2]
    layers = skip_w.shape[0]
    text_depth = ckv_w.shape[2]
    text_count = text.shape[1]
    tables = rotary_tables()
    everyone = ("row", "lat", "tp")
    owners = ("lat", "row")

    def gather_tokens(value):
        return lax.all_gather(value, "tp", axis=0, tiled=True)

    def sum_tokens(value):
        return lax.psum_scatter(
            value.astype(B16), "tp", scatter_dimension=0, tiled=True
        ).astype(F32)

    skip_full, attn_full, cross_full, text_full_w, ffn_full = [], [], [], [], []
    for layer in range(layers):
        skip_full.append(
            lax.all_gather(skip_w[layer].T, everyone, axis=0).reshape(rows, width, -1)
        )
        attn_pack = jnp.concatenate(
            [qkv_w[layer, 0], qkv_w[layer, 1], qkv_w[layer, 2], out_w[layer].T], axis=1
        )
        attn_full.append(
            lax.all_gather(attn_pack, owners, axis=0).reshape(LATENTS, width, 4 * local)
        )
        cross_pack = jnp.concatenate([cq_w[layer], cout_w[layer].T], axis=1)
        cross_full.append(
            lax.all_gather(cross_pack, owners, axis=0).reshape(LATENTS, width, 2 * local)
        )
        text_pack = jnp.concatenate([ckv_w[layer, 0], ckv_w[layer, 1]], axis=1)
        text_full_w.append(
            lax.all_gather(text_pack, owners, axis=0).reshape(LATENTS, rows * text_depth, 2 * local)
        )
        ffn_pack = jnp.concatenate([fc1_w[layer], fc2_w[layer].T], axis=1)
        ffn_full.append(
            lax.all_gather(ffn_pack, owners, axis=0).reshape(LATENTS, width, 2 * hidden_local)
        )

    cond_all = lax.all_gather(cond, "row", axis=0, tiled=True)
    cond_low = silu(cond_all.astype(F32)).astype(B16)
    cond_rows = lax.dynamic_slice_in_dim(cond_low, row * depth, depth, axis=1)
    shift_part = jnp.einsum("sd,ldc->lsc", cond_rows, mod_w, preferred_element_type=F32)
    shift_all = jnp.sum(
        lax.all_gather(shift_part, everyone, axis=0).reshape(
            (rows, LATENTS * ranks) + shift_part.shape
        ),
        axis=0,
    )
    own_latent = row * LATENTS + lat
    shift = lax.dynamic_index_in_dim(shift_all, own_latent, axis=2, keepdims=False)
    shift = jnp.transpose(shift, (1, 0, 2)).reshape(layers, width)

    text_parts = lax.all_gather(text, ("lat", "tp"), axis=0)
    text_own = lax.dynamic_index_in_dim(text_parts, lat, axis=1, keepdims=False)
    text_own = jnp.transpose(text_own, (1, 0, 2)).reshape(text_count, -1)

    def split_heads(stack, index):
        return jnp.concatenate(
            [stack[part][index * local : (index + 1) * local] for part in range(LATENTS)], axis=0
        )

    resid = latent.astype(F32)
    saved = []
    for layer in range(layers):
        keep = {}
        joined = jnp.concatenate([resid, skips[layer].astype(F32)], axis=1)
        normed, rstd = norm_stats(joined)
        keep["skip"] = (normed, rstd)
        skip_low = (normed * skip_gain[layer]).astype(B16)
        keep["skip_low"] = skip_low
        resid_one = jnp.einsum(
            "trc,rdc->td",
            skip_low.reshape(skip_low.shape[0], rows, -1),
            skip_full[layer],
            preferred_element_type=F32,
        )
        normed, rstd = norm_stats(resid_one)
        keep["first"] = (normed, rstd)
        first_low = (normed * attn_gain[layer, 0] + shift[layer]).astype(B16)
        first_all = gather_tokens(first_low)
        keep["first_all"] = first_all
        weight = attn_full[layer]
        raw = [dot(weight[part, :, : 3 * local], first_all, 0, 1) for part in range(LATENTS)]
        query, keys, values = (split_heads(raw, index) for index in range(3))
        self_low, self_lse = attention(query, keys, values, tables, True)
        keep["self"] = (query, keys, values, self_lse, self_low)
        out_t = jnp.concatenate([weight[part, :, 3 * local :] for part in range(LATENTS)], axis=1)
        keep["out_t"] = out_t
        resid_two = resid_one + sum_tokens(dot(self_low, out_t, 0, 1))

        normed, rstd = norm_stats(resid_two)
        keep["third"] = (normed, rstd)
        third_low = (normed * attn_gain[layer, 1]).astype(B16)
        third_all = gather_tokens(third_low)
        keep["third_all"] = third_all
        weight = cross_full[layer]
        query_w = jnp.concatenate([weight[part, :, :local] for part in range(LATENTS)], axis=1)
        cout_t = jnp.concatenate([weight[part, :, local:] for part in range(LATENTS)], axis=1)
        keep["cross_w"] = (query_w, cout_t)
        cross_query = dot(query_w, third_all, 0, 1)
        text_raw = [dot(text_full_w[layer][part], text_own, 0, 1) for part in range(LATENTS)]
        text_keys, text_values = (split_heads(text_raw, index) for index in range(2))
        cross_low, cross_lse = attention(cross_query, text_keys, text_values, tables, False)
        keep["cross"] = (cross_query, text_keys, text_values, cross_lse, cross_low)
        resid_three = resid_two + sum_tokens(dot(cross_low, cout_t, 0, 1))

        normed, rstd = norm_stats(resid_three)
        keep["second"] = (normed, rstd)
        second_low = (normed * ffn_gain[layer]).astype(B16)
        second_all = gather_tokens(second_low)
        keep["second_all"] = second_all
        weight = ffn_full[layer]
        hidden = [
            dot(second_all, weight[part, :, :hidden_local], 1, 0) for part in range(LATENTS)
        ]
        act_low = [gelu_tanh(part).astype(B16) for part in hidden]
        keep["hidden"] = hidden
        keep["act"] = act_low
        term = sum(dot(act_low[part], weight[part, :, hidden_local:], 1, 1) for part in range(LATENTS))
        resid = resid_three + sum_tokens(term)
        saved.append(keep)
    mixed = resid

    def scatter_weights(parts):
        packed = parts.astype(B16).reshape(LATENTS * rows, -1, parts.shape[2])
        return lax.psum_scatter(packed, owners, scatter_dimension=0, tiled=False).astype(F32)

    grad = cotangent.astype(F32)
    text_grad = jnp.zeros((text_count, text_own.shape[1]), F32)
    weight_store = [None] * layers
    gain_store = [None] * layers
    skip_store = [None] * layers
    for layer in range(layers - 1, -1, -1):
        keep = saved[layer]
        weight = ffn_full[layer]
        grad_all = gather_tokens(grad.astype(B16))
        ffn_parts = []
        term = None
        for part in range(LATENTS):
            act_grad = dot(grad_all, weight[part, :, hidden_local:], 1, 0)
            hidden_grad = (act_grad * gelu_grad(keep["hidden"][part])).astype(B16)
            down_grad = dot(grad_all, keep["act"][part], 0, 0)
            up_grad = dot(keep["second_all"], hidden_grad, 0, 0)
            piece = dot(hidden_grad, weight[part, :, :hidden_local], 1, 1)
            term = piece if term is None else term + piece
            ffn_parts.append(jnp.concatenate([up_grad, down_grad], axis=1))
        norm_grad = sum_tokens(term)
        ffn_grad = scatter_weights(jnp.stack(ffn_parts))
        normed, rstd = keep["second"]
        gain_ffn = jnp.sum(norm_grad * normed, axis=0)
        grad_three = grad + norm_back(normed, rstd, norm_grad * ffn_gain[layer])

        query_w, cout_t = keep["cross_w"]
        cross_query, text_keys, text_values, cross_lse, cross_low = keep["cross"]
        grad_all = gather_tokens(grad_three.astype(B16))
        out_grad = dot(cout_t, grad_all, 0, 1).astype(B16)
        cout_grad = dot(grad_all, cross_low, 0, 1)
        query_grad, keys_grad, values_grad = attention_back(
            cross_query, text_keys, text_values, cross_lse, out_grad, tables, False
        )
        norm_grad = sum_tokens(dot(query_grad, query_w, 0, 1))
        cq_grad = dot(keep["third_all"], query_grad, 0, 1)
        cross_parts = jnp.stack(
            [
                jnp.concatenate(
                    [
                        cq_grad[:, part * local : (part + 1) * local],
                        cout_grad[:, part * local : (part + 1) * local],
                    ],
                    axis=1,
                )
                for part in range(LATENTS)
            ]
        )
        cross_grad = scatter_weights(cross_parts)
        text_parts_grad = []
        for part in range(LATENTS):
            span = slice(part * local, (part + 1) * local)
            both = jnp.concatenate([keys_grad[span], values_grad[span]], axis=0)
            text_parts_grad.append(dot(text_own, both, 0, 1))
            text_grad = text_grad + dot(both, text_full_w[layer][part], 0, 1)
        ckv_grad = scatter_weights(jnp.stack(text_parts_grad))
        normed, rstd = keep["third"]
        gain_cross = jnp.sum(norm_grad * normed, axis=0)
        grad_two = grad_three + norm_back(normed, rstd, norm_grad * attn_gain[layer, 1])

        weight = attn_full[layer]
        query, keys, values, self_lse, self_low = keep["self"]
        grad_all = gather_tokens(grad_two.astype(B16))
        out_grad = dot(keep["out_t"], grad_all, 0, 1).astype(B16)
        wout_grad = dot(grad_all, self_low, 0, 1)
        three = attention_back(query, keys, values, self_lse, out_grad, tables, True)
        term = None
        attn_parts = []
        for part in range(LATENTS):
            span = slice(part * local, (part + 1) * local)
            both = jnp.concatenate([value[span] for value in three], axis=0)
            piece = dot(both, weight[part, :, : 3 * local], 0, 1)
            term = piece if term is None else term + piece
            attn_parts.append(
                jnp.concatenate(
                    [dot(keep["first_all"], both, 0, 1), wout_grad[:, span]], axis=1
                )
            )
        norm_grad = sum_tokens(term)
        attn_grad = scatter_weights(jnp.stack(attn_parts))
        normed, rstd = keep["first"]
        gain_self = jnp.sum(norm_grad * normed, axis=0)
        shift_own = jnp.sum(norm_grad, axis=0)
        grad_one = grad_two + norm_back(normed, rstd, norm_grad * attn_gain[layer, 0])

        shift_grad = jnp.sum(
            lax.all_gather(shift_own, everyone, axis=0).reshape(rows * LATENTS, ranks, width),
            axis=1,
        )
        column = (lat * ranks + rank) * local
        shift_cols = lax.dynamic_slice_in_dim(shift_grad, column, local, axis=1).astype(B16)
        mod_grad = dot(cond_rows, shift_cols, 0, 0)

        grad_low = grad_one.astype(B16)
        norm_grad = jnp.einsum(
            "td,rdc->trc", grad_low, skip_full[layer], preferred_element_type=F32
        ).reshape(grad_low.shape[0], -1)
        skip_parts = jnp.einsum(
            "td,trc->rdc",
            grad_low,
            keep["skip_low"].reshape(grad_low.shape[0], rows, -1),
            preferred_element_type=F32,
        )
        packed = skip_parts.astype(B16).reshape(rows * LATENTS * ranks, local, -1)
        skip_w_grad = (
            lax.psum_scatter(packed, everyone, scatter_dimension=0, tiled=False).astype(F32).T
        )
        normed, rstd = keep["skip"]
        gain_skip = jnp.sum(norm_grad * normed, axis=0)
        joined_grad = norm_back(normed, rstd, norm_grad * skip_gain[layer])
        grad = joined_grad[:, :width]
        skip_store[layer] = joined_grad[:, width:]
        gain_store[layer] = (gain_skip, jnp.stack([gain_self, gain_cross]), gain_ffn)
        weight_store[layer] = (
            skip_w_grad,
            mod_grad,
            jnp.stack([attn_grad[:, index * local : (index + 1) * local] for index in range(3)]),
            attn_grad[:, 3 * local :].T,
            cross_grad[:, :local],
            jnp.stack([ckv_grad[:, index * local : (index + 1) * local] for index in range(2)]),
            cross_grad[:, local:].T,
            ffn_grad[:, :hidden_local],
            ffn_grad[:, hidden_local:].T,
        )

    weight_outs = tuple(
        jnp.stack([weight_store[layer][slot] for layer in range(layers)]) for slot in range(9)
    )
    gains = tuple(
        jnp.stack([gain_store[layer][slot] for layer in range(layers)]) for slot in range(3)
    )
    gains = lax.psum(gains, everyone)
    blocks = text_grad.astype(B16).reshape(text_count, LATENTS * ranks, -1)
    blocks = jnp.transpose(blocks, (1, 0, 2))
    blocks = lax.all_to_all(blocks, ("lat", "tp"), split_axis=0, concat_axis=0, tiled=True)
    text_out = jnp.sum(
        blocks.astype(F32).reshape((LATENTS, ranks) + blocks.shape[1:]), axis=1
    )
    return (mixed, grad, jnp.stack(skip_store), text_out) + gains + weight_outs


def solution(mesh):
    rows, columns = mesh.shape["row"], mesh.shape["col"]
    grid = Mesh(
        mesh.devices.reshape(rows, LATENTS, columns // LATENTS), ("row", "lat", "tp")
    )
    col = ("lat", "tp")
    tokens = ("row", "lat", "tp")
    return jax.shard_map(
        on_device,
        mesh=grid,
        in_specs=(
            P(tokens, None),
            P(None, tokens, None),
            P("row", None),
            P("row", None, col),
            P(),
            P(),
            P(),
            P(None, "row", col),
            P(None, "row", col),
            P(None, None, "row", col),
            P(None, col, "row"),
            P(None, "row", col),
            P(None, None, "row", col),
            P(None, col, "row"),
            P(None, "row", col),
            P(None, col, "row"),
            P(tokens, None),
        ),
        out_specs=(
            P(tokens, None),
            P(tokens, None),
            P(None, tokens, None),
            P("row", None, col),
            P(),
            P(),
            P(),
            P(None, "row", col),
            P(None, "row", col),
            P(None, None, "row", col),
            P(None, col, "row"),
            P(None, "row", col),
            P(None, None, "row", col),
            P(None, col, "row"),
            P(None, "row", col),
            P(None, col, "row"),
        ),
        check_vma=False,
    )
```

time: 3900 us -> 3110 us (0.80)
  waiting for transfers between devices: 2220 us -> 1840 us
  local copies, waits for them, and re-layouts: 579 us -> 428 us
  blocking collectives: 319 us -> 203 us
  matrix products: 498 us -> 385 us
    reduce_scatter x20 -> x22, waiting for transfers between devices: 1220 us -> 792 us  [the longest x12 301 us: sum_tokens(): lax.psum_scatter(value.astype(B16), 'tp', scatter_dimension=0, tiled=True)]
    all_gather x25 -> x23, waiting for transfers between devices: 795 us -> 1040 us  [the longest x12 340 us: gather_tokens(): return lax.all_gather(value, 'tp', axis=0, tiled=True)]
    unnamed x65 -> x45, waiting for transfers between devices: 198 us -> 1.93 us
    dynamic_update_slice x24 -> x0, local copies, waits for them, and re-layouts: 169 us -> none  [forward_layer(): lax.map(attend_forward, (query_rot.astype(jnp.bfloat16), keys_rot.astype(...]
    rev x0 -> x12, local copies, waits for them, and re-layouts: none -> 111 us  [swapped(): return pairs[:, :, ::-1].reshape(value.shape)]
    all_gather x14 -> x4, blocking collectives: 257 us -> 160 us  [the longest x2 106 us: on_device(): lax.all_gather(shift_own, everyone, axis=0)]
    dot_general x128 -> x99, matrix products: 463 us -> 385 us  [the longest x68 212 us: dot(): lax.dot_general(left, right, (((left_dim,), (right_dim,)), ((), ())), pre...]
    unnamed x729 -> x728, local copies, waits for them, and re-layouts: 154 us -> 88 us
  transfers between devices with their start and end apart: 58 -> 46, of which waited for: 43 -> 39; matrix products, arithmetic and copies ran while one was open for 17% -> 16% of each run, Pallas kernels for 0% -> 0%
where the time goes in v1:
time: 3110 us; the launch traced here: 3090 us
  waiting for transfers between devices  1840 us (59%)
  local copies, waits for them, and re-layouts  428 us (14%)
  matrix products  385 us (12%)
  other arithmetic  212 us (7%)
  blocking collectives  203 us (7%)
    all_gather x12, waiting for transfers between devices, gather_tokens(): return lax.all_gather(value, 'tp', axis=0, tiled=True)  340 us
    reduce_scatter x12, waiting for transfers between devices, sum_tokens(): lax.psum_scatter(value.astype(B16), 'tp', scatter_dimension=0, tiled=True)  301 us
    all_gather x2, waiting for transfers between devices, on_device(): lax.all_gather(ffn_pack, owners, axis=0)  270 us
    reduce_scatter x8, waiting for transfers between devices, scatter_weights(): lax.psum_scatter(packed, owners, scatter_dimension=0, tiled=False)  245 us
    reduce_scatter x2, waiting for transfers between devices, on_device(): lax.psum_scatter(packed, everyone, scatter_dimension=0, tiled=False)  245 us
    dot_general x68, matrix products, dot(): lax.dot_general(left, right, (((left_dim,), (right_dim,)), ((), ())), pre...  212 us
    all_gather x2, waiting for transfers between devices, on_device(): lax.all_gather(attn_pack, owners, axis=0).reshape(LATENTS, width, 4 * local)  143 us
    rev x12, local copies, waits for them, and re-layouts, swapped(): return pairs[:, :, ::-1].reshape(value.shape)  111 us
  transfers between devices with their start and end apart: 46, of which 39 were waited for; matrix products, arithmetic and copies ran while one was open for 16% of the time, Pallas kernels for 0%

profile of v1, /device:TPU:0, one launch (start us, length us, event | category | flops | bytes accessed | tf_op | source)
XLA Modules:
  0.0 3092.7 jit_solution(6102460015987599110)
XLA Ops:
  16.0 9.6 all-gather.14
  27.1 44.9 %all-gather.2 = f32[64,8,176]{2,1,0:T(8,128)S(1)} all-gather(f32[2,8,176]{2,1,0:T(8,128)S(1)} %convolution_bitcast_fusion.4), channel_id=4, replica_groups=mesh['row'=4,'lat'=2,'tp'=4] {'row','lat','tp'}, dimensions={0}, use_global_device_ids=true | all-gather | bytes 371712 | tf_op jit(solution)/shard_map/all_gather | solution.py:216
  84.4 11.5 all-gather.65.cloned.1.call-done
  108.8 70.4 %all-gather.67.cloned.1.call-done = bf16[2816,704]{1,0:T(8,128)(2,1)} async-done(((bf16[352,704]{1,0:T(8,128)(2,1)}), bf16[2816,704]{1,0:T(8,128)(2,1)}) %all-gather.67.cloned.1.call-update) | async-done | bytes 3964944 | tf_op jit(solution)/shard_map/all_gather | solution.py:196
  183.2 29.9 all-gather.41.cloned.1.call-done
  232.2 10.6 rev.42
  248.9 10.5 rev.43
  274.6 8.5 fusion
  301.1 36.5 %reduce-scatter.23.cloned.1.call-done = bf16[256,1408]{1,0:T(8,128)(2,1)} async-done(((bf16[1024,1408]{1,0:T(8,128)(2,1)}), bf16[256,1408]{1,0:T(8,128)(2,1)}) %reduce-scatter.23.cloned.1.call-update) | async-done | bytes 720912 | tf_op jit(solution)/shard_map/reduce_scatter | solution.py:183
  342.1 48.1 %all-gather.69.cloned.1.call-done = bf16[2048,352]{0,1:T(8,128)(2,1)} async-done(((bf16[256,352]{0,1:T(8,128)(2,1)}), bf16[2048,352]{0,1:T(8,128)(2,1)}) %all-gather.69.cloned.1.call-update) | async-done | bytes 1441808 | tf_op jit(solution)/shard_map/all_gather | solution.py:204
  394.4 51.8 %all-gather.73.cloned.1.call-done = bf16[2816,352]{1,0:T(8,128)(2,1)} async-done(((bf16[352,352]{1,0:T(8,128)(2,1)}), bf16[2816,352]{1,0:T(8,128)(2,1)}) %all-gather.73.cloned.1.call-update) | async-done | bytes 1982480 | tf_op jit(solution)/shard_map/all_gather | solution.py:200
  457.6 22.3 all-gather.43.cloned.1.call-done
  488.5 10.7 rev.44
  518.5 27.0 reduce-scatter.25.cloned.1.call-done
  548.9 135.6 %all-gather.75.cloned.1.call-done = bf16[2816,1536]{1,0:T(8,128)(2,1)} async-done(((bf16[352,1536]{1,0:T(8,128)(2,1)}), bf16[2816,1536]{1,0:T(8,128)(2,1)}) %all-gather.75.cloned.1.call-update) | async-done | bytes 8650768 | tf_op jit(solution)/shard_map/all_gather | solution.py:208
  684.6 33.6 %all-gather.45.cloned.1.call-done = bf16[1024,1408]{1,0:T(8,128)(2,1)} async-done(((bf16[256,1408]{1,0:T(8,128)(2,1)}), bf16[1024,1408]{1,0:T(8,128)(2,1)}) %all-gather.45.cloned.1.call-update) | async-done | bytes 2883600 | tf_op jit(solution)/shard_map/all_gather | solution.py:180
  745.9 21.6 reduce-scatter.27.cloned.1.call-done
  771.7 77.0 %all-gather.77.cloned.1.call-done = bf16[5632,704]{1,0:T(8,128)(2,1)} async-done(((bf16[176,704]{1,0:T(8,128)(2,1)}), bf16[5632,704]{1,0:T(8,128)(2,1)}) %all-gather.77.cloned.1.call-update) | async-done | bytes 7929872 | tf_op jit(solution)/shard_map/all_gather | solution.py:190
  859.0 73.0 %all-gather.79.cloned.1.call-done = bf16[2816,704]{1,0:T(8,128)(2,1)} async-done(((bf16[352,704]{1,0:T(8,128)(2,1)}), bf16[2816,704]{1,0:T(8,128)(2,1)}) %all-gather.79.cloned.1.call-update) | async-done | bytes 3964944 | tf_op jit(solution)/shard_map/all_gather | solution.py:196
  936.0 29.9 all-gather.47.cloned.1.call-done
  987.3 10.7 rev.45
  1004.0 10.5 rev.46
  1029.9 8.5 fusion.1
  1053.9 29.3 reduce-scatter.29.cloned.1.call-done
  1086.1 47.8 %all-gather.81.cloned.1.call-done = bf16[2048,352]{0,1:T(8,128)(2,1)} async-done(((bf16[256,352]{0,1:T(8,128)(2,1)}), bf16[2048,352]{0,1:T(8,128)(2,1)}) %all-gather.81.cloned.1.call-update) | async-done | bytes 1441808 | tf_op jit(solution)/shard_map/all_gather | solution.py:204
  1138.1 51.9 %all-gather.83.cloned.1.call-done = bf16[2816,352]{1,0:T(8,128)(2,1)} async-done(((bf16[352,352]{1,0:T(8,128)(2,1)}), bf16[2816,352]{1,0:T(8,128)(2,1)}) %all-gather.83.cloned.1.call-update) | async-done | bytes 1982480 | tf_op jit(solution)/shard_map/all_gather | solution.py:200
  1201.3 22.3 all-gather.49.cloned.1.call-done
  1232.3 10.6 rev.47
  1259.3 29.9 reduce-scatter.31.cloned.1.call-done
  1293.8 134.2 %all-gather.85.cloned.1.call-done = bf16[2816,1536]{1,0:T(8,128)(2,1)} async-done(((bf16[352,1536]{1,0:T(8,128)(2,1)}), bf16[2816,1536]{1,0:T(8,128)(2,1)}) %all-gather.85.cloned.1.call-update) | async-done | bytes 8650768 | tf_op jit(solution)/shard_map/all_gather | solution.py:208
  1428.1 33.7 %all-gather.51.cloned.1.call-done = bf16[1024,1408]{1,0:T(8,128)(2,1)} async-done(((bf16[256,1408]{1,0:T(8,128)(2,1)}), bf16[1024,1408]{1,0:T(8,128)(2,1)}) %all-gather.51.cloned.1.call-update) | async-done | bytes 2883600 | tf_op jit(solution)/shard_map/all_gather | solution.py:180
  1468.6 27.6 all-gather.53.cloned.1.call-done
  1532.9 20.6 reduce-scatter.35.cloned.1.call-done
  1557.4 30.4 reduce-scatter.33.cloned.1.call-done
  1593.9 31.5 %all-gather.55.cloned.1.call-done = bf16[1024,1408]{1,0:T(8,128)(2,1)} async-done(((bf16[256,1408]{1,0:T(8,128)(2,1)}), bf16[1024,1408]{1,0:T(8,128)(2,1)}) %all-gather.55.cloned.1.call-update) | async-done | bytes 2883600 | tf_op jit(solution)/shard_map/all_gather | solution.py:180
  1640.6 10.5 rev.48
  1661.5 32.4 %reduce-scatter.37.cloned.1.call-done = bf16[256,1408]{1,0:T(8,128)(2,1)} async-done(((bf16[1024,1408]{1,0:T(8,128)(2,1)}), bf16[256,1408]{1,0:T(8,128)(2,1)}) %reduce-scatter.37.cloned.1.call-update) | async-done | bytes 720912 | tf_op jit(solution)/shard_map/reduce_scatter | solution.py:183
  1698.4 32.6 %all-gather.57.cloned.1.call-done = bf16[1024,1408]{1,0:T(8,128)(2,1)} async-done(((bf16[256,1408]{1,0:T(8,128)(2,1)}), bf16[1024,1408]{1,0:T(8,128)(2,1)}) %all-gather.57.cloned.1.call-update) | async-done | bytes 2883600 | tf_op jit(solution)/shard_map/all_gather | solution.py:180
  1734.4 9.8 fusion.134
  1744.2 13.1 multiply_reduce_fusion.1
  1757.3 10.7 multiply_convert_fusion.1
  1818.6 16.4 copy.310
  1866.4 32.4 %all-gather.59.cloned.1.call-done = bf16[1024,1408]{1,0:T(8,128)(2,1)} async-done(((bf16[256,1408]{1,0:T(8,128)(2,1)}), bf16[1024,1408]{1,0:T(8,128)(2,1)}) %all-gather.59.cloned.1.call-update) | async-done | bytes 2883600 | tf_op jit(solution)/shard_map/all_gather | solution.py:180
  1920.0 32.5 %reduce-scatter.41.cloned.1.call-done = bf16[256,1408]{1,0:T(8,128)(2,1)} async-done(((bf16[1024,1408]{1,0:T(8,128)(2,1)}), bf16[256,1408]{1,0:T(8,128)(2,1)}) %reduce-scatter.41.cloned.1.call-update) | async-done | bytes 720912 | tf_op jit(solution)/shard_map/reduce_scatter | solution.py:183
  1959.7 32.4 %all-gather.61.cloned.1.call-done = bf16[1024,1408]{1,0:T(8,128)(2,1)} async-done(((bf16[256,1408]{1,0:T(8,128)(2,1)}), bf16[1024,1408]{1,0:T(8,128)(2,1)}) %all-gather.61.cloned.1.call-update) | async-done | bytes 2883600 | tf_op jit(solution)/shard_map/all_gather | solution.py:180
  2022.6 32.3 %reduce-scatter.43.cloned.1.call-done = bf16[256,1408]{1,0:T(8,128)(2,1)} async-done(((bf16[1024,1408]{1,0:T(8,128)(2,1)}), bf16[256,1408]{1,0:T(8,128)(2,1)}) %reduce-scatter.43.cloned.1.call-update) | async-done | bytes 720912 | tf_op jit(solution)/shard_map/reduce_scatter | solution.py:183
  2081.9 11.8 all-gather.63.cloned.1.call-done
  2096.9 15.8 multiply_reduce_fusion
  2113.5 10.8 multiply_convert_fusion
  2162.5 9.0 fusion.137
  2205.4 12.4 copy.290
  2286.0 12.6 copy.289
  2324.5 12.2 copy.280
  2336.8 16.3 copy.306
  2376.3 11.8 copy.279
  2399.2 64.2 %all-gather.16 = f32[32,1,1408]{2,1,0:T(1,128)S(1)} all-gather(f32[1,1,1408]{2,1,0:T(1,128)S(1)} %reshape.1058), channel_id=15, replica_groups=mesh['row'=4,'lat'=2,'tp'=4] {'row','lat','tp'}, dimensions={0}, use_global_device_ids=true | all-gather | bytes 185856 | tf_op jit(solution)/shard_map/all_gather | solution.py:385
  2465.7 9.8 reduce-scatter.53.cloned.1.call-done
  2479.8 40.4 %reduce-scatter.59.cloned.1.call-done = bf16[1,256,352]{1,2,0:T(8,128)(2,1)} async-done(((bf16[8,256,352]{1,2,0:T(8,128)(2,1)}), bf16[1,256,352]{1,2,0:T(8,128)(2,1)}) %reduce-scatter.59.cloned.1.call-update) | async-done | bytes 180240 | tf_op jit(solution)/shard_map/reduce_scatter | solution.py:298
  2522.2 58.0 %reduce-scatter.55.cloned.1.call-done = bf16[1,352,352]{2,1,0:T(8,128)(2,1)} async-done(((bf16[8,352,352]{2,1,0:T(8,128)(2,1)}), bf16[1,352,352]{2,1,0:T(8,128)(2,1)}) %reduce-scatter.55.cloned.1.call-update) | async-done | bytes 247824 | tf_op jit(solution)/shard_map/reduce_scatter | solution.py:298
  2584.1 137.2 %reduce-scatter.63.cloned.1.call-done = bf16[1,352,1536]{2,1,0:T(8,128)(2,1)} async-done(((bf16[8,352,1536]{2,1,0:T(8,128)(2,1)}), bf16[1,352,1536]{2,1,0:T(8,128)(2,1)}) %reduce-scatter.63.cloned.1.call-update) | async-done | bytes 1081360 | tf_op jit(solution)/shard_map/reduce_scatter | solution.py:298
  2736.3 41.3 %all-gather.15 = f32[32,1,1408]{2,1,0:T(1,128)S(1)} all-gather(f32[1,1,1408]{2,1,0:T(1,128)S(1)} %reshape.1056), channel_id=14, replica_groups=mesh['row'=4,'lat'=2,'tp'=4] {'row','lat','tp'}, dimensions={0}, use_global_device_ids=true | all-gather | bytes 185856 | tf_op jit(solution)/shard_map/all_gather | solution.py:385
  2781.4 42.5 %all-reduce = (f32[2,2816]{1,0:T(2,128)}, f32[2,2,1408]{2,1,0:T(2,128)}, f32[2,1408]{1,0:T(2,128)}) all-reduce(f32[2,2816]{1,0:T(2,128)S(1)} %pad_maximum_fusion.77, f32[2,2,1408]{2,1,0:T(2,128)S(1)} %pad_maximum_fusion.78, f32[2,1408]{1,0:T(2,128)S(1)} %pad_maximum_fusion.79), channel_id=1, replica_groups=mesh['row'=4,'lat'=2,'tp'=4] {'row','lat','tp'}, use_global_device_ids=true, to_apply=%region_94.95 | all-reduce | flops 14080 | bytes 112640 | tf_op jit(solution)/shard_map/psum | solution.py:430
  2837.8 108.4 %reduce-scatter.49.cloned.1.call-done = bf16[1,176,704]{2,1,0:T(8,128)(2,1)} async-done(((bf16[32,176,704]{2,1,0:T(8,128)(2,1)}), bf16[1,176,704]{2,1,0:T(8,128)(2,1)}) %reduce-scatter.49.cloned.1.call-update) | async-done | bytes 247824 | tf_op jit(solution)/shard_map/reduce_scatter | solution.py:404
  2946.2 136.8 %reduce-scatter.47.cloned.1.call-done = bf16[1,176,704]{2,1,0:T(8,128)(2,1)} async-done(((bf16[32,176,704]{2,1,0:T(8,128)(2,1)}), bf16[1,176,704]{2,1,0:T(8,128)(2,1)}) %reduce-scatter.47.cloned.1.call-update) | async-done | bytes 247824 | tf_op jit(solution)/shard_map/reduce_scatter | solution.py:404
  (1276 shorter events, 802.3 us)
Async XLA Ops:
  8.0 87.9 %all-gather.65.cloned.1.call-start = ((), (), s32[]{:S(2)}) async-start(), calls=%async_computation.57 | async-start | bytes 8921088 | tf_op jit(solution)/shard_map/all_gather | solution.py:190
  10.1 169.1 %all-gather.67.cloned.1.call-start = ((), (), s32[]{:S(2)}) async-start(), calls=%async_computation.58 | async-start | bytes 4866048 | tf_op jit(solution)/shard_map/all_gather | solution.py:196
  14.3 198.9 %all-gather.41.cloned.1.call-start = ((), (), s32[]{:S(2)}) async-start(), calls=%async_computation.23 | async-start | bytes 3604480 | tf_op jit(solution)/shard_map/all_gather | solution.py:180
  14.4 69.5 %copy-start.48 = (f32[256,1408]{1,0:T(8,128)}, f32[256,1408]{1,0:T(8,128)S(1)}, u32[]{:S(2)}) copy-start(f32[256,1408]{1,0:T(8,128)S(1)} %convert_element_type.621) | copy-start | bytes 4325380
  26.4 69.6 %copy-start.237 = (f32[4,704]{1,0:T(4,128)}, f32[4,704]{1,0:T(4,128)S(1)}, u32[]{:S(2)}) copy-start(f32[4,704]{1,0:T(4,128)S(1)} %mul.1491) | copy-start | bytes 33796
  80.5 258.8 %copy-start.217 = (f32[1408]{0:T(1024)}, f32[1408]{0:T(1024)S(1)}, u32[]{:S(2)}) copy-start(f32[1408]{0:T(1024)S(1)} %get-tuple-element.141) | copy-start | bytes 16900
  103.9 77.2 %copy-start.269 = (f32[256]{0:T(256)}, f32[256]{0:T(256)S(1)}, u32[]{:S(2)}) copy-start(f32[256]{0:T(256)S(1)} %add_rsqrt_fusion.14) | copy-start | bytes 3076
  105.9 231.6 %reduce-scatter.23.cloned.1.call-start = ((), (), s32[]{:S(2)}) async-start(), calls=%async_computation.24 | async-start | bytes 3604480 | tf_op jit(solution)/shard_map/reduce_scatter | solution.py:183
  295.4 45.1 %all-gather.71.cloned.1.call-start = ((), (), s32[]{:S(2)}) async-start(), calls=%async_computation.60 | async-start | bytes 1548288 | tf_op jit(solution)/shard_map/all_gather | solution.py:225
  297.0 93.2 %all-gather.69.cloned.1.call-start = ((), (), s32[]{:S(2)}) async-start(), calls=%async_computation.59 | async-start | bytes 1622016 | tf_op jit(solution)/shard_map/all_gather | solution.py:204
  298.5 147.7 %all-gather.73.cloned.1.call-start = ((), (), s32[]{:S(2)}) async-start(), calls=%async_computation.61 | async-start | bytes 2433024 | tf_op jit(solution)/shard_map/all_gather | solution.py:200
  301.0 178.8 %all-gather.43.cloned.1.call-start = ((), (), s32[]{:S(2)}) async-start(), calls=%async_computation.25 | async-start | bytes 3604480 | tf_op jit(solution)/shard_map/all_gather | solution.py:180
  338.9 206.6 %copy-start.18 = (f32[256,1408]{1,0:T(8,128)}, f32[256,1408]{1,0:T(8,128)S(1)}, u32[]{:S(2)}) copy-start(f32[256,1408]{1,0:T(8,128)S(1)} %get-tuple-element.176) | copy-start | bytes 4325380
  340.5 205.1 %reduce-scatter.25.cloned.1.call-start = ((), (), s32[]{:S(2)}) async-start(), calls=%async_computation.26 | async-start | bytes 3604480 | tf_op jit(solution)/shard_map/reduce_scatter | solution.py:183
  342.1 50.6 %copy-start.39 = (bf16[42,8,8,128]{3,1,2,0:T(8,128)(2,1)}, bf16[42,8,8,128]{3,1,2,0:T(8,128)(2,1)S(1)}, u32[]{:S(2)}) copy-start(bf16[42,8,8,128]{3,1,2,0:T(8,128)(2,1)S(1)} %copy.393) | copy-start | bytes 2064388
  393.2 113.0 %copy-start.124 = (bf16[352,333]{1,0:T(8,128)(2,1)}, bf16[352,333]{1,0:T(8,128)(2,1)S(1)}, u32[]{:S(2)}) copy-start(bf16[352,333]{1,0:T(8,128)(2,1)S(1)} %copy.248) | copy-start | bytes 703300
  393.6 56.3 %copy-start.27 = (f32[352,333]{1,0:T(8,128)}, f32[352,333]{1,0:T(8,128)S(1)}, u32[]{:S(2)}) copy-start(f32[352,333]{1,0:T(8,128)S(1)} %copy.252) | copy-start | bytes 1406596
  393.7 110.6 %copy-start.199 = (f32[4,333]{1,0:T(4,128)}, f32[4,333]{1,0:T(4,128)S(1)}, u32[]{:S(2)}) copy-start(f32[4,333]{1,0:T(4,128)S(1)} %broadcast_multiply_fusion.30) | copy-start | bytes 15988
  513.2 171.3 %all-gather.75.cloned.1.call-start = ((), (), s32[]{:S(2)}) async-start(), calls=%async_computation.62 | async-start | bytes 9732096 | tf_op jit(solution)/shard_map/all_gather | solution.py:208
  517.8 200.3 %all-gather.45.cloned.1.call-start = ((), (), s32[]{:S(2)}) async-start(), calls=%async_computation.27 | async-start | bytes 3604480 | tf_op jit(solution)/shard_map/all_gather | solution.py:180
  546.9 220.5 %copy-start.14 = (f32[256,1408]{1,0:T(8,128)}, f32[256,1408]{1,0:T(8,128)S(1)}, u32[]{:S(2)}) copy-start(f32[256,1408]{1,0:T(8,128)S(1)} %get-tuple-element.174) | copy-start | bytes 4325380
  547.2 176.1 %copy-start.273 = (f32[256]{0:T(256)}, f32[256]{0:T(256)S(1)}, u32[]{:S(2)}) copy-start(f32[256]{0:T(256)S(1)} %add_rsqrt_fusion.12) | copy-start | bytes 3076
  548.4 219.0 %reduce-scatter.27.cloned.1.call-start = ((), (), s32[]{:S(2)}) async-start(), calls=%async_computation.28 | async-start | bytes 3604480 | tf_op jit(solution)/shard_map/reduce_scatter | solution.py:183
  734.9 113.8 %all-gather.77.cloned.1.call-start = ((), (), s32[]{:S(2)}) async-start(), calls=%async_computation.63 | async-start | bytes 8921088 | tf_op jit(solution)/shard_map/all_gather | solution.py:190
  735.5 196.5 %all-gather.79.cloned.1.call-start = ((), (), s32[]{:S(2)}) async-start(), calls=%async_computation.64 | async-start | bytes 4866048 | tf_op jit(solution)/shard_map/all_gather | solution.py:196
  743.9 222.0 %all-gather.47.cloned.1.call-start = ((), (), s32[]{:S(2)}) async-start(), calls=%async_computation.29 | async-start | bytes 3604480 | tf_op jit(solution)/shard_map/all_gather | solution.py:180
  744.2 104.5 %copy-start.239 = (f32[4,704]{1,0:T(4,128)}, f32[4,704]{1,0:T(4,128)S(1)}, u32[]{:S(2)}) copy-start(f32[4,704]{1,0:T(4,128)S(1)} %mul.1566) | copy-start | bytes 33796
  770.4 86.0 %copy-start.266 = (f32[256]{0:T(256)}, f32[256]{0:T(256)S(1)}, u32[]{:S(2)}) copy-start(f32[256]{0:T(256)S(1)} %add_multiply_fusion) | copy-start | bytes 3076
  771.7 84.7 %copy-start.285 = (f32[256]{0:T(256)}, f32[256]{0:T(256)S(1)}, u32[]{:S(2)}) copy-start(f32[256]{0:T(256)S(1)} %add_rsqrt_fusion.11) | copy-start | bytes 3076
  856.7 77.2 %copy-start.275 = (f32[256]{0:T(256)}, f32[256]{0:T(256)S(1)}, u32[]{:S(2)}) copy-start(f32[256]{0:T(256)S(1)} %add_rsqrt_fusion.10) | copy-start | bytes 3076
  858.7 224.5 %reduce-scatter.29.cloned.1.call-start = ((), (), s32[]{:S(2)}) async-start(), calls=%async_computation.30 | async-start | bytes 3604480 | tf_op jit(solution)/shard_map/reduce_scatter | solution.py:183
  1051.0 82.9 %all-gather.81.cloned.1.call-start = ((), (), s32[]{:S(2)}) async-start(), calls=%async_computation.65 | async-start | bytes 1622016 | tf_op jit(solution)/shard_map/all_gather | solution.py:204
  1052.6 137.4 %all-gather.83.cloned.1.call-start = ((), (), s32[]{:S(2)}) async-start(), calls=%async_computation.66 | async-start | bytes 2433024 | tf_op jit(solution)/shard_map/all_gather | solution.py:200
  1053.8 169.8 %all-gather.49.cloned.1.call-start = ((), (), s32[]{:S(2)}) async-start(), calls=%async_computation.31 | async-start | bytes 3604480 | tf_op jit(solution)/shard_map/all_gather | solution.py:180
  1084.6 49.4 %copy-start.40 = (bf16[42,8,8,128]{3,1,2,0:T(8,128)(2,1)S(1)}, bf16[42,8,8,128]{3,1,2,0:T(8,128)(2,1)}, u32[]{:S(2)}) copy-start(bf16[42,8,8,128]{3,1,2,0:T(8,128)(2,1)} %copy-done.39) | copy-start | bytes 2064388
  1086.1 203.1 %reduce-scatter.31.cloned.1.call-start = ((), (), s32[]{:S(2)}) async-start(), calls=%async_computation.32 | async-start | bytes 3604480 | tf_op jit(solution)/shard_map/reduce_scatter | solution.py:183
  1137.3 56.4 %copy-start.31 = (f32[352,333]{1,0:T(8,128)}, f32[352,333]{1,0:T(8,128)S(1)}, u32[]{:S(2)}) copy-start(f32[352,333]{1,0:T(8,128)S(1)} %copy.267) | copy-start | bytes 1406596
  1256.9 171.2 %all-gather.85.cloned.1.call-start = ((), (), s32[]{:S(2)}) async-start(), calls=%async_computation.67 | async-start | bytes 9732096 | tf_op jit(solution)/shard_map/all_gather | solution.py:208
  1259.2 202.6 %all-gather.51.cloned.1.call-start = ((), (), s32[]{:S(2)}) async-start(), calls=%async_computation.33 | async-start | bytes 3604480 | tf_op jit(solution)/shard_map/all_gather | solution.py:180
  1292.8 203.4 %all-gather.53.cloned.1.call-start = ((), (), s32[]{:S(2)}) async-start(), calls=%async_computation.35 | async-start | bytes 3604480 | tf_op jit(solution)/shard_map/all_gather | solution.py:180
  1293.6 260.0 %reduce-scatter.35.cloned.1.call-start = ((), (), s32[]{:S(2)}) async-start(), calls=%async_computation.36 | async-start | bytes 3604480 | tf_op jit(solution)/shard_map/reduce_scatter | solution.py:183
  1521.0 66.9 %reduce-scatter.33.cloned.1.call-start = ((), (), s32[]{:S(2)}) async-start(), calls=%async_computation.34 | async-start | bytes 3604480 | tf_op jit(solution)/shard_map/reduce_scatter | solution.py:183
  1532.9 92.6 %all-gather.55.cloned.1.call-start = ((), (), s32[]{:S(2)}) async-start(), calls=%async_computation.37 | async-start | bytes 3604480 | tf_op jit(solution)/shard_map/all_gather | solution.py:180
  1592.5 101.4 %reduce-scatter.37.cloned.1.call-start = ((), (), s32[]{:S(2)}) async-start(), calls=%async_computation.38 | async-start | bytes 3604480 | tf_op jit(solution)/shard_map/reduce_scatter | solution.py:183
  1661.4 69.5 %all-gather.57.cloned.1.call-start = ((), (), s32[]{:S(2)}) async-start(), calls=%async_computation.39 | async-start | bytes 3604480 | tf_op jit(solution)/shard_map/all_gather | solution.py:180
  1698.3 152.8 %reduce-scatter.39.cloned.1.call-start = ((), (), s32[]{:S(2)}) async-start(), calls=%async_computation.40 | async-start | bytes 3604480 | tf_op jit(solution)/shard_map/reduce_scatter | solution.py:183
  1818.5 80.3 %all-gather.59.cloned.1.call-start = ((), (), s32[]{:S(2)}) async-start(), calls=%async_computation.41 | async-start | bytes 3604480 | tf_op jit(solution)/shard_map/all_gather | solution.py:180
  1866.1 86.4 %reduce-scatter.41.cloned.1.call-start = ((), (), s32[]{:S(2)}) async-start(), calls=%async_computation.42 | async-start | bytes 3604480 | tf_op jit(solution)/shard_map/reduce_scatter | solution.py:183
  1920.0 72.0 %all-gather.61.cloned.1.call-start = ((), (), s32[]{:S(2)}) async-start(), calls=%async_computation.43 | async-start | bytes 3604480 | tf_op jit(solution)/shard_map/all_gather | solution.py:180
  1959.3 95.5 %reduce-scatter.43.cloned.1.call-start = ((), (), s32[]{:S(2)}) async-start(), calls=%async_computation.44 | async-start | bytes 3604480 | tf_op jit(solution)/shard_map/reduce_scatter | solution.py:183
  2022.6 71.1 %all-gather.63.cloned.1.call-start = ((), (), s32[]{:S(2)}) async-start(), calls=%async_computation.45 | async-start | bytes 3604480 | tf_op jit(solution)/shard_map/all_gather | solution.py:180
  2060.8 303.1 %reduce-scatter.61.cloned.1.call-start = ((), (), s32[]{:S(2)}) async-start(), calls=%async_computation.54 | async-start | bytes 1622016 | tf_op jit(solution)/shard_map/reduce_scatter | solution.py:298
  2073.8 291.2 %reduce-scatter.57.cloned.1.call-start = ((), (), s32[]{:S(2)}) async-start(), calls=%async_computation.52 | async-start | bytes 2433024 | tf_op jit(solution)/shard_map/reduce_scatter | solution.py:298
  2081.6 285.3 %reduce-scatter.45.cloned.1.call-start = ((), (), s32[]{:S(2)}) async-start(), calls=%async_computation.46 | async-start | bytes 3604480 | tf_op jit(solution)/shard_map/reduce_scatter | solution.py:183
  2179.5 210.0 %reduce-scatter.65.cloned.1.call-start = ((), (), s32[]{:S(2)}) async-start(), calls=%async_computation.56 | async-start | bytes 9732096 | tf_op jit(solution)/shard_map/reduce_scatter | solution.py:298
  2217.9 257.6 %reduce-scatter.53.cloned.1.call-start = ((), (), s32[]{:S(2)}) async-start(), calls=%async_computation.50 | async-start | bytes 4866048 | tf_op jit(solution)/shard_map/reduce_scatter | solution.py:298
  2236.2 284.1 %reduce-scatter.59.cloned.1.call-start = ((), (), s32[]{:S(2)}) async-start(), calls=%async_computation.53 | async-start | bytes 1622016 | tf_op jit(solution)/shard_map/reduce_scatter | solution.py:298
  2249.9 330.2 %reduce-scatter.55.cloned.1.call-start = ((), (), s32[]{:S(2)}) async-start(), calls=%async_computation.51 | async-start | bytes 2433024 | tf_op jit(solution)/shard_map/reduce_scatter | solution.py:298
  2263.1 458.3 %reduce-scatter.63.cloned.1.call-start = ((), (), s32[]{:S(2)}) async-start(), calls=%async_computation.55 | async-start | bytes 9732096 | tf_op jit(solution)/shard_map/reduce_scatter | solution.py:298
  2298.7 534.2 %reduce-scatter.51.cloned.1.call-start = ((), (), s32[]{:S(2)}) async-start(), calls=%async_computation.49 | async-start | bytes 4866048 | tf_op jit(solution)/shard_map/reduce_scatter | solution.py:298
  2316.9 629.3 %reduce-scatter.49.cloned.1.call-start = ((), (), s32[]{:S(2)}) async-start(), calls=%async_computation.48 | async-start | bytes 8921088 | tf_op jit(solution)/shard_map/reduce_scatter | solution.py:404
  2336.7 746.3 %reduce-scatter.47.cloned.1.call-start = ((), (), s32[]{:S(2)}) async-start(), calls=%async_computation.47 | async-start | bytes 8921088 | tf_op jit(solution)/shard_map/reduce_scatter | solution.py:404
  2395.4 83.4 %all-to-all-start = ((bf16[8,333,128]{2,1,0:T(8,128)(2,1)}), bf16[8,333,128]{2,1,0:T(8,128)(2,1)S(1)}, u32[]{:S(2)}, u32[]{:S(2)}) async-start(bf16[8,333,128]{2,1,0:T(8,128)(2,1)} %bitcast.508), calls=%async_computation.12 | async-start | bytes 1376256 | tf_op jit(solution)/shard_map/all_to_all | solution.py:433
  2835.8 249.3 %copy-start.1 = (bf16[2,352,176]{1,2,0:T(8,128)(2,1)S(1)}, bf16[2,352,176]{1,2,0:T(8,128)(2,1)}, u32[]{:S(2)}) copy-start(bf16[2,352,176]{1,2,0:T(8,128)(2,1)} %param.25) | copy-start | bytes 743428
  (328 other events, 2511.7 us)
Sparse Core Ops, SparseCore 0:
  12.5 83.3 all-gather.64
  98.7 80.3 all-gather.66
  181.3 31.7 all-gather.40
  295.5 42.0 reduce-scatter.22
  735.0 32.4 reduce-scatter.26
  770.3 78.3 all-gather.76
  851.5 80.3 all-gather.78
  934.0 31.7 all-gather.46
  1521.1 32.3 reduce-scatter.34
  1555.7 32.1 reduce-scatter.32
  1592.6 32.7 all-gather.54
  1661.5 32.3 reduce-scatter.36
  1818.6 32.4 reduce-scatter.38
  1920.1 32.3 reduce-scatter.40
  2060.8 32.7 all-gather.62
  2095.8 43.1 reduce-scatter.60
  2143.3 54.8 reduce-scatter.56
  2201.0 30.9 reduce-scatter.44
  2236.3 137.2 reduce-scatter.64
  2378.1 97.3 reduce-scatter.52
  2478.5 41.7 reduce-scatter.58
  2525.2 54.9 reduce-scatter.54
  2585.1 136.1 reduce-scatter.62
  2725.2 84.0 reduce-scatter.50
  2815.3 130.8 reduce-scatter.48
  2952.0 131.0 reduce-scatter.46
Sparse Core Ops, SparseCore 1:
  298.1 41.3 all-gather.70
  342.1 48.0 all-gather.68
  392.9 53.2 all-gather.72
  448.3 31.5 all-gather.42
  513.3 32.2 reduce-scatter.24
  548.4 136.2 all-gather.74
  686.6 31.5 all-gather.44
  1051.1 32.1 reduce-scatter.28
  1085.8 48.1 all-gather.80
  1136.8 53.2 all-gather.82
  1192.1 31.5 all-gather.48
  1257.0 32.2 reduce-scatter.30
  1291.8 136.2 all-gather.84
  1430.2 31.5 all-gather.50
  1463.4 32.8 all-gather.52
  1698.4 32.5 all-gather.56
  1866.2 32.5 all-gather.58
  1959.4 32.5 all-gather.60
  2022.6 32.2 reduce-scatter.42

commit v2 on v1

v2 whole, which is shorter than its diff:
```python
import functools

import jax
import jax.numpy as jnp
from jax import lax
from jax.experimental import pallas as pl
from jax.experimental.pallas import tpu as pltpu
from jax.sharding import Mesh
from jax.sharding import PartitionSpec as P

HD = 88
SIDE = 32
SEQ = 1024
LATENTS = 2

HIGHEST = lax.Precision.HIGHEST
EPSILON = 1e-06
F32 = jnp.float32
B16 = jnp.bfloat16
SCALE = HD ** (-0.5)
VMEM_LIMIT = 48 * 2**20


def norm_stats(value):
    center = value - jnp.mean(value, axis=-1, keepdims=True)
    spread = jnp.mean(center * center, axis=-1, keepdims=True)
    rstd = lax.rsqrt(spread + EPSILON)
    return center * rstd, rstd


def norm_back(normed, rstd, grad):
    return rstd * (
        grad
        - jnp.mean(grad, axis=-1, keepdims=True)
        - normed * jnp.mean(grad * normed, axis=-1, keepdims=True)
    )


def silu(value):
    return value * jax.nn.sigmoid(value)


def gelu_tanh(value):
    inner = 0.7978845608028654 * (value + 0.044715 * value * value * value)
    return 0.5 * value * (1.0 + jnp.tanh(inner))


def gelu_grad(value):
    inner = 0.7978845608028654 * (value + 0.044715 * value * value * value)
    tanh = jnp.tanh(inner)
    slope = 0.7978845608028654 * (1.0 + 3.0 * 0.044715 * value * value)
    return 0.5 * (1.0 + tanh) + 0.5 * value * (1.0 - tanh * tanh) * slope


def rotary_tables():
    place = jnp.arange(SEQ, dtype=jnp.int32)
    grid_row = (place // SIDE).astype(F32)
    grid_col = (place % SIDE).astype(F32)
    feature = jnp.arange(HD, dtype=jnp.int32)
    pair = feature // 2
    quarter = HD // 4
    power = (pair % quarter).astype(F32) * (4.0 / HD)
    freq = jnp.exp(-power * jnp.log(10000.0))
    coordinate = jnp.where(pair[:, None] < quarter, grid_row[None, :], grid_col[None, :])
    angle = coordinate * freq[:, None]
    sign = jnp.where(feature % 2 == 0, -1.0, 1.0)[:, None]
    return (jnp.cos(angle), jnp.sin(angle) * sign)


def swap_rows(value):
    down = pltpu.roll(value, 1, 0)
    up = pltpu.roll(value, value.shape[0] - 1, 0)
    even = lax.broadcasted_iota(jnp.int32, value.shape, 0) % 2 == 0
    return jnp.where(even, up, down)


def head_stats(value):
    center = value - jnp.mean(value, axis=0, keepdims=True)
    rstd = lax.rsqrt(jnp.mean(center * center, axis=0, keepdims=True) + EPSILON)
    return center * rstd, rstd


def head_back(normed, rstd, grad):
    return rstd * (
        grad
        - jnp.mean(grad, axis=0, keepdims=True)
        - normed * jnp.mean(grad * normed, axis=0, keepdims=True)
    )


QUERY_CHUNK = 512


def attention_kernel(
    count, turn, query_ref, keys_ref, values_ref, cos_ref, sin_ref, out_ref, logsum_ref
):
    cos, sin = cos_ref[...], sin_ref[...]
    query = head_stats(query_ref[...])[0]
    query_low = (query * cos + swap_rows(query) * sin).astype(B16)
    keys = head_stats(keys_ref[...])[0]
    if turn:
        keys = keys * cos + swap_rows(keys) * sin
    keys_t = keys.astype(B16).T
    values_low = values_ref[...].astype(B16)
    for start in range(0, query_low.shape[1], QUERY_CHUNK):
        span = slice(start, start + QUERY_CHUNK)
        scores = jnp.dot(keys_t, query_low[:, span], preferred_element_type=F32) * SCALE
        if count < keys_t.shape[0]:
            inside = lax.broadcasted_iota(jnp.int32, scores.shape, 0) < count
            scores = jnp.where(inside, scores, -1e30)
        highest = jnp.max(scores, axis=0, keepdims=True)
        expo = jnp.exp(scores - highest)
        total = jnp.sum(expo, axis=0, keepdims=True)
        probs_low = (expo * (1.0 / total)).astype(B16)
        out = jnp.dot(values_low, probs_low, preferred_element_type=F32)
        out_ref[:, span] = out.astype(B16)
        logsum_ref[0, :, span] = highest + jnp.log(total)


def attention_back_kernel(
    count,
    turn,
    query_ref,
    keys_ref,
    values_ref,
    logsum_ref,
    grad_ref,
    cos_ref,
    sin_ref,
    query_out,
    keys_out,
    values_out,
    keys_sum,
    values_sum,
):
    cos, sin = cos_ref[...], sin_ref[...]
    query, query_rstd = head_stats(query_ref[...])
    query_low = (query * cos + swap_rows(query) * sin).astype(B16)
    keys, keys_rstd = head_stats(keys_ref[...])
    keys_low = (keys * cos + swap_rows(keys) * sin if turn else keys).astype(B16)
    keys_t = keys_low.T
    values_t = values_ref[...].astype(B16).T
    grad = grad_ref[...]
    grad_t = grad.T
    query_t = query_low.T
    query_grad = []
    for start in range(0, query_low.shape[1], QUERY_CHUNK):
        span = slice(start, start + QUERY_CHUNK)
        scores = jnp.dot(keys_t, query_low[:, span], preferred_element_type=F32)
        probs = jnp.exp(scores * SCALE - logsum_ref[0, :, span])
        if count < keys_t.shape[0]:
            inside = lax.broadcasted_iota(jnp.int32, scores.shape, 0) < count
            probs = jnp.where(inside, probs, 0.0)
        values_part = jnp.dot(probs.astype(B16), grad_t[span], preferred_element_type=F32)
        probs_grad = jnp.dot(values_t, grad[:, span], preferred_element_type=F32)
        delta = jnp.sum(probs * probs_grad, axis=0, keepdims=True)
        scores_grad = (probs * (probs_grad - delta)).astype(B16)
        query_grad.append(jnp.dot(keys_low, scores_grad, preferred_element_type=F32))
        keys_part = jnp.dot(scores_grad, query_t[span], preferred_element_type=F32)
        if start == 0:
            values_sum[...] = values_part
            keys_sum[...] = keys_part
        else:
            values_sum[...] += values_part
            keys_sum[...] += keys_part
    grad_query = jnp.concatenate(query_grad, axis=1) * SCALE
    grad_query = grad_query * cos - swap_rows(grad_query) * sin
    query_out[...] = head_back(query, query_rstd, grad_query).astype(B16)
    grad_keys = keys_sum[...].T * SCALE
    if turn:
        grad_keys = grad_keys * cos - swap_rows(grad_keys) * sin
    keys_out[...] = head_back(keys, keys_rstd, grad_keys).astype(B16)
    values_out[...] = values_sum[...].T.astype(B16)


def head_block(columns):
    return pl.BlockSpec((HD, columns), lambda head: (head, 0))


def logsum_block(columns):
    return pl.BlockSpec((1, 1, columns), lambda head: (head, 0, 0))


def attention(query, keys, values, tables, count, turn):
    heads, tokens, others = query.shape[0] // HD, query.shape[1], keys.shape[1]
    table = pl.BlockSpec((HD, tokens), lambda head: (0, 0))
    work = heads * tokens * others
    return pl.pallas_call(
        functools.partial(attention_kernel, count, turn),
        grid=(heads,),
        in_specs=[head_block(tokens), head_block(others), head_block(others), table, table],
        out_specs=[head_block(tokens), logsum_block(tokens)],
        out_shape=[
            jax.ShapeDtypeStruct(query.shape, B16),
            jax.ShapeDtypeStruct((heads, 1, tokens), F32),
        ],
        compiler_params=pltpu.CompilerParams(vmem_limit_bytes=VMEM_LIMIT),
        cost_estimate=pl.CostEstimate(
            flops=4 * HD * work, bytes_accessed=8 * query.size, transcendentals=work
        ),
    )(query, keys, values, *tables)


def attention_back(query, keys, values, logsum, grad_low, tables, count, turn):
    heads, tokens, others = query.shape[0] // HD, query.shape[1], keys.shape[1]
    table = pl.BlockSpec((HD, tokens), lambda head: (0, 0))
    work = heads * tokens * others
    return pl.pallas_call(
        functools.partial(attention_back_kernel, count, turn),
        grid=(heads,),
        in_specs=[
            head_block(tokens),
            head_block(others),
            head_block(others),
            logsum_block(tokens),
            head_block(tokens),
            table,
            table,
        ],
        out_specs=[head_block(tokens), head_block(others), head_block(others)],
        out_shape=[
            jax.ShapeDtypeStruct(value.shape, B16) for value in (query, keys, values)
        ],
        scratch_shapes=[pltpu.VMEM((others, HD), F32), pltpu.VMEM((others, HD), F32)],
        compiler_params=pltpu.CompilerParams(vmem_limit_bytes=VMEM_LIMIT),
        cost_estimate=pl.CostEstimate(
            flops=10 * HD * work, bytes_accessed=16 * query.size, transcendentals=work
        ),
    )(query, keys, values, logsum, grad_low, *tables)


MESH = pl.DeviceIdType.MESH
CHUNKS = 4
NUMBERS = {}


def number_of(name, key):
    return NUMBERS.setdefault((name, key), len(NUMBERS))


def here():
    return lax.axis_index("row"), lax.axis_index("lat"), lax.axis_index("tp")


def device_at(row, lat, rank):
    return {"row": row, "lat": lat, "tp": rank}


def row_peers():
    row, lat, rank = here()
    rows = lax.axis_size("row")
    return [((row + step) % rows, device_at((row + step) % rows, lat, rank)) for step in range(1, rows)]


def peers_along(axis):
    row, lat, rank = here()
    if axis == "lat":
        return lat, LATENTS, [(1 - lat, device_at(row, 1 - lat, rank))]
    fast = lax.axis_size("row") // 2
    slow_at, fast_at = row // fast, row % fast
    if axis == "a":
        other = 1 - slow_at
        return slow_at, 2, [(other, device_at(other * fast + fast_at, lat, rank))]
    others = [(fast_at + step) % fast for step in range(1, fast)]
    return fast_at, fast, [(other, device_at(slow_at * fast + other, lat, rank)) for other in others]


def lat_peer():
    return peers_along("lat")[2][0][1]


def places():
    row, lat, rank = here()
    chips = lax.axis_size("tp") // 2
    chip, core = rank // 2, rank % 2
    sibling = device_at(row, lat, 2 * chip + 1 - core)
    ahead = [(chip + step) % chips for step in range(1, chips)]
    behind = [(chip + chips - step) % chips for step in range(1, chips)]
    return rank, chip, core, sibling, ahead, behind


def chip_peer(chip, core):
    row, lat, _ = here()
    return device_at(row, lat, 2 * chip + core)


def greet(others):
    barrier = pltpu.get_barrier_semaphore()
    for device in others:
        pl.semaphore_signal(barrier, inc=1, device_id=device, device_id_type=MESH)
    pl.semaphore_wait(barrier, len(others))


def remote(source, target, sems, index, device):
    return pltpu.make_async_remote_copy(
        src_ref=source,
        dst_ref=target,
        send_sem=sems.at[0, index],
        recv_sem=sems.at[1, index],
        device_id=device,
        device_id_type=MESH,
    )


def rider_count(axis):
    return {"lat": LATENTS, "a": 2, "b": lax.axis_size("row") // 2}[axis]


def rider_shape(rider):
    kind, axis, place, part, array = rider
    shape = array.shape if part is None else array.shape[1:]
    if kind == "gather":
        shape = shape[:place] + (rider_count(axis),) + shape[place:]
    if kind == "scatter":
        shape = (rider_count(axis) - 1,) + shape[:place] + shape[place + 1 :]
    return jax.ShapeDtypeStruct(shape, array.dtype)


def rider_scratch(modes):
    if not modes:
        return []
    most = sum(rider_count(mode[1]) for mode in modes)
    return [pltpu.SemaphoreType.DMA((2, most)), pltpu.SemaphoreType.DMA((len(modes),))]


def rider_peers(modes, met=()):
    peers = []
    for axis in ("lat", "a", "b"):
        if axis not in met and any(mode[1] == axis for mode in modes):
            peers += [device for _, device in peers_along(axis)[2]]
    return peers


def piece_of(ref, place, index):
    return ref.at[index] if place == 0 else ref.at[:, index]


def start_riders(modes, sources, targets, sems, local_sems):
    copies, index = [], 0
    for order, (mode, source, target) in enumerate(zip(modes, sources, targets)):
        kind, axis, place, part = mode
        me, _, others = peers_along(axis)
        if part is not None:
            source = source.at[part]
        for step, (other, device) in enumerate(others):
            if kind == "swap":
                copies.append(remote(source, target, sems, index, device))
            if kind == "gather":
                copies.append(remote(source, piece_of(target, place, me), sems, index, device))
            if kind == "scatter":
                piece = piece_of(source, place, other)
                copies.append(remote(piece, target.at[step], sems, index, device))
            index += 1
        if kind == "gather":
            own = piece_of(target, place, me)
            copies.append(pltpu.make_async_copy(source, own, local_sems.at[order]))
    for copy in copies:
        copy.start()
    return copies


def split_riders(riders):
    modes = tuple(rider[:4] for rider in riders)
    key = tuple((mode, rider[4].shape) for mode, rider in zip(modes, riders))
    return modes, key, [rider[4] for rider in riders], [rider_shape(rider) for rider in riders]


def swap(array):
    return ("swap", "lat", 0, None, array)


def gather_everyone(source, target, sems, local_sem, between):
    row, lat, _ = here()
    ranks = lax.axis_size("tp")
    rank, chip, core, sibling, ahead, _ = places()
    chips = ranks // 2
    fast_at, fast, fast_peers = peers_along("b")
    slow_at, slow, slow_peers = peers_along("a")
    counter = iter(range(sems.shape[1]))
    sent, last = [], []

    def block(at_row, at_lat, at_rank):
        return target.at[at_row, at_lat * ranks + at_rank]

    def push(piece, device, kept):
        copy = remote(piece, piece, sems, next(counter), device)
        copy.start()
        kept.append(copy)

    def landed(copies):
        for copy in copies:
            copy.wait_recv()
        sent.extend(copies)

    mine = block(row, lat, rank)
    local = pltpu.make_async_copy(source, mine, local_sem.at[0])
    local.start()
    first = remote(source, mine, sems, next(counter), lat_peer())
    first.start()

    def finish():
        local.wait()
        landed([first])
        between()
        step = []
        for place in ahead:
            for at_lat in range(LATENTS):
                push(block(row, at_lat, rank), chip_peer(place, core), step)
        landed(step)
        step = []
        for place in range(chips):
            at_rank = 2 * place + core
            for _, device in fast_peers:
                push(block(row, 0, at_rank), device, step)
            for _, device in slow_peers:
                push(block(row, 1, at_rank), device, step)
        for place in range(chips):
            for at_lat in range(LATENTS):
                push(block(row, at_lat, 2 * place + core), sibling, last)
        landed(step)
        step = []
        for place in range(chips):
            at_rank = 2 * place + core
            for index in range(fast):
                for _, device in slow_peers:
                    push(block(slow_at * fast + index, 0, at_rank), device, step)
            for index in range(slow):
                for _, device in fast_peers:
                    push(block(index * fast + fast_at, 1, at_rank), device, step)
        for place in range(chips):
            at_rank = 2 * place + core
            for index, _ in fast_peers:
                push(block(slow_at * fast + index, 0, at_rank), sibling, last)
            for index, _ in slow_peers:
                push(block(index * fast + fast_at, 1, at_rank), sibling, last)
        landed(step)
        for place in range(chips):
            at_rank = 2 * place + core
            for other, _ in slow_peers:
                for index in range(fast):
                    push(block(other * fast + index, 0, at_rank), sibling, last)
            for other, _ in fast_peers:
                for index in range(slow):
                    push(block(index * fast + other, 1, at_rank), sibling, last)
        for copy in sent:
            copy.wait_send()
        for copy in last:
            copy.wait()

    return finish


def gather_copies():
    rows, chips = lax.axis_size("row"), lax.axis_size("tp") // 2
    fast, slow = rows // 2, 2
    count = 1 + (chips - 1) * LATENTS + chips * (fast - 1 + slow - 1)
    count += chips * (fast * (slow - 1) + slow * (fast - 1))
    return count + chips * LATENTS * rows


def token_kernel(sums, spreads, body, n_in, n_out, modes, shared, *refs):
    refs = list(refs)
    take = lambda count: [refs.pop(0) for _ in range(count)]
    part = refs.pop(0) if sums else None
    ins, sources = take(n_in), take(len(modes))
    block = refs.pop(0) if shared else None
    outs = take(n_out)
    everyone = refs.pop(0) if spreads else None
    targets = take(len(modes))
    blocks = refs.pop(0) if shared else None
    if sums:
        from_sibling, outgoing, incoming, pair_sems, sum_sems = take(5)
    if spreads:
        chip_sems, own_sems, forward_sems = take(3)
    rank, chip, core, sibling, ahead, behind = places()
    chips = len(ahead) + 1
    rows = ins[0].shape[0]
    step = rows // CHUNKS
    spans = [pl.ds(index * step, step) for index in range(CHUNKS)]
    met = [sibling] + [chip_peer(place, core) for place in ahead]
    if shared:
        met += [device for axis in ("lat", "a", "b") for _, device in peers_along(axis)[2]]
    else:
        met += rider_peers(modes)
    greet(met)
    started, riding = [], []

    def ride():
        if modes:
            riding.extend(start_riders(modes, sources, targets, *refs[:2]))

    if shared:
        finish_gather = gather_everyone(block, blocks, *refs[-2:], ride)
    if sums:
        pair = {}
        for order, place in enumerate(ahead + [chip]):
            for index, span in enumerate(spans):
                copy = remote(
                    part.at[2 * place + 1 - core, span],
                    from_sibling.at[order, span],
                    pair_sems,
                    order * CHUNKS + index,
                    sibling,
                )
                copy.start()
                pair[order, index] = copy
        crossing = {}
        for order, place in enumerate(ahead):
            for index, span in enumerate(spans):
                pair[order, index].wait_recv()
                outgoing[order, span] = (
                    part[2 * place + core, span].astype(F32)
                    + from_sibling[order, span].astype(F32)
                ).astype(B16)
                copy = remote(
                    outgoing.at[order, span],
                    incoming.at[order, span],
                    sum_sems,
                    order * CHUNKS + index,
                    chip_peer(place, core),
                )
                copy.start()
                crossing[order, index] = copy
    if not shared:
        ride()
    direct = {}
    for index, span in enumerate(spans):
        total = None
        if sums:
            pair[chips - 1, index].wait_recv()
            total = part[rank, span].astype(F32) + from_sibling[chips - 1, span].astype(F32)
            for order in range(chips - 1):
                crossing[order, index].wait_recv()
                total = total + incoming[order, span].astype(F32)
        low = body(index, span, total, ins, outs)
        if spreads:
            everyone[rank, span] = low
            mine = everyone.at[rank, span]
            for order, place in enumerate(ahead):
                copy = remote(
                    mine, mine, chip_sems, order * CHUNKS + index, chip_peer(place, core)
                )
                copy.start()
                direct[order, index] = copy
            copy = remote(mine, mine, own_sems, index, sibling)
            copy.start()
            started.append(copy)
    if shared:
        finish_gather()
    if spreads:
        for index, span in enumerate(spans):
            for order, place in enumerate(behind):
                direct[order, index].wait_recv()
                landed = everyone.at[2 * place + core, span]
                copy = remote(landed, landed, forward_sems, order * CHUNKS + index, sibling)
                copy.start()
                started.append(copy)
        for copy in direct.values():
            copy.wait_send()
        for copy in started:
            copy.wait()
    if sums:
        for copy in list(pair.values()) + list(crossing.values()):
            copy.wait_send()
    for copy in riding:
        copy.wait()


def comm_params(number):
    return pltpu.CompilerParams(
        collective_id=number, has_side_effects=True, vmem_limit_bytes=VMEM_LIMIT
    )


def token_call(name, body, part, ins, outs, spreads, riders=(), shared=None):
    ranks = lax.axis_size("tp")
    chips = ranks // 2
    rows, width = ins[0].shape
    sums = part is not None
    modes, key, cargo, cargo_shapes = split_riders(riders)
    shapes = [jax.ShapeDtypeStruct(shape, F32) for shape in outs]
    scratch = []
    if sums:
        scratch += [
            pltpu.VMEM((chips, rows, width), B16),
            pltpu.VMEM((chips - 1, rows, width), B16),
            pltpu.VMEM((chips - 1, rows, width), B16),
            pltpu.SemaphoreType.DMA((2, chips * CHUNKS)),
            pltpu.SemaphoreType.DMA((2, (chips - 1) * CHUNKS)),
        ]
    if spreads:
        shapes.append(jax.ShapeDtypeStruct((ranks, rows, width), B16))
        scratch += [
            pltpu.SemaphoreType.DMA((2, (chips - 1) * CHUNKS)),
            pltpu.SemaphoreType.DMA((2, CHUNKS)),
            pltpu.SemaphoreType.DMA((2, (chips - 1) * CHUNKS)),
        ]
    scratch += rider_scratch(modes)
    if shared is not None:
        key = key + shared.shape
        cargo = cargo + [shared]
        blocks = (lax.axis_size("row"), LATENTS * ranks) + shared.shape
        cargo_shapes = cargo_shapes + [jax.ShapeDtypeStruct(blocks, shared.dtype)]
        scratch += [
            pltpu.SemaphoreType.DMA((2, gather_copies())),
            pltpu.SemaphoreType.DMA((1,)),
        ]
    args = ([part.reshape(ranks, rows, width)] if sums else []) + list(ins)
    whole = pl.BlockSpec(memory_space=pltpu.VMEM)
    away = pl.BlockSpec(memory_space=pl.ANY)
    results = pl.pallas_call(
        functools.partial(
            token_kernel, sums, spreads, body, len(ins), len(outs), modes, shared is not None
        ),
        out_shape=shapes + cargo_shapes,
        in_specs=[whole] * len(args) + [away] * len(cargo),
        out_specs=[whole] * len(shapes) + [away] * len(cargo),
        scratch_shapes=scratch,
        name=name,
        compiler_params=comm_params(number_of(name, key)),
        cost_estimate=pl.CostEstimate(
            flops=20 * rows * width, bytes_accessed=12 * rows * width, transcendentals=0
        ),
    )(*args, *cargo)
    results = list(results)
    if spreads:
        place = len(outs)
        results[place] = results[place].reshape(ranks * rows, width)
    return results


def start_kernel(modes, *refs):
    refs = list(refs)
    take = lambda count: [refs.pop(0) for _ in range(count)]
    cond, mod = take(2)
    sources = take(len(modes))
    low_ref, out = take(2)
    targets = take(len(modes))
    got, terms, landed, cond_sems, term_sems, out_sems = take(6)
    row, lat, rank = here()
    rows, ranks = lax.axis_size("row"), lax.axis_size("tp")
    columns = LATENTS * ranks
    column = lat * ranks + rank
    others = row_peers()
    company = []
    for step in range(1, columns):
        place = (column + step) % columns
        company.append(device_at(row, place // ranks, place % ranks))
    greet([device for _, device in others] + company)
    riding = start_riders(modes, sources, targets, *refs) if modes else []
    copies = []
    got[row] = cond[row]
    for index, (other, device) in enumerate(others):
        copy = remote(cond.at[other], got.at[row], cond_sems, index, device)
        copy.start()
        copies.append(copy)
    for copy in copies:
        copy.wait()
    value = got[...]
    low = (value / (1.0 + jnp.exp(-value))).astype(B16)
    low_ref[...] = low.astype(F32)
    flat = low.reshape(rows * 8, low.shape[2])
    first = jnp.dot(flat, mod[0], preferred_element_type=F32)
    second = jnp.dot(flat, mod[1], preferred_element_type=F32)
    upper = lax.broadcasted_iota(jnp.int32, first.shape, 0) % 8 < LATENTS
    terms[...] = jnp.where(upper, first, second).reshape(terms.shape)
    copies = []
    landed[row] = terms[row]
    for index, (other, device) in enumerate(others):
        copy = remote(terms.at[other], landed.at[row], term_sems, index, device)
        copy.start()
        copies.append(copy)
    for copy in copies:
        copy.wait()
    out[column] = jnp.sum(landed[...], axis=0)
    copies = []
    for index, device in enumerate(company):
        copy = remote(out.at[column], out.at[column], out_sems, index, device)
        copy.start()
        copies.append(copy)
    for copy in copies:
        copy.wait()
    for copy in riding:
        copy.wait()


def start_call(cond, mod_w, riders):
    rows, ranks = lax.axis_size("row"), lax.axis_size("tp")
    layers, depth, local = mod_w.shape
    tall, wide = depth + -depth % 128, local + -local % 128
    blocks = jnp.transpose(cond.astype(F32).reshape(LATENTS, rows, depth), (1, 0, 2))
    blocks = jnp.concatenate([blocks] * layers, axis=1)
    blocks = jnp.pad(blocks, ((0, 0), (0, 8 - layers * LATENTS), (0, tall - depth)))
    mod = jnp.pad(mod_w, ((0, 0), (0, tall - depth), (0, wide - local)))
    modes, key, cargo, cargo_shapes = split_riders(riders)
    whole = pl.BlockSpec(memory_space=pltpu.VMEM)
    away = pl.BlockSpec(memory_space=pl.ANY)
    columns = LATENTS * ranks
    low, out, *rest = pl.pallas_call(
        functools.partial(start_kernel, modes),
        out_shape=[
            jax.ShapeDtypeStruct(blocks.shape, F32),
            jax.ShapeDtypeStruct((columns, 8, wide), F32),
        ]
        + cargo_shapes,
        in_specs=[whole] * 2 + [away] * len(cargo),
        out_specs=[whole] * 2 + [away] * len(cargo),
        scratch_shapes=[
            pltpu.VMEM(blocks.shape, F32),
            pltpu.VMEM((rows, 8, wide), F32),
            pltpu.VMEM((rows, 8, wide), F32),
            pltpu.SemaphoreType.DMA((2, rows - 1)),
            pltpu.SemaphoreType.DMA((2, rows - 1)),
            pltpu.SemaphoreType.DMA((2, columns - 1)),
        ]
        + rider_scratch(modes),
        name="shift",
        compiler_params=comm_params(number_of("shift", key)),
    )(blocks, mod, *cargo)
    cond_rows = low[:, :LATENTS, :depth].reshape(rows * LATENTS, depth).astype(B16)
    own = lax.dynamic_index_in_dim(
        out[:, : layers * LATENTS].reshape(columns, layers, LATENTS, wide),
        lax.axis_index("lat"),
        axis=2,
        keepdims=False,
    )
    shift = jnp.transpose(own[:, :, :local], (1, 0, 2)).reshape(layers, columns * local)
    return cond_rows, shift, rest


def end_kernel(modes, *refs):
    refs = list(refs)
    take = lambda count: [refs.pop(0) for _ in range(count)]
    (value,) = take(1)
    sources = take(len(modes))
    (out,) = take(1)
    targets = take(len(modes))
    parts, pair, part_sems, pair_sems, out_sems = take(5)
    row, lat, rank = here()
    ranks = lax.axis_size("tp")
    others = row_peers()
    company = [device_at(row, lat, (rank + step) % ranks) for step in range(1, ranks)]
    greet(company + [lat_peer()] + [device for _, device in others])
    riding = start_riders(modes, sources, targets, *refs) if modes else []
    copies = []
    for index, device in enumerate(company):
        copy = remote(value, parts.at[index], part_sems, index, device)
        copy.start()
        copies.append(copy)
    for copy in copies:
        copy.wait()
    pair[lat] = value[...] + jnp.sum(parts[...], axis=0)
    copy = remote(pair.at[lat], pair.at[lat], pair_sems, 0, lat_peer())
    copy.start()
    copy.wait()
    out[row] = pair[...]
    copies = []
    for index, (_, device) in enumerate(others):
        copy = remote(pair, out.at[row], out_sems, index, device)
        copy.start()
        copies.append(copy)
    for copy in copies:
        copy.wait()
    for copy in riding:
        copy.wait()


def end_call(value, riders):
    rows, ranks = lax.axis_size("row"), lax.axis_size("tp")
    modes, key, cargo, cargo_shapes = split_riders(riders)
    whole = pl.BlockSpec(memory_space=pltpu.VMEM)
    away = pl.BlockSpec(memory_space=pl.ANY)
    return pl.pallas_call(
        functools.partial(end_kernel, modes),
        out_shape=[jax.ShapeDtypeStruct((rows, LATENTS) + value.shape, F32)]
        + cargo_shapes,
        in_specs=[whole] + [away] * len(cargo),
        out_specs=[whole] + [away] * len(cargo),
        scratch_shapes=[
            pltpu.VMEM((ranks - 1,) + value.shape, F32),
            pltpu.VMEM((LATENTS,) + value.shape, F32),
            pltpu.SemaphoreType.DMA((2, ranks - 1)),
            pltpu.SemaphoreType.DMA((2, 1)),
            pltpu.SemaphoreType.DMA((2, rows - 1)),
        ]
        + rider_scratch(modes),
        name="gains",
        compiler_params=comm_params(number_of("gains", key)),
    )(value, *cargo)


def first_body(index, span, total, ins, outs):
    resid, gain, shift = ins
    return (norm_stats(resid[span])[0] * gain[...] + shift[...]).astype(B16)


def middle_body(index, span, total, ins, outs):
    resid, gain = ins
    value = resid[span] + total
    outs[0][span] = value
    return (norm_stats(value)[0] * gain[...]).astype(B16)


def last_body(index, span, total, ins, outs):
    outs[0][span] = ins[0][span] + total
    return None


def spread_body(index, span, total, ins, outs):
    return ins[0][span].astype(B16)


def add_rows(out, index, value):
    value = jnp.sum(value, axis=0, keepdims=True)
    if index == 0:
        out[...] = value
    else:
        out[...] += value


def back_body(index, span, total, ins, outs):
    grad, resid, gain = ins
    normed, rstd = norm_stats(resid[span])
    value = grad[span] + norm_back(normed, rstd, total * gain[...])
    outs[0][span] = value
    add_rows(outs[1], index, total * normed)
    return value.astype(B16)


def back_last_body(index, span, total, ins, outs):
    back_body(index, span, total, ins, outs)
    add_rows(outs[2], index, total)
    return None


def first_tokens(resid, gain, shift, riders=()):
    return token_call("first", first_body, None, [resid, gain, shift], [], True, riders)


def middle_tokens(part, resid, gain, riders=()):
    ins = [resid, gain]
    return token_call("middle", middle_body, part, ins, [resid.shape], True, riders)


def last_tokens(part, resid, riders=()):
    return token_call("last", last_body, part, [resid], [resid.shape], False, riders)


def spread_tokens(grad, riders=(), shared=None):
    return token_call("spread", spread_body, None, [grad], [], True, riders, shared)


def back_tokens(part, grad, resid, gain, riders=()):
    shapes = [grad.shape, gain.shape]
    ins = [grad, resid, gain]
    return token_call("back", back_body, part, ins, shapes, True, riders)


def back_last_tokens(part, grad, resid, gain, riders=()):
    shapes = [grad.shape, gain.shape, gain.shape]
    ins = [grad, resid, gain]
    return token_call("back_last", back_last_body, part, ins, shapes, False, riders)


def dot(left, right, left_dim, right_dim):
    return lax.dot_general(
        left, right, (((left_dim,), (right_dim,)), ((), ())), preferred_element_type=F32
    )


def skip_kernel(resid_ref, skip_ref, gain_ref, weight_ref, low_ref, out_ref):
    tokens, width = resid_ref.shape
    parts, _, depth = weight_ref.shape
    step = tokens // CHUNKS
    for index in range(CHUNKS):
        span = pl.ds(index * step, step)
        joined = jnp.concatenate([resid_ref[span], skip_ref[span].astype(F32)], axis=1)
        low_ref[span] = (norm_stats(joined)[0] * gain_ref[...]).astype(B16)
    for part in range(parts):
        low = low_ref[:, part * depth : (part + 1) * depth]
        term = dot(low, weight_ref[part], 1, 1)
        if part == 0:
            out_ref[...] = term
        else:
            out_ref[...] += term


def skip_back_kernel(
    grad_ref, low_ref, resid_ref, skip_ref, gain_ref, weight_ref, weight_out, resid_out, skip_out, gain_out, norm_grad
):
    tokens, width = resid_ref.shape
    parts, _, depth = weight_ref.shape
    step = tokens // CHUNKS
    grad_low = grad_ref[...].astype(B16)
    grad_t = grad_low.T
    for part in range(parts):
        columns = slice(part * depth, (part + 1) * depth)
        weight_out[part] = dot(grad_t, low_ref[:, columns], 1, 0).astype(B16)
        norm_grad[:, columns] = dot(grad_low, weight_ref[part], 1, 0)
    for index in range(CHUNKS):
        span = pl.ds(index * step, step)
        joined = jnp.concatenate([resid_ref[span], skip_ref[span].astype(F32)], axis=1)
        normed, rstd = norm_stats(joined)
        grad = norm_grad[span]
        add_rows(gain_out, index, grad * normed)
        value = norm_back(normed, rstd, grad * gain_ref[...])
        resid_out[span] = value[:, :width]
        skip_out[span] = value[:, width:]


def local_call(name, body, args, shapes, scratch=()):
    return pl.pallas_call(
        body,
        out_shape=shapes,
        in_specs=[pl.BlockSpec(memory_space=pltpu.VMEM)] * len(args),
        out_specs=[pl.BlockSpec(memory_space=pltpu.VMEM)] * len(shapes),
        scratch_shapes=list(scratch),
        name=name,
        compiler_params=pltpu.CompilerParams(vmem_limit_bytes=VMEM_LIMIT),
    )(*args)


def skip_forward(resid, skip, gain, weight):
    tokens, width = resid.shape
    shapes = [
        jax.ShapeDtypeStruct((tokens, 2 * width), B16),
        jax.ShapeDtypeStruct((tokens, width), F32),
    ]
    return local_call("skip", skip_kernel, [resid, skip, gain, weight], shapes)


def skip_backward(grad, low, resid, skip, gain, weight):
    tokens, width = resid.shape
    shapes = [
        jax.ShapeDtypeStruct(weight.shape, B16),
        jax.ShapeDtypeStruct(resid.shape, F32),
        jax.ShapeDtypeStruct(resid.shape, F32),
        jax.ShapeDtypeStruct(gain.shape, F32),
    ]
    scratch = [pltpu.VMEM((tokens, 2 * width), F32)]
    args = [grad, low, resid, skip, gain, weight]
    return local_call("skip_back", skip_back_kernel, args, shapes, scratch)


def on_device(
    latent,
    skips,
    cond,
    text,
    skip_gain,
    attn_gain,
    ffn_gain,
    skip_w,
    mod_w,
    qkv_w,
    out_w,
    cq_w,
    ckv_w,
    cout_w,
    fc1_w,
    fc2_w,
    cotangent,
):
    rows = lax.axis_size("row")
    ranks = lax.axis_size("tp")
    row = lax.axis_index("row")
    lat = lax.axis_index("lat")
    rank = lax.axis_index("tp")
    width = latent.shape[1]
    depth = qkv_w.shape[2]
    local = qkv_w.shape[3]
    hidden_local = fc1_w.shape[2]
    layers = skip_w.shape[0]
    text_depth = ckv_w.shape[2]
    text_count = text.shape[1]
    tables = rotary_tables()
    everyone = ("row", "lat", "tp")


    def gather_both(pack, other, sizes):
        low, high = jnp.where(lat == 0, pack, other), jnp.where(lat == 0, other, pack)
        pieces, start = [], 0
        for size in sizes:
            pieces += [low[:, start : start + size], high[:, start : start + size]]
            start += size
        return lax.all_gather(jnp.concatenate(pieces, axis=1), "row", axis=0, tiled=True)

    attn_pack, cross_pack, text_pack, up_pack, down_pack = [], [], [], [], []
    attn_full, cross_full, text_full_w = [], [], []
    for layer in range(layers):
        attn_pack.append(
            jnp.concatenate(
                [qkv_w[layer, 0], qkv_w[layer, 1], qkv_w[layer, 2], out_w[layer].T], axis=1
            )
        )
        cross_pack.append(jnp.concatenate([cq_w[layer], cout_w[layer].T], axis=1))
        text_pack.append(jnp.concatenate([ckv_w[layer, 0], ckv_w[layer, 1]], axis=1))
        up_pack.append(fc1_w[layer])
        down_pack.append(fc2_w[layer].T)

    cond_rows, shift, others = start_call(
        cond, mod_w, [swap(attn_pack[0])]
    )
    attn_full.append(gather_both(attn_pack[0], others[0], [local] * 4))


    def stack(array):
        return [("gather", "lat", 0, None, array)]

    def gather_one(array):
        return [("gather", "b", 0, 0, array), ("gather", "a", 0, 1, array)]

    def gather_two(halves):
        return [("gather", "a", 0, None, halves[0]), ("gather", "b", 1, None, halves[1])]

    def whole(halves):
        return [half.reshape(width, -1) for half in halves]

    grad = cotangent.astype(F32)
    grad_all, cross_other, text_other, up_stack, skip_blocks = spread_tokens(
        grad, [swap(cross_pack[0]), swap(text_pack[0])] + stack(up_pack[0]), skip_w[0].T
    )
    skip_full = [skip_blocks.reshape(rows, width, -1)]
    down_stack = down_half = None

    def own_text(text):
        text_parts = lax.all_gather(text, ("lat", "tp"), axis=0)
        text_own = lax.dynamic_index_in_dim(text_parts, lat, axis=1, keepdims=False)
        text_own = jnp.transpose(text_own, (1, 0, 2)).reshape(text_count, -1)
        return jnp.pad(text_own, ((0, -text_count % 128), (0, 0)))

    wide = LATENTS * local

    def thirds(stack, count):
        return [stack[index * wide : (index + 1) * wide] for index in range(count)]

    resid = latent.astype(F32)
    saved = []
    for layer in range(layers):
        keep = {}
        keep["skip_in"] = resid
        keep["skip_low"], resid_one = skip_forward(
            resid, skips[layer], skip_gain[layer : layer + 1], skip_full[layer]
        )
        keep["first"] = resid_one
        following = layer + 1 < layers
        if layer == 0:
            riders = gather_one(up_stack) + stack(down_pack[0])
        else:
            riders = [swap(cross_pack[layer]), swap(text_pack[layer])]
        first_all, *others = first_tokens(
            resid_one, attn_gain[layer, 0:1], shift[layer : layer + 1], riders
        )
        if layer == 0:
            up_half, down_stack = others[:2], others[2]
            text, cross_other, text_other, first_all = lax.optimization_barrier(
                (text, cross_other, text_other, first_all)
            )
            text_own = own_text(text)
        else:
            cross_other, text_other = others
        cross_full.append(gather_both(cross_pack[layer], cross_other, [local] * 2))
        text_full_w.append(gather_both(text_pack[layer], text_other, [local] * 2))
        keep["first_all"] = first_all
        weight = attn_full[layer]
        query, keys, values = thirds(dot(weight[:, : 3 * wide], first_all, 0, 1), 3)
        self_low, self_lse = attention(query, keys, values, tables, SEQ, True)
        keep["self"] = (query, keys, values, self_lse, self_low)
        out_t = weight[:, 3 * wide :]
        keep["out_t"] = out_t
        if following:
            skip_next, self_low = lax.optimization_barrier((skip_w[layer + 1].T, self_low))
            skip_full.append(
                lax.all_gather(skip_next, everyone, axis=0).reshape(rows, width, -1)
            )
        riders = gather_two(up_half) + gather_one(down_stack)
        if following:
            riders.append(swap(attn_pack[layer + 1]))
        resid_two, third_all, *others = middle_tokens(
            dot(self_low, out_t, 0, 1).astype(B16), resid_one, attn_gain[layer, 1:2], riders
        )
        up_w, down_half = whole(others[:2]), others[2:4]
        if following:
            attn_full.append(gather_both(attn_pack[layer + 1], others[4], [local] * 4))
        keep["third"] = resid_two
        keep["third_all"] = third_all
        weight = cross_full[layer]
        query_w, cout_t = weight[:, :wide], weight[:, wide:]
        keep["cross_w"] = (query_w, cout_t)
        cross_query = dot(query_w, third_all, 0, 1)
        text_keys, text_values = thirds(dot(text_full_w[layer], text_own, 0, 1), 2)
        cross_low, cross_lse = attention(
            cross_query, text_keys, text_values, tables, text_count, False
        )
        keep["cross"] = (cross_query, text_keys, text_values, cross_lse, cross_low)
        riders = gather_two(down_half) + (stack(up_pack[layer + 1]) if following else [])
        resid_three, second_all, *others = middle_tokens(
            dot(cross_low, cout_t, 0, 1).astype(B16),
            resid_two,
            ffn_gain[layer : layer + 1],
            riders,
        )
        down_w = whole(others[:2])
        if following:
            up_stack = others[2]
        keep["second"] = resid_three
        keep["second_all"] = second_all
        hidden = [dot(second_all, up_w[part], 1, 0) for part in range(LATENTS)]
        act_low = [gelu_tanh(part).astype(B16) for part in hidden]
        keep["hidden"] = hidden
        keep["act"] = act_low
        keep["ffn_w"] = (up_w, down_w)
        term = sum(dot(act_low[part], down_w[part], 1, 1) for part in range(LATENTS))
        riders = gather_one(up_stack) + stack(down_pack[layer + 1]) if following else []
        term = term.astype(B16)
        if following:
            resid, *others = last_tokens(term, resid_three, riders)
        if following:
            up_half, down_stack = others[:2], others[2]
        saved.append(keep)

    final_term, final_resid = term, resid_three

    def sum_over_rows(parts, counts):
        pieces = []
        for part, count in zip(parts, counts):
            pieces += [
                part[:, index * local : (index + 1) * local].astype(B16)
                for index in range(LATENTS * count)
            ]
        packed = jnp.concatenate(pieces[0::2] + pieces[1::2], axis=1)
        summed = lax.psum_scatter(packed, "row", scatter_dimension=0, tiled=True)
        half = summed.shape[1] // 2
        low, high = summed[:, :half], summed[:, half:]
        return jnp.where(lat == 0, low, high), jnp.where(lat == 0, high, low)

    def finish(mine, other):
        total = mine.astype(F32) + other.astype(F32)
        return [
            total[:, start : start + local] for start in range(0, total.shape[1], local)
        ]

    fast = rows // 2
    slow_at, fast_at = row // fast, row % fast

    def by_rows(value):
        return value.astype(B16).reshape(2, fast, -1, value.shape[1])

    def pick(value, index, axis):
        return lax.dynamic_index_in_dim(value, index, axis=axis, keepdims=False).astype(F32)

    def scatter_one(halves):
        return [("scatter", "a", 0, None, halves[0]), ("scatter", "b", 1, None, halves[1])]

    def added_one(halves, arrived):
        low = pick(halves[0], slow_at, 0) + jnp.sum(arrived[0].astype(F32), axis=0)
        high = pick(halves[1], fast_at, 1) + jnp.sum(arrived[1].astype(F32), axis=0)
        return [low.astype(B16), high.astype(B16)]

    def scatter_two(halves):
        return [("scatter", "b", 0, None, halves[0]), ("scatter", "a", 0, None, halves[1])]

    def added_two(halves, arrived):
        low = pick(halves[0], fast_at, 0) + jnp.sum(arrived[0].astype(F32), axis=0)
        high = pick(halves[1], slow_at, 0) + jnp.sum(arrived[1].astype(F32), axis=0)
        mine = jnp.where(lat == 0, low, high)
        return mine, jnp.where(lat == 0, high, low).astype(B16)

    text_grad = jnp.zeros(text_own.shape, F32)
    weight_store = [None] * layers
    gain_store = [None] * layers
    skip_store = [None] * layers
    shift_store = [None] * layers
    waiting = None
    for layer in range(layers - 1, -1, -1):
        keep = saved[layer]
        up_w, down_w = keep["ffn_w"]
        if waiting is not None:
            grad_all, other = spread_tokens(grad, [swap(waiting["down"][1])])
            waiting["store"]["down"] = waiting["down"][0] + other.astype(F32)
        ups, downs = [], []
        term = None
        for part in range(LATENTS):
            act_grad = dot(grad_all, down_w[part], 1, 0)
            hidden_grad = (act_grad * gelu_grad(keep["hidden"][part])).astype(B16)
            downs.append(by_rows(dot(grad_all, keep["act"][part], 0, 0)))
            ups.append(by_rows(dot(keep["second_all"], hidden_grad, 0, 0)))
            piece = dot(hidden_grad, up_w[part], 1, 1)
            term = piece if term is None else term + piece
        riders = scatter_one(ups)
        names = ("attn", "cross", "text")
        if waiting is not None:
            riders += [swap(waiting[name][1]) for name in names]
        grad_three, gain_ffn, grad_all, *others = back_tokens(
            term.astype(B16), grad, keep["second"], ffn_gain[layer : layer + 1], riders
        )
        ups = added_one(ups, others[:2])
        if waiting is not None:
            for name, other in zip(names, others[2:]):
                waiting["store"][name] = finish(waiting[name][0], other)

        query_w, cout_t = keep["cross_w"]
        cross_query, text_keys, text_values, cross_lse, cross_low = keep["cross"]
        out_grad = dot(cout_t, grad_all, 0, 1).astype(B16)
        cout_grad = dot(grad_all, cross_low, 0, 1)
        query_grad, keys_grad, values_grad = attention_back(
            cross_query, text_keys, text_values, cross_lse, out_grad, tables, text_count, False
        )
        cq_grad = dot(keep["third_all"], query_grad, 0, 1)
        cross_sum = sum_over_rows([cq_grad, cout_grad], [1, 1])
        both = jnp.concatenate([keys_grad, values_grad], axis=0)
        text_sum = sum_over_rows([dot(text_own, both, 0, 1)], [2])
        text_grad = text_grad + dot(both, text_full_w[layer], 0, 1)
        riders = scatter_two(ups) + scatter_one(downs)
        if waiting is not None:
            query_grad, waiting["store"]["skip"] = lax.optimization_barrier(
                (query_grad, waiting["store"]["skip"])
            )
        grad_two, gain_cross, grad_all, *others = back_tokens(
            dot(query_grad, query_w, 0, 1).astype(B16),
            grad_three,
            keep["third"],
            attn_gain[layer, 1:2],
            riders,
        )
        up_mine, up_theirs = added_two(ups, others[:2])
        downs = added_one(downs, others[2:])

        weight = attn_full[layer]
        query, keys, values, self_lse, self_low = keep["self"]
        out_grad = dot(keep["out_t"], grad_all, 0, 1).astype(B16)
        wout_grad = dot(grad_all, self_low, 0, 1)
        three = attention_back(query, keys, values, self_lse, out_grad, tables, SEQ, True)
        both = jnp.concatenate(three, axis=0)
        term = dot(both, weight[:, : 3 * wide], 0, 1)
        qkv_grad = dot(keep["first_all"], both, 0, 1)
        grad_one, gain_self, shift_own, *others = back_last_tokens(
            term.astype(B16),
            grad_two,
            keep["first"],
            attn_gain[layer, 0:1],
            scatter_two(downs) + [swap(up_theirs)],
        )
        down_sum = added_two(downs, others[:2])
        up_grad = up_mine + others[2].astype(F32)
        attn_sum = sum_over_rows([qkv_grad, wout_grad], [3, 1])

        packed, grad, skip_store[layer], gain_skip = skip_backward(
            grad_one,
            keep["skip_low"],
            keep["skip_in"],
            skips[layer],
            skip_gain[layer : layer + 1],
            skip_full[layer],
        )
        packed = packed.reshape(rows * LATENTS * ranks, local, -1)
        skip_sum = lax.psum_scatter(packed, everyone, scatter_dimension=0, tiled=False)
        gain_store[layer] = (gain_skip[0], jnp.concatenate([gain_self, gain_cross]), gain_ffn[0])
        store = dict(skip=skip_sum, up=up_grad)
        waiting = dict(attn=attn_sum, cross=cross_sum, text=text_sum, down=down_sum, store=store)
        weight_store[layer] = store
        shift_store[layer] = shift_own

    sizes = [gain_store[0][slot].size for slot in range(3)] + [width]
    flat = jnp.concatenate(
        [
            gain_store[layer][slot].reshape(-1)
            for slot in range(3)
            for layer in range(layers)
        ]
        + [shift_store[layer].reshape(-1) for layer in range(layers)]
    )
    flat = jnp.pad(flat, (0, -flat.size % 1024)).reshape(-1, 128)
    flat_all, down_other, *others = end_call(
        flat, [swap(waiting[name][1]) for name in ("down",) + names]
    )
    waiting["store"]["down"] = waiting["down"][0] + down_other.astype(F32)
    for name, other in zip(names, others):
        waiting["store"][name] = finish(waiting[name][0], other)
    final_term, text_grad, flat_all = lax.optimization_barrier((final_term, text_grad, flat_all))
    mixed = last_tokens(final_term, final_resid)[0]
    flat_all = flat_all.reshape(rows * LATENTS, -1)
    totals = jnp.sum(flat_all, axis=0)
    gains, start = [], 0
    for slot in range(3):
        size = layers * sizes[slot]
        gains.append(
            totals[start : start + size].reshape((layers,) + gain_store[0][slot].shape)
        )
        start += size
    shift_grad = flat_all[:, start : start + layers * width].reshape(-1, layers, width)
    column = (lat * ranks + rank) * local
    shift_cols = lax.dynamic_slice_in_dim(shift_grad, column, local, axis=2).astype(B16)

    weight_store = [
        (
            store["skip"].astype(F32).T,
            dot(cond_rows, shift_cols[:, layer], 0, 0),
            jnp.stack(store["attn"][:3]),
            store["attn"][3].T,
            store["cross"][0],
            jnp.stack(store["text"]),
            store["cross"][1].T,
            store["up"],
            store["down"].T,
        )
        for layer, store in enumerate(weight_store)
    ]
    weight_outs = tuple(
        jnp.stack([weight_store[layer][slot] for layer in range(layers)]) for slot in range(9)
    )
    blocks = text_grad[:text_count].astype(B16).reshape(text_count, LATENTS * ranks, -1)
    blocks = jnp.transpose(blocks, (1, 0, 2))
    blocks = lax.all_to_all(blocks, ("lat", "tp"), split_axis=0, concat_axis=0, tiled=True)
    text_out = jnp.sum(
        blocks.astype(F32).reshape((LATENTS, ranks) + blocks.shape[1:]), axis=1
    )
    return (mixed, grad, jnp.stack(skip_store), text_out) + tuple(gains) + weight_outs


def solution(mesh):
    NUMBERS.clear()
    rows, columns = mesh.shape["row"], mesh.shape["col"]
    grid = Mesh(
        mesh.devices.reshape(rows, LATENTS, columns // LATENTS), ("row", "lat", "tp")
    )
    col = ("lat", "tp")
    tokens = ("row", "lat", "tp")
    return jax.shard_map(
        on_device,
        mesh=grid,
        in_specs=(
            P(tokens, None),
            P(None, tokens, None),
            P("row", None),
            P("row", None, col),
            P(),
            P(),
            P(),
            P(None, "row", col),
            P(None, "row", col),
            P(None, None, "row", col),
            P(None, col, "row"),
            P(None, "row", col),
            P(None, None, "row", col),
            P(None, col, "row"),
            P(None, "row", col),
            P(None, col, "row"),
            P(tokens, None),
        ),
        out_specs=(
            P(tokens, None),
            P(tokens, None),
            P(None, tokens, None),
            P("row", None, col),
            P(),
            P(),
            P(),
            P(None, "row", col),
            P(None, "row", col),
            P(None, None, "row", col),
            P(None, col, "row"),
            P(None, "row", col),
            P(None, None, "row", col),
            P(None, col, "row"),
            P(None, "row", col),
            P(None, col, "row"),
        ),
        check_vma=False,
    )
```

time: 3110 us -> 1540 us (0.50)
  waiting for transfers between devices: 1840 us -> 0.41 us
  Pallas kernels: 0 us -> 1070 us
  local copies, waits for them, and re-layouts: 428 us -> 149 us
  blocking collectives: 203 us -> 0 us
  matrix products: 385 us -> 216 us
  other arithmetic: 212 us -> 72.1 us
    pallas_call x0 -> x30, Pallas kernels: none -> 1070 us  [the longest x16 809 us: token_call(): pl.pallas_call(functools.partial(token_kernel, sums, spreads, body, len(i...]
    all_gather x23 -> x8, waiting for transfers between devices: 1040 us -> 0.07 us  [the longest x6 0.07 us: gather_both(): lax.all_gather(jnp.concatenate(pieces, axis=1), 'row', axis=0, tiled=True)]
    reduce_scatter x20 -> x6, waiting for transfers between devices: 546 us -> 0.07 us  [sum_over_rows(): summed = lax.psum_scatter(packed, 'row', scatter_dimension=0, tiled=True)]
    reduce_scatter x2, waiting for transfers between devices: 245 us -> 0.01 us  [on_device(): lax.psum_scatter(packed, everyone, scatter_dimension=0, tiled=False)]
    dot_general x31 -> x0, matrix products: 173 us -> none  [the longest x4 37.6 us: attention_back(): jnp.einsum('heq,hek->hqk', grad_low, values_low, preferred_element_type=F32)]
    all_gather x4 -> x0, blocking collectives: 160 us -> none  [the longest x2 106 us: on_device(): lax.all_gather(shift_own, everyone, axis=0)]
    rev x12 -> x0, local copies, waits for them, and re-layouts: 111 us -> none  [swapped(): return pairs[:, :, ::-1].reshape(value.shape)]
    reshape x30 -> x11, local copies, waits for them, and re-layouts: 91.5 us -> 4.92 us  [the longest x3 1.85 us: on_device(): totals[start:start + size].reshape((layers,) + gain_store[0][slot].shape)]
  transfers between devices with their start and end apart: 46 -> 17, of which waited for: 39 -> 0; matrix products, arithmetic and copies ran while one was open for 16% -> 21% of each run, Pallas kernels for 0% -> 62%
where the time goes in v2:
time: 1540 us; the launch traced here: 1530 us
  Pallas kernels  1070 us (69%)
  matrix products  216 us (14%)
  local copies, waits for them, and re-layouts  149 us (10%)
  other arithmetic  72.1 us (5%)
  between operations  17.9 us (1%)
    pallas_call x16, Pallas kernels, token_call(): pl.pallas_call(functools.partial(token_kernel, sums, spreads, body, len(i...  809 us
    dot_general x56, matrix products, dot(): lax.dot_general(left, right, (((left_dim,), (right_dim,)), ((), ())), pre...  216 us
    pallas_call x1, Pallas kernels, end_call(): pl.pallas_call(functools.partial(end_kernel, modes), out_shape=[jax.Shape...  111 us
    unnamed x585, local copies, waits for them, and re-layouts  79.1 us
    pallas_call x4, Pallas kernels, attention_back(): pl.pallas_call(functools.partial(attention_back_kernel, count, turn), gri...  48.9 us
    pallas_call x4, Pallas kernels, local_call(): pl.pallas_call(body, out_shape=shapes, in_specs=[pl.BlockSpec(memory_spac...  40.8 us
    pallas_call x1, Pallas kernels, start_call(): pl.pallas_call(functools.partial(start_kernel, modes), out_shape=[jax.Sha...  31.6 us
  transfers between devices with their start and end apart: 17, of which 0 were waited for; matrix products, arithmetic and copies ran while one was open for 21% of the time, Pallas kernels for 62%

profile of v2, /device:TPU:0, one launch (start us, length us, event | category | flops | bytes accessed | tf_op | source)
XLA Modules:
  0.0 1534.1 jit_solution(2183363449594858776)
XLA Ops:
  13.8 31.6 %shift.1 = (f32[4,8,384]{2,1,0:T(8,128)S(1)}, f32[8,8,256]{2,1,0:T(8,128)S(1)}, bf16[352,704]{1,0:T(8,128)(2,1)S(1)}) custom-call(f32[4,8,384]{2,1,0:T(8,128)S(1)} %fusion.77.refs_0_, bf16[2,384,256]{2,1,0:T(8,128)(2,1)S(1)} %pad.20.refs_1_, bf16[352,704]{1,0:T(8,128)(2,1)S(1)} %pad_maximum_fusion.12.refs_2_), custom_call_target="tpu_custom_call" | custom-call | tf_op jit(solution)/shard_map/shift/pallas_call | solution.py:699
  59.2 94.4 %spread.2 = (bf16[4,256,1408]{2,1,0:T(8,128)(2,1)}, bf16[352,352]{1,0:T(8,128)(2,1)S(1)}, bf16[256,352]{1,0:T(8,128)(2,1)S(1)}, bf16[2,352,768]{2,1,0:T(8,128)(2,1)S(1)}, bf16[4,8,176,704]{3,2,1,0:T(8,128)(2,1)}) custom-call(f32[256,1408]{1,0:T(8,128)S(1)} %convert_element_type.493.refs_0_.refs_1_, bf16[352,352]{1,0:T(8,128)(2,1)S(1)} %pad_maximum_fusion.20.refs_1_, ...), custom_call_target="tpu_custom_call" | custom-call | flops 7208960 | bytes 4325376 | tf_op jit(solution)/shard_map/spread/pallas_call | solution.py:611
  154.7 7.0 skip.2
  164.1 44.2 %first.2 = (bf16[4,256,1408]{2,1,0:T(8,128)(2,1)}, bf16[2,352,768]{2,1,0:T(8,128)(2,1)S(1)}, bf16[2,352,768]{2,1,0:T(8,128)(2,1)S(1)}, bf16[2,352,768]{2,1,0:T(8,128)(2,1)S(1)}) custom-call(f32[256,1408]{1,0:T(8,128)} %copy-done, f32[1,1408]{1,0:T(1,128)S(1)} %get-tuple-element.486.refs_1_.refs_3_, f32[1,1408]{1,0:T(1,128)S(1)} %slice.535.refs_2_, ...), custom_call_target="tpu_custom_call" | custom-call | flops 7208960 | bytes 4325376 | tf_op jit(solution)/shard_map/first/pallas_call | solution.py:611
  216.6 7.0 fusion.36
  224.2 9.8 shard_map.288
  242.9 5.2 convolution_convert_fusion.9
  248.2 59.8 %middle.4 = (f32[256,1408]{1,0:T(8,128)}, bf16[4,256,1408]{2,1,0:T(8,128)(2,1)}, bf16[2,2,352,768]{3,2,1,0:T(8,128)(2,1)}, bf16[2,2,352,768]{3,2,1,0:T(8,128)(2,...) custom-call(bf16[4,256,1408]{2,1,0:T(8,128)(2,1)} %bitcast.416, ...), custom_call_target="tpu_custom_call" | custom-call | flops 7208960 | bytes 4325376 | tf_op jit(solution)/shard_map/middle/pallas_call | solution.py:611
  322.5 3.9 fusion.58.query_ref
  326.5 5.4 shard_map.289
  336.1 78.2 %middle.5 = (f32[256,1408]{1,0:T(8,128)S(1)}, bf16[4,256,1408]{2,1,0:T(8,128)(2,1)}, bf16[2,2,352,768]{3,2,1,0:T(8,128)(2,1)}, bf16[2,2,352,768]{3,2,1,0:T(8,128)(2,1)}, bf16[2,352,768]{2,1,0:T(8,128)(2,1)S(1)}) custom-call(bf16[4,256,1408]{2,1,0:T(8,128)(2,1)} %bitcast.409, f32[256,1408]{1,0:T(8,128)} %get-tuple-element.165.refs_1_.refs_2_, ...), custom_call_target="tpu_custom_call" | custom-call | flops 7208960 | bytes 4325376 | tf_op jit(solution)/shard_map/middle/pallas_call | solution.py:611
  414.4 5.0 fusion.133
  425.1 4.2 add_convert_fusion.3
  429.3 35.3 %last.2 = (f32[256,1408]{1,0:T(8,128)}, bf16[2,352,768]{2,1,0:T(8,128)(2,1)S(1)}, bf16[2,352,768]{2,1,0:T(8,128)(2,1)S(1)}, bf16[2,352,768]{2,1,0:T(8,128)(2,1)S(1)}) custom-call(bf16[4,256,1408]{2,1,0:T(8,128)(2,1)} %bitcast.413, f32[256,1408]{1,0:T(8,128)} %copy-done.19, bf16[2,352,768]{2,1,0:T(8,128)(2,1)S(1)} %get-tuple-element.174.refs_2_.refs_3_, ...), custom_call_target="tpu_custom_call" | custom-call | flops 7208960 | bytes 4325376 | tf_op jit(solution)/shard_map/last/pallas_call | solution.py:611
  470.1 6.8 skip.3
  478.0 30.4 %first.3 = (bf16[4,256,1408]{2,1,0:T(8,128)(2,1)S(1)}, bf16[352,352]{1,0:T(8,128)(2,1)S(1)}, bf16[256,352]{1,0:T(8,128)(2,1)S(1)}) custom-call(f32[256,1408]{1,0:T(8,128)S(1)} %get-tuple-element.177.refs_0_.refs_1_.refs_2_, f32[1,1408]{1,0:T(1,128)S(1)} %get-tuple-element.487.refs_1_.refs_3_, f32[1,1408]{1,0:T(1,128)S(1)} %copy-done.138, ...), custom_call_target="tpu_custom_call" | custom-call | flops 7208960 | bytes 4325376 | tf_op jit(solution)/shard_map/first/pallas_call | solution.py:611
  514.9 6.8 fusion.33
  522.7 10.2 shard_map.290
  532.9 5.0 convolution_convert_fusion.7
  538.0 62.2 %middle.6 = (f32[256,1408]{1,0:T(8,128)}, bf16[4,256,1408]{2,1,0:T(8,128)(2,1)}, bf16[2,2,352,768]{3,2,1,0:T(8,128)(2,1)}, bf16[2,2,352,768]{3,2,1,0:T(8,128)(2,...) custom-call(bf16[4,256,1408]{2,1,0:T(8,128)(2,1)} %bitcast.412, f32[256,1408]{1,0:T(8,128)} %copy-done.2, ...), custom_call_target="tpu_custom_call" | custom-call | flops 7208960 | bytes 4325376 | tf_op jit(solution)/shard_map/middle/pallas_call | solution.py:611
  609.2 5.4 shard_map.291
  618.2 39.9 %middle.7 = (f32[256,1408]{1,0:T(8,128)S(1)}, bf16[4,256,1408]{2,1,0:T(8,128)(2,1)}, bf16[2,2,352,768]{3,2,1,0:T(8,128)(2,1)}, bf16[2,2,352,768]{3,2,1,0:T(8,128)(2,1)}) custom-call(bf16[4,256,1408]{2,1,0:T(8,128)(2,1)} %bitcast.414, f32[256,1408]{1,0:T(8,128)S(1)} %copy-done.20, f32[1,1408]{1,0:T(1,128)S(1)} %copy-done.137, ...), custom_call_target="tpu_custom_call" | custom-call | flops 7208960 | bytes 4325376 | tf_op jit(solution)/shard_map/middle/pallas_call | solution.py:611
  658.1 5.6 fusion.135
  663.8 4.1 fusion.13
  685.0 4.3 add_convert_fusion.1
  689.3 40.7 %back.4 = (f32[256,1408]{1,0:T(8,128)S(1)}, f32[1,1408]{1,0:T(1,128)S(1)}, bf16[4,256,1408]{2,1,0:T(8,128)(2,1)}, bf16[1,2,352,768]{3,2,1,0:T(8,128)(2,1)S(1)}, bf16[1,2,352,768]{3,2,1,0:T(8,128)(2,1)S(1)}) custom-call(bf16[4,256,1408]{2,1,0:T(8,128)(2,1)} %bitcast.419, f32[256,1408]{1,0:T(8,128)S(1)} %convert_element_type.493.refs_0_.refs_1_, ...), custom_call_target="tpu_custom_call" | custom-call | flops 7208960 | bytes 4325376 | tf_op jit(solution)/shard_map/back/pallas_call | solution.py:611
  730.1 5.8 convolution_convert_fusion.21
  737.9 7.4 shard_map.292
  759.3 6.9 convolution_convert_fusion.15
  766.3 4.0 convolution_convert_fusion.14
  776.3 62.7 %back.5 = (f32[256,1408]{1,0:T(8,128)}, f32[1,1408]{1,0:T(1,128)S(1)}, bf16[4,256,1408]{2,1,0:T(8,128)(2,1)}, bf16[1,352,768]{2,1,0:T(8,128)(2,1)S(1)}, bf16[1,3...) custom-call(bf16[4,256,1408]{2,1,0:T(8,128)(2,1)} %bitcast.417, ...), custom_call_target="tpu_custom_call" | custom-call | flops 7208960 | bytes 4325376 | tf_op jit(solution)/shard_map/back/pallas_call | solution.py:611
  842.6 4.2 convolution_convert_fusion.28.grad_ref
  846.8 16.9 %shard_map.293 = (bf16[352,1024]{1,0:T(8,128)(2,1)S(1)}, bf16[352,1024]{1,0:T(8,128)(2,1)S(1)}, bf16[352,1024]{1,0:T(8,128)(2,1)S(1)}) custom-call(f32[352,1024]{1,0:T(8,128)S(1)} %copy-done.80, f32[352,1024]{1,0:T(8,128)} %copy-done.78, f32[352,1024]{1,0:T(8,128)} %copy-done.77, f32[4,1,1024]{2,1,0:T(1,128)S(1)} %get-tuple-element.203.logsum_ref, ...), custom_call_target="tpu_custom_call" | custom-call | flops 3690987520 | bytes 5767168 | tf_op jit(solution)/shard_map/pallas_call | solution.py:208
  869.6 4.0 convolution_convert_fusion.1
  873.6 4.0 fusion.101
  877.6 8.8 concatenate.94
  892.0 7.9 convolution_convert_fusion.4
  899.9 33.7 %back_last.2 = (f32[256,1408]{1,0:T(8,128)S(1)}, f32[1,1408]{1,0:T(1,128)S(1)}, f32[1,1408]{1,0:T(1,128)S(1)}, bf16[1,352,768]{2,1,0:T(8,128)(2,1)S(1)}, bf16[1,...) custom-call(bf16[4,256,1408]{2,1,0:T(8,128)(2,1)} %bitcast.410, f32[256,1408]{1,0:T(8,128)} %get-tuple-element.212.refs_1_, ...), custom_call_target="tpu_custom_call" | custom-call | flops 7208960 | bytes 4325376 | tf_op jit(solution)/shard_map/back_last/pallas_call | solution.py:611
  936.0 13.4 skip_back.2
  953.8 32.9 %spread.3 = (bf16[4,256,1408]{2,1,0:T(8,128)(2,1)S(1)}, bf16[352,768]{1,0:T(8,128)(2,1)S(1)}) custom-call(f32[256,1408]{1,0:T(8,128)S(1)} %copy-done.22, bf16[352,768]{1,0:T(8,128)(2,1)S(1)} %fusion.67.refs_1_), custom_call_target="tpu_custom_call" | custom-call | flops 7208960 | bytes 4325376 | tf_op jit(solution)/shard_map/spread/pallas_call | solution.py:611
  986.7 6.6 fusion.25
  999.9 4.3 fusion.31
  1008.0 4.0 convolution_convert_fusion.11
  1012.0 4.0 add_convert_fusion
  1019.9 75.5 %back.6 = (f32[256,1408]{1,0:T(8,128)S(1)}, f32[1,1408]{1,0:T(1,128)S(1)}, bf16[4,256,1408]{2,1,0:T(8,128)(2,1)}, bf16[1,2,352,768]{3,2,1,0:T(8,128)(2,1)S(1)}, ...) custom-call(bf16[4,256,1408]{2,1,0:T(8,128)(2,1)} %bitcast.415, ...), custom_call_target="tpu_custom_call" | custom-call | flops 7208960 | bytes 4325376 | tf_op jit(solution)/shard_map/back/pallas_call | solution.py:611
  1097.3 4.7 convolution_convert_fusion.27.grad_ref
  1102.2 7.6 shard_map.294
  1114.8 6.8 convolution_convert_fusion.10
  1132.8 5.0 convolution_convert_fusion.3
  1137.7 62.2 %back.7 = (f32[256,1408]{1,0:T(8,128)}, f32[1,1408]{1,0:T(1,128)S(1)}, bf16[4,256,1408]{2,1,0:T(8,128)(2,1)}, bf16[1,352,768]{2,1,0:T(8,128)(2,1)S(1)}, bf16[1,3...) custom-call(bf16[4,256,1408]{2,1,0:T(8,128)(2,1)} %bitcast.418, ...), custom_call_target="tpu_custom_call" | custom-call | flops 7208960 | bytes 4325376 | tf_op jit(solution)/shard_map/back/pallas_call | solution.py:611
  1200.9 4.8 convolution_convert_fusion.26.grad_ref
  1205.8 16.9 %shard_map.295 = (bf16[352,1024]{1,0:T(8,128)(2,1)S(1)}, bf16[352,1024]{1,0:T(8,128)(2,1)S(1)}, bf16[352,1024]{1,0:T(8,128)(2,1)S(1)}) custom-call(f32[352,1024]{1,0:T(8,128)S(1)} %copy-done.73, f32[352,1024]{1,0:T(8,128)} %copy-done.71, f32[352,1024]{1,0:T(8,128)} %copy-done.70, f32[4,1,1024]{2,1,0:T(1,128)S(1)} %copy-done.170, ...), custom_call_target="tpu_custom_call" | custom-call | flops 3690987520 | bytes 5767168 | tf_op jit(solution)/shard_map/pallas_call | solution.py:208
  1228.9 4.0 convolution_convert_fusion
  1232.9 3.9 fusion.100
  1236.8 8.9 concatenate.102
  1251.7 4.2 fusion.138
  1259.4 5.7 convolution_convert_fusion.2
  1265.1 34.3 %back_last.3 = (f32[256,1408]{1,0:T(8,128)S(1)}, f32[1,1408]{1,0:T(1,128)S(1)}, f32[1,1408]{1,0:T(1,128)S(1)}, bf16[1,352,768]{2,1,0:T(8,128)(2,1)S(1)}, bf16[1,...) custom-call(bf16[4,256,1408]{2,1,0:T(8,128)(2,1)} %bitcast.411, f32[256,1408]{1,0:T(8,128)} %get-tuple-element.237.refs_1_, ...), custom_call_target="tpu_custom_call" | custom-call | flops 7208960 | bytes 4325376 | tf_op jit(solution)/shard_map/back_last/pallas_call | solution.py:611
  1301.1 13.7 skip_back.3
  1317.9 5.5 fusion.97
  1323.4 4.4 add_convert_fusion.2
  1350.8 110.6 %gains.1 = (f32[4,2,136,128]{3,2,1,0:T(8,128)S(1)}, bf16[352,768]{1,0:T(8,128)(2,1)S(1)}, bf16[352,704]{1,0:T(8,128)(2,1)S(1)}, bf16[352,352]{1,0:T(8,128)(2,1)S(1)}, bf16[256,352]{1,0:T(8,128)(2,1)S(1)}) custom-call(f32[136,128]{1,0:T(8,128)S(1)} %copy-done.122, bf16[352,768]{1,0:T(8,128)(2,1)S(1)} %fusion.69.refs_1_, ...), custom_call_target="tpu_custom_call" | custom-call | tf_op jit(solution)/shard_map/gains/pallas_call | solution.py:773
  1466.3 22.5 %last.3 = f32[256,1408]{1,0:T(8,128)S(1)} custom-call(bf16[4,256,1408]{2,1,0:T(8,128)(2,1)S(1)} %bitcast.377, f32[256,1408]{1,0:T(8,128)S(1)} %copy-done.18), custom_call_target="tpu_custom_call" | custom-call | flops 7208960 | bytes 4325376 | tf_op jit(solution)/shard_map/last/pallas_call | solution.py:611
  1490.2 4.7 all-to-all-start
  (817 shorter events, 265.8 us)
Async XLA Ops:
  7.2 209.4 %all-gather.13.cloned.1.call-start = ((), (), s32[]{:S(2)}) async-start(), calls=%async_computation.10 | async-start | bytes 4956160 | tf_op jit(solution)/shard_map/all_gather | solution.py:986
  48.9 268.6 %all-gather.23.cloned.1.call-start = ((), (), s32[]{:S(2)}) async-start(), calls=%async_computation.23 | async-start | bytes 1548288 | tf_op jit(solution)/shard_map/all_gather | solution.py:1027
  54.3 100.4 %copy-start.1 = (f32[256,1408]{1,0:T(8,128)}, f32[256,1408]{1,0:T(8,128)S(1)}, u32[]{:S(2)}) copy-start(f32[256,1408]{1,0:T(8,128)S(1)} %convert_element_type.494.resid_ref) | copy-start | bytes 4325380
  58.3 95.3 %copy-start.195 = (bf16[2,256,1408]{2,1,0:T(8,128)(2,1)S(1)}, bf16[2,256,1408]{2,1,0:T(8,128)(2,1)}, u32[]{:S(2)}) copy-start(bf16[2,256,1408]{2,1,0:T(8,128)(2,1)} %param.18) | copy-start | bytes 4325380
  59.2 95.4 %copy-start.230 = (f32[2,2816]{1,0:T(2,128)S(1)}, f32[2,2816]{1,0:T(2,128)}, u32[]{:S(2)}) copy-start(f32[2,2816]{1,0:T(2,128)} %param.21) | copy-start | bytes 67588
  154.7 8.1 copy-start.205
  163.7 46.6 %copy-start.222 = (bf16[2,333,128]{2,0,1:T(2,128)(2,1)S(1)}, bf16[2,333,128]{2,0,1:T(2,128)(2,1)}, u32[]{:S(2)}) copy-start(bf16[2,333,128]{2,0,1:T(2,128)(2,1)} %param.20) | copy-start | bytes 511492
  163.8 44.6 %copy-start.133 = (f32[1,1408]{1,0:T(1,128)}, f32[1,1408]{1,0:T(1,128)S(1)}, u32[]{:S(2)}) copy-start(f32[1,1408]{1,0:T(1,128)S(1)} %get-tuple-element.486.refs_1_.refs_3_) | copy-start | bytes 16900
  163.8 84.4 %copy-start.135 = (f32[1,1408]{1,0:T(1,128)}, f32[1,1408]{1,0:T(1,128)S(1)}, u32[]{:S(2)}) copy-start(f32[1,1408]{1,0:T(1,128)S(1)} %get-tuple-element.485.refs_2_.refs_3_) | copy-start | bytes 16900
  211.0 108.8 %all-gather.15.cloned.1.call-start = ((), (), s32[]{:S(2)}) async-start(), calls=%async_computation.11 | async-start | bytes 1966080 | tf_op jit(solution)/shard_map/all_gather | solution.py:986
  213.3 109.3 %all-gather.11.cloned.1.call-start = ((), (), s32[]{:S(2)}) async-start(), calls=%async_computation.9 | async-start | bytes 2703360 | tf_op jit(solution)/shard_map/all_gather | solution.py:986
  214.8 252.8 %all-gather.25.cloned.1.call-start = ((), (), s32[]{:S(2)}) async-start(), calls=%async_computation.24 | async-start | bytes 8921088 | tf_op jit(solution)/shard_map/all_gather | solution.py:1074
  216.5 110.0 %copy-start.32 = (f32[88,1024]{1,0:T(8,128)}, f32[88,1024]{1,0:T(8,128)S(1)}, u32[]{:S(2)}) copy-start(f32[88,1024]{1,0:T(8,128)S(1)} %get-tuple-element.495.cos_ref) | copy-start | bytes 1081348
  216.5 630.2 %copy-start.29 = (f32[88,1024]{1,0:T(8,128)}, f32[88,1024]{1,0:T(8,128)S(1)}, u32[]{:S(2)}) copy-start(f32[88,1024]{1,0:T(8,128)S(1)} %get-tuple-element.494.sin_ref) | copy-start | bytes 1081348
  224.2 9.9 copy-start.70
  224.2 9.9 copy-start.71
  224.2 9.9 copy-start.72
  224.2 16.3 %copy-start.210 = (bf16[1,1,352,176]{2,3,1,0:T(8,128)(2,1)S(1)}, bf16[1,1,352,176]{2,3,1,0:T(8,128)(2,1)}, u32[]{:S(2)}) copy-start(bf16[1,1,352,176]{2,3,1,0:T(8,128)(2,1)} %get-tuple-element.416) | copy-start | bytes 371716
  234.9 13.2 copy-start.169
  235.0 279.9 %all-gather.19.cloned.1.call-start = ((), (), s32[]{:S(2)}) async-start(), calls=%async_computation.13 | async-start | bytes 4956160 | tf_op jit(solution)/shard_map/all_gather | solution.py:986
  248.1 59.9 %copy-start.182 = (bf16[1,176,352]{1,2,0:T(8,128)(2,1)S(1)}, bf16[1,176,352]{1,2,0:T(8,128)(2,1)}, u32[]{:S(2)}) copy-start(bf16[1,176,352]{1,2,0:T(8,128)(2,1)} %copy.254) | copy-start | bytes 371716
  248.2 59.9 %copy-start.183 = (bf16[1,1,352,176]{3,2,1,0:T(8,128)(2,1)S(1)}, bf16[1,1,352,176]{3,2,1,0:T(8,128)(2,1)}, u32[]{:S(2)}) copy-start(bf16[1,1,352,176]{3,2,1,0:T(8,128)(2,1)} %copy.253) | copy-start | bytes 371716
  248.2 59.9 %copy-start.184 = (bf16[1,1,352,176]{3,2,1,0:T(8,128)(2,1)S(1)}, bf16[1,1,352,176]{3,2,1,0:T(8,128)(2,1)}, u32[]{:S(2)}) copy-start(bf16[1,1,352,176]{3,2,1,0:T(8,128)(2,1)} %copy.252) | copy-start | bytes 371716
  248.2 59.9 %copy-start.185 = (bf16[1,1,352,176]{3,2,1,0:T(8,128)(2,1)S(1)}, bf16[1,1,352,176]{3,2,1,0:T(8,128)(2,1)}, u32[]{:S(2)}) copy-start(bf16[1,1,352,176]{3,2,1,0:T(8,128)(2,1)} %copy.251) | copy-start | bytes 371716
  313.7 288.6 %all-gather.21.cloned.1.call-start = ((), (), s32[]{:S(2)}) async-start(), calls=%async_computation.14 | async-start | bytes 1966080 | tf_op jit(solution)/shard_map/all_gather | solution.py:986
  326.5 9.6 copy-start.66
  336.1 78.3 %copy-start.250 = (bf16[2,2,352,768]{3,2,1,0:T(8,128)(2,1)S(1)}, bf16[2,2,352,768]{3,2,1,0:T(8,128)(2,1)}, u32[]{:S(2)}) copy-start(bf16[2,2,352,768]{3,2,1,0:T(8,128)(2,1)} %get-tuple-element.169) | copy-start | bytes 6488068
  470.1 7.9 copy-start.111
  470.1 7.9 copy-start.138
  470.1 40.7 %copy-start.201 = (bf16[1,1,256,176]{3,2,1,0:T(8,128)(2,1)S(1)}, bf16[1,1,256,176]{3,2,1,0:T(8,128)(2,1)}, u32[]{:S(2)}) copy-start(bf16[1,1,256,176]{3,2,1,0:T(8,128)(2,1)} %copy-done.200) | copy-start | bytes 270340
  470.1 40.7 %copy-start.203 = (bf16[1,1,256,176]{3,2,1,0:T(8,128)(2,1)S(1)}, bf16[1,1,256,176]{3,2,1,0:T(8,128)(2,1)}, u32[]{:S(2)}) copy-start(bf16[1,1,256,176]{3,2,1,0:T(8,128)(2,1)} %copy-done.202) | copy-start | bytes 270340
  478.0 34.1 %copy-start.2 = (f32[256,1408]{1,0:T(8,128)}, f32[256,1408]{1,0:T(8,128)S(1)}, u32[]{:S(2)}) copy-start(f32[256,1408]{1,0:T(8,128)S(1)} %get-tuple-element.177.refs_0_.refs_1_.refs_2_) | copy-start | bytes 4325380
  512.1 93.4 %all-gather.17.cloned.1.call-start = ((), (), s32[]{:S(2)}) async-start(), calls=%async_computation.12 | async-start | bytes 2703360 | tf_op jit(solution)/shard_map/all_gather | solution.py:986
  514.8 501.3 %reduce-scatter.13.cloned.1.call-start = ((), (), s32[]{:S(2)}) async-start(), calls=%async_computation.17 | async-start | bytes 1966080 | tf_op jit(solution)/shard_map/reduce_scatter | solution.py:1132
  522.3 10.6 copy-start.77
  522.3 10.6 copy-start.78
  522.3 10.6 copy-start.79
  538.0 64.2 %copy-start.207 = (bf16[42,8,8,128]{3,1,2,0:T(8,128)(2,1)S(1)}, bf16[42,8,8,128]{3,1,2,0:T(8,128)(2,1)}, u32[]{:S(2)}) copy-start(bf16[42,8,8,128]{3,1,2,0:T(8,128)(2,1)} %copy.261) | copy-start | bytes 2064388
  752.8 264.4 %reduce-scatter.11.cloned.1.call-start = ((), (), s32[]{:S(2)}) async-start(), calls=%async_computation.16 | async-start | bytes 2703360 | tf_op jit(solution)/shard_map/reduce_scatter | solution.py:1132
  770.3 248.1 %reduce-scatter.9.cloned.1.call-start = ((), (), s32[]{:S(2)}) async-start(), calls=%async_computation.15 | async-start | bytes 4956160 | tf_op jit(solution)/shard_map/reduce_scatter | solution.py:1132
  886.4 246.4 %reduce-scatter.15.cloned.1.call-start = ((), (), s32[]{:S(2)}) async-start(), calls=%async_computation.18 | async-start | bytes 8921088 | tf_op jit(solution)/shard_map/reduce_scatter | solution.py:1257
  889.6 62.3 %copy-start.5 = (bf16[1,2,352,768]{3,2,1,0:T(8,128)(2,1)}, bf16[1,2,352,768]{3,2,1,0:T(8,128)(2,1)S(1)}, u32[]{:S(2)}) copy-start(bf16[1,2,352,768]{3,2,1,0:T(8,128)(2,1)S(1)} %add_convert_fusion.6) | copy-start | bytes 3244036
  892.0 7.9 copy-start.7
  899.9 36.1 %copy-start.16 = (bf16[256,1408]{1,0:T(8,128)(2,1)S(1)}, bf16[256,1408]{1,0:T(8,128)(2,1)}, u32[]{:S(2)}) copy-start(bf16[256,1408]{1,0:T(8,128)(2,1)} %get-tuple-element.382.skip_ref) | copy-start | bytes 2162692
  935.2 14.2 copy-start.147
  951.6 392.6 %reduce-scatter.21.cloned.1.call-start = ((), (), s32[]{:S(2)}) async-start(), calls=%async_computation.21 | async-start | bytes 1966080 | tf_op jit(solution)/shard_map/reduce_scatter | solution.py:1132
  951.9 34.8 %copy-start.258 = (bf16[2,2,352,768]{3,2,1,0:T(8,128)(2,1)S(1)}, bf16[2,2,352,768]{3,2,1,0:T(8,128)(2,1)}, u32[]{:S(2)}) copy-start(bf16[2,2,352,768]{3,2,1,0:T(8,128)(2,1)} %get-tuple-element.170) | copy-start | bytes 6488068
  986.7 21.4 %copy-start.156 = (bf16[4,256,1408]{2,1,0:T(8,128)(2,1)}, bf16[4,256,1408]{2,1,0:T(8,128)(2,1)S(1)}, u32[]{:S(2)}) copy-start(bf16[4,256,1408]{2,1,0:T(8,128)(2,1)S(1)} %get-tuple-element.222) | copy-start | bytes 8650756
  1019.9 77.3 %copy-start.247 = (bf16[1408,704]{1,0:T(8,128)(2,1)S(1)}, bf16[1408,704]{1,0:T(8,128)(2,1)}, u32[]{:S(2)}) copy-start(bf16[1408,704]{1,0:T(8,128)(2,1)} %all-gather.11.cloned.1.call-done) | copy-start | bytes 5947396
  1102.2 8.6 copy-start.209
  1114.7 231.4 %reduce-scatter.19.cloned.1.call-start = ((), (), s32[]{:S(2)}) async-start(), calls=%async_computation.20 | async-start | bytes 2703360 | tf_op jit(solution)/shard_map/reduce_scatter | solution.py:1132
  1129.9 217.5 %reduce-scatter.17.cloned.1.call-start = ((), (), s32[]{:S(2)}) async-start(), calls=%async_computation.19 | async-start | bytes 4956160 | tf_op jit(solution)/shard_map/reduce_scatter | solution.py:1132
  1245.8 278.3 %reduce-scatter.23.cloned.1.call-start = ((), (), s32[]{:S(2)}) async-start(), calls=%async_computation.22 | async-start | bytes 8921088 | tf_op jit(solution)/shard_map/reduce_scatter | solution.py:1257
  1250.4 8.1 copy-start.233
  1265.1 35.9 %copy-start.14 = (bf16[256,1408]{1,0:T(8,128)(2,1)S(1)}, bf16[256,1408]{1,0:T(8,128)(2,1)}, u32[]{:S(2)}) copy-start(bf16[256,1408]{1,0:T(8,128)(2,1)} %copy-done.13) | copy-start | bytes 2162692
  1265.1 35.9 %copy-start.69 = (bf16[256,2816]{1,0:T(8,128)(2,1)S(1)}, bf16[256,2816]{1,0:T(8,128)(2,1)}, u32[]{:S(2)}) copy-start(bf16[256,2816]{1,0:T(8,128)(2,1)} %copy-done.68) | copy-start | bytes 4325380
  1265.1 35.9 %copy-start.132 = (f32[1,2816]{1,0:T(1,128)S(1)}, f32[1,2816]{1,0:T(1,128)}, u32[]{:S(2)}) copy-start(f32[1,2816]{1,0:T(1,128)} %copy-done.131) | copy-start | bytes 33796
  1301.0 13.7 copy-start.118
  1301.0 13.7 copy-start.143
  1301.0 13.7 copy-start.151
  1347.3 117.0 %copy-start.18 = (f32[256,1408]{1,0:T(8,128)S(1)}, f32[256,1408]{1,0:T(8,128)}, u32[]{:S(2)}) copy-start(f32[256,1408]{1,0:T(8,128)} %copy-done.17) | copy-start | bytes 4325380
  1466.3 22.5 %slice-start = ((bf16[384,1024]{1,0:T(8,128)(2,1)}), bf16[333,1024]{1,0:T(8,128)(2,1)S(1)}, s32[]{:S(2)}) async-start(bf16[384,1024]{1,0:T(8,128)(2,1)} %convolution_add_fusion), calls=%async_computation.25 | async-start | bytes 1376256 | tf_op jit(solution)/shard_map/slice | solution.py:1312
  1489.1 8.5 copy-start.121
  1490.2 31.6 %all-to-all-start = ((bf16[8,333,128]{2,1,0:T(8,128)(2,1)}), bf16[8,333,128]{2,1,0:T(8,128)(2,1)}, u32[]{:S(2)}, u32[]{:S(2)}) async-start(bf16[8,333,128]{2,1,0:T(8,128)(2,1)} %bitcast.421), calls=%async_computation.7 | async-start | bytes 1376256 | tf_op jit(solution)/shard_map/all_to_all | solution.py:1314
  (226 other events, 705.1 us)
Sparse Core Ops, SparseCore 0:
  49.0 50.7 all-gather.12
  211.2 22.7 all-gather.22
  236.4 38.7 all-gather.14
  277.4 41.8 all-gather.10
  322.7 100.7 all-gather.24
  425.8 59.9 all-gather.18
  512.3 29.0 all-gather.20
  543.7 53.4 all-gather.16
  753.0 28.5 reduce-scatter.12
  784.4 53.0 reduce-scatter.10
  886.5 56.3 reduce-scatter.8
  951.8 160.1 reduce-scatter.14
  1114.9 30.9 reduce-scatter.20
  1148.7 51.3 reduce-scatter.18
  1245.9 53.2 reduce-scatter.16
  1316.0 164.8 reduce-scatter.22

commit v3 on v2

--- a/solution.py
+++ b/solution.py
@@ -239,11 +239,16 @@
 
 
 def here():
-    return lax.axis_index("row"), lax.axis_index("lat"), lax.axis_index("tp")
+    rank = 2 * lax.axis_index("chip") + lax.axis_index("core")
+    return lax.axis_index("row"), lax.axis_index("lat"), rank
+
+
+def rank_count():
+    return 2 * lax.axis_size("chip")
 
 
 def device_at(row, lat, rank):
-    return {"row": row, "lat": lat, "tp": rank}
+    return {"row": row, "lat": lat, "chip": rank // 2, "core": rank % 2}
 
 
 def row_peers():
@@ -254,6 +259,14 @@
 
 def peers_along(axis):
     row, lat, rank = here()
+    if axis == "core":
+        other = 1 - rank % 2
+        return rank % 2, 2, [(other, device_at(row, lat, rank // 2 * 2 + other))]
+    if axis == "chip":
+        count = rank_count() // 2
+        me = rank // 2
+        places = [(me + step) % count for step in range(1, count)]
+        return me, count, [(place, device_at(row, lat, 2 * place + rank % 2)) for place in places]
     if axis == "lat":
         return lat, LATENTS, [(1 - lat, device_at(row, 1 - lat, rank))]
     fast = lax.axis_size("row") // 2
@@ -271,7 +284,7 @@
 
 def places():
     row, lat, rank = here()
-    chips = lax.axis_size("tp") // 2
+    chips = rank_count() // 2
     chip, core = rank // 2, rank % 2
     sibling = device_at(row, lat, 2 * chip + 1 - core)
     ahead = [(chip + step) % chips for step in range(1, chips)]
@@ -303,7 +316,8 @@
 
 
 def rider_count(axis):
-    return {"lat": LATENTS, "a": 2, "b": lax.axis_size("row") // 2}[axis]
+    counts = {"lat": LATENTS, "a": 2, "b": lax.axis_size("row") // 2, "chip": rank_count() // 2}
+    return counts[axis]
 
 
 def rider_shape(rider):
@@ -371,7 +385,7 @@
 
 def gather_everyone(source, target, sems, local_sem, between):
     row, lat, _ = here()
-    ranks = lax.axis_size("tp")
+    ranks = rank_count()
     rank, chip, core, sibling, ahead, _ = places()
     chips = ranks // 2
     fast_at, fast, fast_peers = peers_along("b")
@@ -451,7 +465,7 @@
 
 
 def gather_copies():
-    rows, chips = lax.axis_size("row"), lax.axis_size("tp") // 2
+    rows, chips = lax.axis_size("row"), rank_count() // 2
     fast, slow = rows // 2, 2
     count = 1 + (chips - 1) * LATENTS + chips * (fast - 1 + slow - 1)
     count += chips * (fast * (slow - 1) + slow * (fast - 1))
@@ -461,7 +475,8 @@
 def token_kernel(sums, spreads, body, n_in, n_out, modes, shared, *refs):
     refs = list(refs)
     take = lambda count: [refs.pop(0) for _ in range(count)]
-    part = refs.pop(0) if sums else None
+    if sums:
+        lefts, rights = take(sums[1]), take(sums[1])
     ins, sources = take(n_in), take(len(modes))
     block = refs.pop(0) if shared else None
     outs = take(n_out)
@@ -469,7 +484,11 @@
     targets = take(len(modes))
     blocks = refs.pop(0) if shared else None
     if sums:
-        from_sibling, outgoing, incoming, pair_sems, sum_sems = take(5)
+        part, from_sibling, outgoing, incoming, pair_sems, sum_sems = take(6)
+        if sums[0]:
+            turned = take(1)
+            turned[0][...] = lefts[0][...].T
+            lefts = turned
     if spreads:
         chip_sems, own_sems, forward_sems = take(3)
     rank, chip, core, sibling, ahead, behind = places()
@@ -485,6 +504,15 @@
     greet(met)
     started, riding = [], []
 
+    def multiply(place):
+        some = pl.ds(pl.multiple_of(place * rows, 128), rows)
+        term = None
+        for left, right in zip(lefts, rights):
+            piece = dot(left[some], right[...], 1, 1)
+            term = piece if term is None else term + piece
+        part[place] = term.astype(B16)
+
+
     def ride():
         if modes:
             riding.extend(start_riders(modes, sources, targets, *refs[:2]))
@@ -494,6 +522,7 @@
     if sums:
         pair = {}
         for order, place in enumerate(ahead + [chip]):
+            multiply(2 * place + 1 - core)
             for index, span in enumerate(spans):
                 copy = remote(
                     part.at[2 * place + 1 - core, span],
@@ -506,6 +535,7 @@
                 pair[order, index] = copy
         crossing = {}
         for order, place in enumerate(ahead):
+            multiply(2 * place + core)
             for index, span in enumerate(spans):
                 pair[order, index].wait_recv()
                 outgoing[order, span] = (
@@ -523,6 +553,8 @@
                 crossing[order, index] = copy
     if not shared:
         ride()
+    if sums:
+        multiply(rank)
     direct = {}
     for index, span in enumerate(spans):
         total = None
@@ -573,21 +605,28 @@
 
 
 def token_call(name, body, part, ins, outs, spreads, riders=(), shared=None):
-    ranks = lax.axis_size("tp")
+    ranks = rank_count()
     chips = ranks // 2
     rows, width = ins[0].shape
-    sums = part is not None
+    sums = None
+    if part is not None:
+        turn, lefts, rights = part
+        sums = (turn, len(lefts))
     modes, key, cargo, cargo_shapes = split_riders(riders)
     shapes = [jax.ShapeDtypeStruct(shape, F32) for shape in outs]
     scratch = []
     if sums:
+        key = key + tuple(left.shape for left in lefts)
         scratch += [
+            pltpu.VMEM((ranks, rows, width), B16),
             pltpu.VMEM((chips, rows, width), B16),
             pltpu.VMEM((chips - 1, rows, width), B16),
             pltpu.VMEM((chips - 1, rows, width), B16),
             pltpu.SemaphoreType.DMA((2, chips * CHUNKS)),
             pltpu.SemaphoreType.DMA((2, (chips - 1) * CHUNKS)),
         ]
+        if turn:
+            scratch.append(pltpu.VMEM(lefts[0].shape[::-1], B16))
     if spreads:
         shapes.append(jax.ShapeDtypeStruct((ranks, rows, width), B16))
         scratch += [
@@ -605,7 +644,7 @@
             pltpu.SemaphoreType.DMA((2, gather_copies())),
             pltpu.SemaphoreType.DMA((1,)),
         ]
-    args = ([part.reshape(ranks, rows, width)] if sums else []) + list(ins)
+    args = (list(lefts) + list(rights) if sums else []) + list(ins)
     whole = pl.BlockSpec(memory_space=pltpu.VMEM)
     away = pl.BlockSpec(memory_space=pl.ANY)
     results = pl.pallas_call(
@@ -638,7 +677,7 @@
     targets = take(len(modes))
     got, terms, landed, cond_sems, term_sems, out_sems = take(6)
     row, lat, rank = here()
-    rows, ranks = lax.axis_size("row"), lax.axis_size("tp")
+    rows, ranks = lax.axis_size("row"), rank_count()
     columns = LATENTS * ranks
     column = lat * ranks + rank
     others = row_peers()
@@ -685,7 +724,7 @@
 
 
 def start_call(cond, mod_w, riders):
-    rows, ranks = lax.axis_size("row"), lax.axis_size("tp")
+    rows, ranks = lax.axis_size("row"), rank_count()
     layers, depth, local = mod_w.shape
     tall, wide = depth + -depth % 128, local + -local % 128
     blocks = jnp.transpose(cond.astype(F32).reshape(LATENTS, rows, depth), (1, 0, 2))
@@ -737,7 +776,7 @@
     targets = take(len(modes))
     parts, pair, part_sems, pair_sems, out_sems = take(5)
     row, lat, rank = here()
-    ranks = lax.axis_size("tp")
+    ranks = rank_count()
     others = row_peers()
     company = [device_at(row, lat, (rank + step) % ranks) for step in range(1, ranks)]
     greet(company + [lat_peer()] + [device for _, device in others])
@@ -766,7 +805,7 @@
 
 
 def end_call(value, riders):
-    rows, ranks = lax.axis_size("row"), lax.axis_size("tp")
+    rows, ranks = lax.axis_size("row"), rank_count()
     modes, key, cargo, cargo_shapes = split_riders(riders)
     whole = pl.BlockSpec(memory_space=pltpu.VMEM)
     away = pl.BlockSpec(memory_space=pl.ANY)
@@ -886,16 +925,46 @@
 
 
 def skip_back_kernel(
-    grad_ref, low_ref, resid_ref, skip_ref, gain_ref, weight_ref, weight_out, resid_out, skip_out, gain_out, norm_grad
+    grad_ref,
+    low_ref,
+    resid_ref,
+    skip_ref,
+    gain_ref,
+    weight_ref,
+    weight_out,
+    resid_out,
+    skip_out,
+    gain_out,
+    norm_grad,
+    leaving,
+    grad_sibling,
+    low_sibling,
+    sems,
 ):
     tokens, width = resid_ref.shape
     parts, _, depth = weight_ref.shape
+    blocks = LATENTS * rank_count()
+    local = width // blocks
     step = tokens // CHUNKS
+    sibling = peers_along("core")[2][0][1]
+    core = lax.axis_index("core")
+    greet([sibling])
     grad_low = grad_ref[...].astype(B16)
-    grad_t = grad_low.T
+    even, odd = [], []
+    for block in range(0, blocks, 2):
+        even.append(grad_ref[:, block * local : (block + 1) * local])
+        odd.append(grad_ref[:, (block + 1) * local : (block + 2) * local])
+    even, odd = jnp.concatenate(even, axis=1), jnp.concatenate(odd, axis=1)
+    leaving[...] = jnp.where(core == 0, odd, even).astype(B16)
+    staying = jnp.where(core == 0, even, odd).astype(B16)
+    copies = [
+        remote(leaving, grad_sibling, sems, 0, sibling),
+        remote(low_ref, low_sibling, sems, 1, sibling),
+    ]
+    for copy in copies:
+        copy.start()
     for part in range(parts):
         columns = slice(part * depth, (part + 1) * depth)
-        weight_out[part] = dot(grad_t, low_ref[:, columns], 1, 0).astype(B16)
         norm_grad[:, columns] = dot(grad_low, weight_ref[part], 1, 0)
     for index in range(CHUNKS):
         span = pl.ds(index * step, step)
@@ -906,9 +975,17 @@
         value = norm_back(normed, rstd, grad * gain_ref[...])
         resid_out[span] = value[:, :width]
         skip_out[span] = value[:, width:]
-
-
-def local_call(name, body, args, shapes, scratch=()):
+    for copy in copies:
+        copy.wait()
+    mine_t, theirs_t = staying.T, grad_sibling[...].T
+    for part in range(parts):
+        columns = slice(part * depth, (part + 1) * depth)
+        term = dot(mine_t, low_ref[:, columns], 1, 0)
+        term = term + dot(theirs_t, low_sibling[:, columns], 1, 0)
+        weight_out[part] = term.astype(B16)
+
+
+def local_call(name, body, args, shapes, scratch=(), params=None):
     return pl.pallas_call(
         body,
         out_shape=shapes,
@@ -916,7 +993,7 @@
         out_specs=[pl.BlockSpec(memory_space=pltpu.VMEM)] * len(shapes),
         scratch_shapes=list(scratch),
         name=name,
-        compiler_params=pltpu.CompilerParams(vmem_limit_bytes=VMEM_LIMIT),
+        compiler_params=params or pltpu.CompilerParams(vmem_limit_bytes=VMEM_LIMIT),
     )(*args)
 
 
@@ -931,15 +1008,24 @@
 
 def skip_backward(grad, low, resid, skip, gain, weight):
     tokens, width = resid.shape
+    parts, _, depth = weight.shape
+    half = width // 2
     shapes = [
-        jax.ShapeDtypeStruct(weight.shape, B16),
+        jax.ShapeDtypeStruct((parts, half, depth), B16),
         jax.ShapeDtypeStruct(resid.shape, F32),
         jax.ShapeDtypeStruct(resid.shape, F32),
         jax.ShapeDtypeStruct(gain.shape, F32),
     ]
-    scratch = [pltpu.VMEM((tokens, 2 * width), F32)]
+    scratch = [
+        pltpu.VMEM((tokens, 2 * width), F32),
+        pltpu.VMEM((tokens, half), B16),
+        pltpu.VMEM((tokens, half), B16),
+        pltpu.VMEM((tokens, 2 * width), B16),
+        pltpu.SemaphoreType.DMA((2, 2)),
+    ]
     args = [grad, low, resid, skip, gain, weight]
-    return local_call("skip_back", skip_back_kernel, args, shapes, scratch)
+    params = comm_params(number_of("skip_back", ()))
+    return local_call("skip_back", skip_back_kernel, args, shapes, scratch, params)
 
 
 def on_device(
@@ -962,10 +1048,10 @@
     cotangent,
 ):
     rows = lax.axis_size("row")
-    ranks = lax.axis_size("tp")
+    ranks = rank_count()
     row = lax.axis_index("row")
     lat = lax.axis_index("lat")
-    rank = lax.axis_index("tp")
+    rank = here()[2]
     width = latent.shape[1]
     depth = qkv_w.shape[2]
     local = qkv_w.shape[3]
@@ -974,7 +1060,6 @@
     text_depth = ckv_w.shape[2]
     text_count = text.shape[1]
     tables = rotary_tables()
-    everyone = ("row", "lat", "tp")
 
 
     def gather_both(pack, other, sizes):
@@ -1024,7 +1109,7 @@
     down_stack = down_half = None
 
     def own_text(text):
-        text_parts = lax.all_gather(text, ("lat", "tp"), axis=0)
+        text_parts = lax.all_gather(text, ("lat", "chip", "core"), axis=0)
         text_own = lax.dynamic_index_in_dim(text_parts, lat, axis=1, keepdims=False)
         text_own = jnp.transpose(text_own, (1, 0, 2)).reshape(text_count, -1)
         return jnp.pad(text_own, ((0, -text_count % 128), (0, 0)))
@@ -1071,13 +1156,15 @@
         if following:
             skip_next, self_low = lax.optimization_barrier((skip_w[layer + 1].T, self_low))
             skip_full.append(
-                lax.all_gather(skip_next, everyone, axis=0).reshape(rows, width, -1)
+                lax.all_gather(skip_next, ("row", "lat", "chip", "core"), axis=0).reshape(
+                    rows, width, -1
+                )
             )
         riders = gather_two(up_half) + gather_one(down_stack)
         if following:
             riders.append(swap(attn_pack[layer + 1]))
         resid_two, third_all, *others = middle_tokens(
-            dot(self_low, out_t, 0, 1).astype(B16), resid_one, attn_gain[layer, 1:2], riders
+            (True, [self_low], [out_t]), resid_one, attn_gain[layer, 1:2], riders
         )
         up_w, down_half = whole(others[:2]), others[2:4]
         if following:
@@ -1095,7 +1182,7 @@
         keep["cross"] = (cross_query, text_keys, text_values, cross_lse, cross_low)
         riders = gather_two(down_half) + (stack(up_pack[layer + 1]) if following else [])
         resid_three, second_all, *others = middle_tokens(
-            dot(cross_low, cout_t, 0, 1).astype(B16),
+            (True, [cross_low], [cout_t]),
             resid_two,
             ffn_gain[layer : layer + 1],
             riders,
@@ -1110,9 +1197,9 @@
         keep["hidden"] = hidden
         keep["act"] = act_low
         keep["ffn_w"] = (up_w, down_w)
-        term = sum(dot(act_low[part], down_w[part], 1, 1) for part in range(LATENTS))
-        riders = gather_one(up_stack) + stack(down_pack[layer + 1]) if following else []
-        term = term.astype(B16)
+        term = (False, act_low, down_w)
+        if following:
+            riders = gather_one(up_stack) + stack(down_pack[layer + 1])
         if following:
             resid, *others = last_tokens(term, resid_three, riders)
         if following:
@@ -1157,6 +1244,14 @@
         high = pick(halves[1], fast_at, 1) + jnp.sum(arrived[1].astype(F32), axis=0)
         return [low.astype(B16), high.astype(B16)]
 
+    def chip_rider(value):
+        return ("scatter", "chip", 1, None, value)
+
+    def added_chips(value, arrived):
+        total = pick(value, rank // 2, 1) + jnp.sum(arrived.astype(F32), axis=0)
+        mine = jnp.where(lat == 0, total[0], total[1])
+        return mine, jnp.where(lat == 0, total[1], total[0]).astype(B16)
+
     def scatter_two(halves):
         return [("scatter", "b", 0, None, halves[0]), ("scatter", "a", 0, None, halves[1])]
 
@@ -1178,25 +1273,26 @@
         if waiting is not None:
             grad_all, other = spread_tokens(grad, [swap(waiting["down"][1])])
             waiting["store"]["down"] = waiting["down"][0] + other.astype(F32)
-        ups, downs = [], []
-        term = None
+        ups, downs, hidden_grads = [], [], []
         for part in range(LATENTS):
             act_grad = dot(grad_all, down_w[part], 1, 0)
             hidden_grad = (act_grad * gelu_grad(keep["hidden"][part])).astype(B16)
             downs.append(by_rows(dot(grad_all, keep["act"][part], 0, 0)))
             ups.append(by_rows(dot(keep["second_all"], hidden_grad, 0, 0)))
-            piece = dot(hidden_grad, up_w[part], 1, 1)
-            term = piece if term is None else term + piece
+            hidden_grads.append(hidden_grad)
         riders = scatter_one(ups)
+        if waiting is not None:
+            riders.append(chip_rider(waiting["skip"]))
         names = ("attn", "cross", "text")
         if waiting is not None:
             riders += [swap(waiting[name][1]) for name in names]
         grad_three, gain_ffn, grad_all, *others = back_tokens(
-            term.astype(B16), grad, keep["second"], ffn_gain[layer : layer + 1], riders
+            (False, hidden_grads, up_w), grad, keep["second"], ffn_gain[layer : layer + 1], riders
         )
         ups = added_one(ups, others[:2])
         if waiting is not None:
-            for name, other in zip(names, others[2:]):
+            waiting["skip"] = added_chips(waiting["skip"], others[2])
+            for name, other in zip(names, others[3:]):
                 waiting["store"][name] = finish(waiting[name][0], other)
 
         query_w, cout_t = keep["cross_w"]
@@ -1213,18 +1309,18 @@
         text_grad = text_grad + dot(both, text_full_w[layer], 0, 1)
         riders = scatter_two(ups) + scatter_one(downs)
         if waiting is not None:
-            query_grad, waiting["store"]["skip"] = lax.optimization_barrier(
-                (query_grad, waiting["store"]["skip"])
-            )
+            riders.append(swap(waiting["skip"][1]))
         grad_two, gain_cross, grad_all, *others = back_tokens(
-            dot(query_grad, query_w, 0, 1).astype(B16),
+            (True, [query_grad], [query_w]),
             grad_three,
             keep["third"],
             attn_gain[layer, 1:2],
             riders,
         )
         up_mine, up_theirs = added_two(ups, others[:2])
-        downs = added_one(downs, others[2:])
+        downs = added_one(downs, others[2:4])
+        if waiting is not None:
+            waiting["store"]["skip"] = waiting["skip"][0] + others[4].astype(F32)
 
         weight = attn_full[layer]
         query, keys, values, self_lse, self_low = keep["self"]
@@ -1232,17 +1328,29 @@
         wout_grad = dot(grad_all, self_low, 0, 1)
         three = attention_back(query, keys, values, self_lse, out_grad, tables, SEQ, True)
         both = jnp.concatenate(three, axis=0)
-        term = dot(both, weight[:, : 3 * wide], 0, 1)
         qkv_grad = dot(keep["first_all"], both, 0, 1)
+        riders = scatter_two(downs) + [swap(up_theirs)]
+        if layer == 0:
+            blocks = text_grad[:text_count].astype(B16).reshape(text_count, LATENTS * ranks, -1)
+            blocks = jnp.transpose(blocks, (1, 0, 2))
+            blocks = lax.all_to_all(
+                blocks, ("lat", "chip", "core"), split_axis=0, concat_axis=0, tiled=True
+            )
+            both, blocks = lax.optimization_barrier((both, blocks))
+            text_out = jnp.sum(
+                blocks.astype(F32).reshape((LATENTS, ranks) + blocks.shape[1:]), axis=1
+            )
+            riders += [swap(cross_sum[1]), swap(text_sum[1])]
         grad_one, gain_self, shift_own, *others = back_last_tokens(
-            term.astype(B16),
+            (True, [both], [weight[:, : 3 * wide]]),
             grad_two,
             keep["first"],
             attn_gain[layer, 0:1],
-            scatter_two(downs) + [swap(up_theirs)],
+            riders,
         )
         down_sum = added_two(downs, others[:2])
         up_grad = up_mine + others[2].astype(F32)
+        early = others[3:]
         attn_sum = sum_over_rows([qkv_grad, wout_grad], [3, 1])
 
         packed, grad, skip_store[layer], gain_skip = skip_backward(
@@ -1253,11 +1361,12 @@
             skip_gain[layer : layer + 1],
             skip_full[layer],
         )
-        packed = packed.reshape(rows * LATENTS * ranks, local, -1)
-        skip_sum = lax.psum_scatter(packed, everyone, scatter_dimension=0, tiled=False)
+        skip_sum = lax.psum_scatter(packed, "row", scatter_dimension=0, tiled=False)
+        skip_sum = skip_sum.reshape(LATENTS, ranks // 2, local, -1)
         gain_store[layer] = (gain_skip[0], jnp.concatenate([gain_self, gain_cross]), gain_ffn[0])
-        store = dict(skip=skip_sum, up=up_grad)
+        store = dict(up=up_grad)
         waiting = dict(attn=attn_sum, cross=cross_sum, text=text_sum, down=down_sum, store=store)
+        waiting["skip"] = skip_sum
         weight_store[layer] = store
         shift_store[layer] = shift_own
 
@@ -1271,14 +1380,16 @@
         + [shift_store[layer].reshape(-1) for layer in range(layers)]
     )
     flat = jnp.pad(flat, (0, -flat.size % 1024)).reshape(-1, 128)
-    flat_all, down_other, *others = end_call(
-        flat, [swap(waiting[name][1]) for name in ("down",) + names]
-    )
+    flat_all, down_other = end_call(flat, [swap(waiting["down"][1])])
     waiting["store"]["down"] = waiting["down"][0] + down_other.astype(F32)
-    for name, other in zip(names, others):
+    final_resid, flat_all = lax.optimization_barrier((final_resid, flat_all))
+    riders = [chip_rider(waiting["skip"]), swap(waiting["attn"][1])]
+    mixed, arrived, attn_other = last_tokens(final_term, final_resid, riders)
+    mine, theirs = added_chips(waiting["skip"], arrived)
+    other = lax.ppermute(theirs, "lat", [(0, 1), (1, 0)])
+    waiting["store"]["skip"] = mine + other.astype(F32)
+    for name, other in zip(names, [attn_other] + early):
         waiting["store"][name] = finish(waiting[name][0], other)
-    final_term, text_grad, flat_all = lax.optimization_barrier((final_term, text_grad, flat_all))
-    mixed = last_tokens(final_term, final_resid)[0]
     flat_all = flat_all.reshape(rows * LATENTS, -1)
     totals = jnp.sum(flat_all, axis=0)
     gains, start = [], 0
@@ -1294,7 +1405,7 @@
 
     weight_store = [
         (
-            store["skip"].astype(F32).T,
+            store["skip"].T,
             dot(cond_rows, shift_cols[:, layer], 0, 0),
             jnp.stack(store["attn"][:3]),
             store["attn"][3].T,
@@ -1309,12 +1420,6 @@
     weight_outs = tuple(
         jnp.stack([weight_store[layer][slot] for layer in range(layers)]) for slot in range(9)
     )
-    blocks = text_grad[:text_count].astype(B16).reshape(text_count, LATENTS * ranks, -1)
-    blocks = jnp.transpose(blocks, (1, 0, 2))
-    blocks = lax.all_to_all(blocks, ("lat", "tp"), split_axis=0, concat_axis=0, tiled=True)
-    text_out = jnp.sum(
-        blocks.astype(F32).reshape((LATENTS, ranks) + blocks.shape[1:]), axis=1
-    )
     return (mixed, grad, jnp.stack(skip_store), text_out) + tuple(gains) + weight_outs
 
 
@@ -1322,10 +1427,11 @@
     NUMBERS.clear()
     rows, columns = mesh.shape["row"], mesh.shape["col"]
     grid = Mesh(
-        mesh.devices.reshape(rows, LATENTS, columns // LATENTS), ("row", "lat", "tp")
+        mesh.devices.reshape(rows, LATENTS, columns // (2 * LATENTS), 2),
+        ("row", "lat", "chip", "core"),
     )
-    col = ("lat", "tp")
-    tokens = ("row", "lat", "tp")
+    col = ("lat", "chip", "core")
+    tokens = ("row", "lat", "chip", "core")
     return jax.shard_map(
         on_device,
         mesh=grid,

time: 1540 us -> 1490 us (0.968)
  matrix products: 216 us -> 147 us
  waiting for transfers between devices: 0.41 us -> 17.1 us
    pallas_call x1, Pallas kernels: 111 us -> 38.5 us  [end_call(): pl.pallas_call(functools.partial(end_kernel, modes), out_shape=[jax.Shape...]
    dot_general x56 -> x40, matrix products: 216 us -> 147 us  [dot(): lax.dot_general(left, right, (((left_dim,), (right_dim,)), ((), ())), pre...]
    pallas_call x16, Pallas kernels: 809 us -> 866 us  [token_call(): pl.pallas_call(functools.partial(token_kernel, sums, spreads, body, len(i...]
    slice x2 -> x6, local copies, waits for them, and re-layouts: 0.01 us -> 15.6 us  [the longest x2 8.02 us: on_device(): query, keys, values = thirds(dot(weight[:, :3 * wide], first_all, 0, 1), 3)]
    unnamed x585 -> x548, local copies, waits for them, and re-layouts: 79.1 us -> 82.2 us
  transfers between devices with their start and end apart: 17 -> 18, of which waited for: 0 -> 2; matrix products, arithmetic and copies ran while one was open for 21% -> 17% of each run, Pallas kernels for 62% -> 53%
where the time goes in v3:
time: 1490 us; the launch traced here: 1480 us
  Pallas kernels  1060 us (71%)
  local copies, waits for them, and re-layouts  159 us (11%)
  matrix products  147 us (10%)
  other arithmetic  76.8 us (5%)
  between operations  17.7 us (1%)
  waiting for transfers between devices  17.1 us (1%)
    pallas_call x16, Pallas kernels, token_call(): pl.pallas_call(functools.partial(token_kernel, sums, spreads, body, len(i...  866 us
    dot_general x40, matrix products, dot(): lax.dot_general(left, right, (((left_dim,), (right_dim,)), ((), ())), pre...  147 us
    unnamed x548, local copies, waits for them, and re-layouts  82.2 us
    pallas_call x4, Pallas kernels, attention_back(): pl.pallas_call(functools.partial(attention_back_kernel, count, turn), gri...  49 us
    pallas_call x4, Pallas kernels, local_call(): pl.pallas_call(body, out_shape=shapes, in_specs=[pl.BlockSpec(memory_spac...  40.4 us
    pallas_call x1, Pallas kernels, end_call(): pl.pallas_call(functools.partial(end_kernel, modes), out_shape=[jax.Shape...  38.5 us
    pallas_call x1, Pallas kernels, start_call(): pl.pallas_call(functools.partial(start_kernel, modes), out_shape=[jax.Sha...  31.6 us
    pallas_call x4, Pallas kernels, attention(): pl.pallas_call(functools.partial(attention_kernel, count, turn), grid=(he...  30.8 us
  transfers between devices with their start and end apart: 18, of which 2 were waited for; matrix products, arithmetic and copies ran while one was open for 17% of the time, Pallas kernels for 53%

profile of v3, /device:TPU:0, one launch (start us, length us, event | category | flops | bytes accessed | tf_op | source)
XLA Modules:
  0.0 1482.3 jit_solution(18113491692845698563)
XLA Ops:
  11.3 31.6 %shift.1 = (f32[4,8,384]{2,1,0:T(8,128)S(1)}, f32[8,8,256]{2,1,0:T(8,128)S(1)}, bf16[352,704]{1,0:T(8,128)(2,1)S(1)}) custom-call(f32[4,8,384]{2,1,0:T(8,128)S(1)} %fusion.62.refs_0_, bf16[2,384,256]{2,1,0:T(8,128)(2,1)S(1)} %pad.20.refs_1_, bf16[352,704]{1,0:T(8,128)(2,1)S(1)} %pad_maximum_fusion.13.refs_2_), custom_call_target="tpu_custom_call" | custom-call | tf_op jit(solution)/shard_map/shift/pallas_call | solution.py:738
  52.8 94.6 %spread.2 = (bf16[4,256,1408]{2,1,0:T(8,128)(2,1)}, bf16[352,352]{1,0:T(8,128)(2,1)S(1)}, bf16[256,352]{1,0:T(8,128)(2,1)S(1)}, bf16[2,352,768]{2,1,0:T(8,128)(2,1)S(1)}, bf16[4,8,176,704]{3,2,1,0:T(8,128)(2,1)}) custom-call(f32[256,1408]{1,0:T(8,128)S(1)} %convert_element_type.483.refs_0_.refs_4_, bf16[352,352]{1,0:T(8,128)(2,1)S(1)} %pad_maximum_fusion.21.refs_1_, ...), custom_call_target="tpu_custom_call" | custom-call | flops 7208960 | bytes 4325376 | tf_op jit(solution)/shard_map/spread/pallas_call | solution.py:650
  148.5 7.0 skip.2
  157.9 44.0 %first.2 = (bf16[4,256,1408]{2,1,0:T(8,128)(2,1)}, bf16[2,352,768]{2,1,0:T(8,128)(2,1)S(1)}, bf16[2,352,768]{2,1,0:T(8,128)(2,1)S(1)}, bf16[2,352,768]{2,1,0:T(8,128)(2,1)S(1)}) custom-call(f32[256,1408]{1,0:T(8,128)} %copy-done, f32[1,1408]{1,0:T(1,128)S(1)} %get-tuple-element.496.refs_1_.refs_4_, f32[1,1408]{1,0:T(1,128)S(1)} %slice.551.refs_2_, ...), custom_call_target="tpu_custom_call" | custom-call | flops 7208960 | bytes 4325376 | tf_op jit(solution)/shard_map/first/pallas_call | solution.py:650
  211.0 6.9 fusion.91
  218.6 9.8 shard_map.288
  239.3 60.3 %middle.4 = (f32[256,1408]{1,0:T(8,128)}, bf16[4,256,1408]{2,1,0:T(8,128)(2,1)}, bf16[2,2,352,768]{3,2,1,0:T(8,128)(2,1)}, bf16[2,2,352,768]{3,2,1,0:T(8,128)(2,...) custom-call(bf16[352,1024]{1,0:T(8,128)(2,1)S(1)} %copy-done.110, ...), custom_call_target="tpu_custom_call" | custom-call | flops 7208960 | bytes 4325376 | tf_op jit(solution)/shard_map/middle/pallas_call | solution.py:650
  320.1 5.4 shard_map.289
  326.1 75.6 %middle.5 = (f32[256,1408]{1,0:T(8,128)}, bf16[4,256,1408]{2,1,0:T(8,128)(2,1)}, bf16[2,2,352,768]{3,2,1,0:T(8,128)(2,1)}, bf16[2,2,352,768]{3,2,1,0:T(8,128)(2,1)}, bf16[2,352,768]{2,1,0:T(8,128)(2,1)S(1)}) custom-call(bf16[352,1024]{1,0:T(8,128)(2,1)S(1)} %get-tuple-element.167.refs_0_, bf16[1408,352]{1,0:T(8,128)(2,1)S(1)} %get-tuple-element.381.refs_1_, ...), custom_call_target="tpu_custom_call" | custom-call | flops 7208960 | bytes 4325376 | tf_op jit(solution)/shard_map/middle/pallas_call | solution.py:650
  401.7 7.0 multiply_convert_fusion.2
  408.8 4.6 multiply_convert_fusion.3
  413.3 39.5 %last.2 = (f32[256,1408]{1,0:T(8,128)}, bf16[2,352,768]{2,1,0:T(8,128)(2,1)S(1)}, bf16[2,352,768]{2,1,0:T(8,128)(2,1)S(1)}, bf16[2,352,768]{2,1,0:T(8,128)(2,1)S(1)}) custom-call(bf16[1024,768]{1,0:T(8,128)(2,1)} %get-tuple-element.506.refs_0_, bf16[1024,768]{1,0:T(8,128)(2,1)} %get-tuple-element.508.refs_1_, bf16[1408,768]{1,0:T(8,128)(2,1)} %bitcast.424, ...), custom_call_target="tpu_custom_call" | custom-call | flops 7208960 | bytes 4325376 | tf_op jit(solution)/shard_map/last/pallas_call | solution.py:650
  458.3 6.8 skip.3
  466.2 30.3 %first.3 = (bf16[4,256,1408]{2,1,0:T(8,128)(2,1)S(1)}, bf16[352,352]{1,0:T(8,128)(2,1)S(1)}, bf16[256,352]{1,0:T(8,128)(2,1)S(1)}) custom-call(f32[256,1408]{1,0:T(8,128)S(1)} %get-tuple-element.180.refs_0_.refs_2_.refs_3_, f32[1,1408]{1,0:T(1,128)S(1)} %get-tuple-element.497.refs_1_.refs_4_, f32[1,1408]{1,0:T(1,128)S(1)} %copy-done.146, ...), custom_call_target="tpu_custom_call" | custom-call | flops 7208960 | bytes 4325376 | tf_op jit(solution)/shard_map/first/pallas_call | solution.py:650
  504.7 7.0 fusion.89
  512.6 10.2 shard_map.290
  522.9 57.8 %middle.6 = (f32[256,1408]{1,0:T(8,128)}, bf16[4,256,1408]{2,1,0:T(8,128)(2,1)}, bf16[2,2,352,768]{3,2,1,0:T(8,128)(2,1)}, bf16[2,2,352,768]{3,2,1,0:T(8,128)(2,...) custom-call(bf16[352,1024]{1,0:T(8,128)(2,1)S(1)} %get-tuple-element.184.refs_0_, ...), custom_call_target="tpu_custom_call" | custom-call | flops 7208960 | bytes 4325376 | tf_op jit(solution)/shard_map/middle/pallas_call | solution.py:650
  586.2 3.9 fusion.83.query_ref
  590.2 5.4 shard_map.291
  597.4 40.7 %middle.7 = (f32[256,1408]{1,0:T(8,128)S(1)}, bf16[4,256,1408]{2,1,0:T(8,128)(2,1)}, bf16[2,2,352,768]{3,2,1,0:T(8,128)(2,1)}, bf16[2,2,352,768]{3,2,1,0:T(8,128)(2,1)}) custom-call(bf16[352,1024]{1,0:T(8,128)(2,1)S(1)} %get-tuple-element.190.refs_0_, bf16[1408,352]{1,0:T(8,128)(2,1)S(1)} %get-tuple-element.383.refs_1_, ...), custom_call_target="tpu_custom_call" | custom-call | flops 7208960 | bytes 4325376 | tf_op jit(solution)/shard_map/middle/pallas_call | solution.py:650
  638.2 6.6 multiply_convert_fusion
  644.9 4.0 fusion.19.refs_1_
  648.8 3.9 convolution_convert_fusion.8
  652.7 4.2 multiply_convert_fusion.1
  656.9 4.1 fusion.13.refs_0_
  661.0 3.9 convolution_convert_fusion.9
  664.9 45.5 %back.4 = (f32[256,1408]{1,0:T(8,128)S(1)}, f32[1,1408]{1,0:T(1,128)S(1)}, bf16[4,256,1408]{2,1,0:T(8,128)(2,1)}, bf16[1,2,352,768]{3,2,1,0:T(8,128)(2,1)S(1)}, bf16[1,2,352,768]{3,2,1,0:T(8,128)(2,1)S(1)}) custom-call(bf16[1024,768]{1,0:T(8,128)(2,1)} %copy-done.203, bf16[1024,768]{1,0:T(8,128)(2,1)} %copy-done.202, bf16[1408,768]{1,0:T(8,128)(2,1)} %bitcast.420, ...), custom_call_target="tpu_custom_call" | custom-call | flops 7208960 | bytes 4325376 | tf_op jit(solution)/shard_map/back/pallas_call | solution.py:650
  711.4 4.6 convolution_convert_fusion.21.grad_ref
  716.1 7.9 shard_map.292
  736.9 6.3 convolution_convert_fusion.6
  748.4 5.9 convolution_convert_fusion.7
  754.4 62.8 %back.5 = (f32[256,1408]{1,0:T(8,128)}, f32[1,1408]{1,0:T(1,128)S(1)}, bf16[4,256,1408]{2,1,0:T(8,128)(2,1)}, bf16[1,352,768]{2,1,0:T(8,128)(2,1)S(1)}, bf16[1,3...) custom-call(bf16[352,1024]{1,0:T(8,128)(2,1)S(1)} %copy-done.113, ...), custom_call_target="tpu_custom_call" | custom-call | flops 7208960 | bytes 4325376 | tf_op jit(solution)/shard_map/back/pallas_call | solution.py:650
  819.2 4.5 convolution_convert_fusion.20.grad_ref
  823.7 16.8 %shard_map.293 = (bf16[352,1024]{1,0:T(8,128)(2,1)S(1)}, bf16[352,1024]{1,0:T(8,128)(2,1)S(1)}, bf16[352,1024]{1,0:T(8,128)(2,1)S(1)}) custom-call(f32[352,1024]{1,0:T(8,128)S(1)} %copy-done.68, f32[352,1024]{1,0:T(8,128)} %copy-done.66, f32[352,1024]{1,0:T(8,128)} %copy-done.65, f32[4,1,1024]{2,1,0:T(1,128)S(1)} %get-tuple-element.202.logsum_ref, ...), custom_call_target="tpu_custom_call" | custom-call | flops 3690987520 | bytes 5767168 | tf_op jit(solution)/shard_map/pallas_call | solution.py:208
  846.6 4.0 convolution_convert_fusion.1
  850.6 3.7 fusion.96
  854.3 8.5 concatenate.93
  863.3 4.0 slice.734.refs_1_
  870.1 39.2 %back_last.2 = (f32[256,1408]{1,0:T(8,128)S(1)}, f32[1,1408]{1,0:T(1,128)S(1)}, f32[1,1408]{1,0:T(1,128)S(1)}, bf16[1,352,768]{2,1,0:T(8,128)(2,1)S(1)}, bf16[1,...) custom-call(bf16[1056,1024]{1,0:T(8,128)(2,1)} %copy-done.175, bf16[1408,1056]{1,0:T(8,128)(2,1)} %slice.734.refs_1_, ...), custom_call_target="tpu_custom_call" | custom-call | flops 7208960 | bytes 4325376 | tf_op jit(solution)/shard_map/back_last/pallas_call | solution.py:650
  911.1 13.4 skip_back.2
  928.6 32.1 %spread.3 = (bf16[4,256,1408]{2,1,0:T(8,128)(2,1)S(1)}, bf16[352,768]{1,0:T(8,128)(2,1)S(1)}) custom-call(f32[256,1408]{1,0:T(8,128)S(1)} %copy-done.13, bf16[352,768]{1,0:T(8,128)(2,1)S(1)} %fusion.48.refs_1_), custom_call_target="tpu_custom_call" | custom-call | flops 7208960 | bytes 4325376 | tf_op jit(solution)/shard_map/spread/pallas_call | solution.py:650
  960.8 3.9 convolution_convert_fusion.2
  965.3 3.9 fusion.31.refs_1_
  969.2 3.8 convolution_convert_fusion.4
  973.1 4.1 fusion.25.refs_0_
  978.4 3.8 convolution_convert_fusion.5
  987.3 79.6 %back.6 = (f32[256,1408]{1,0:T(8,128)}, f32[1,1408]{1,0:T(1,128)S(1)}, bf16[4,256,1408]{2,1,0:T(8,128)(2,1)}, bf16[1,2,352,768]{3,2,1,0:T(8,128)(2,1)S(1)}, bf16...) custom-call(bf16[1024,768]{1,0:T(8,128)(2,1)} %copy-done.201, ...), custom_call_target="tpu_custom_call" | custom-call | flops 7208960 | bytes 4325376 | tf_op jit(solution)/shard_map/back/pallas_call | solution.py:650
  1067.9 4.3 convolution_convert_fusion.19.grad_ref
  1072.3 7.9 shard_map.294
  1085.1 6.2 convolution_convert_fusion.3
  1104.7 58.7 %back.7 = (f32[256,1408]{1,0:T(8,128)}, f32[1,1408]{1,0:T(1,128)S(1)}, bf16[4,256,1408]{2,1,0:T(8,128)(2,1)}, bf16[1,352,768]{2,1,0:T(8,128)(2,1)S(1)}, bf16[1,3...) custom-call(bf16[352,1024]{1,0:T(8,128)(2,1)S(1)} %copy-done.108, ...), custom_call_target="tpu_custom_call" | custom-call | flops 7208960 | bytes 4325376 | tf_op jit(solution)/shard_map/back/pallas_call | solution.py:650
  1164.4 5.0 convolution_convert_fusion.18.grad_ref
  1169.4 16.5 %shard_map.295 = (bf16[352,1024]{1,0:T(8,128)(2,1)S(1)}, bf16[352,1024]{1,0:T(8,128)(2,1)S(1)}, bf16[352,1024]{1,0:T(8,128)(2,1)S(1)}) custom-call(f32[352,1024]{1,0:T(8,128)S(1)} %copy-done.61, f32[352,1024]{1,0:T(8,128)} %copy-done.59, f32[352,1024]{1,0:T(8,128)} %copy-done.58, f32[4,1,1024]{2,1,0:T(1,128)S(1)} %copy-done.154, ...), custom_call_target="tpu_custom_call" | custom-call | flops 3690987520 | bytes 5767168 | tf_op jit(solution)/shard_map/pallas_call | solution.py:208
  1191.7 4.0 convolution_convert_fusion
  1195.8 4.0 fusion.95
  1199.7 8.8 concatenate.104
  1214.3 4.6 all-to-all-start
  1220.2 4.0 slice.708.refs_1_
  1229.4 8.5 all-to-all-done
  1241.3 56.2 %back_last.3 = (f32[256,1408]{1,0:T(8,128)}, f32[1,1408]{1,0:T(1,128)S(1)}, f32[1,1408]{1,0:T(1,128)S(1)}, bf16[1,352,768]{2,1,0:T(8,128)(2,1)S(1)}, bf16[1,352,...) custom-call(bf16[1056,1024]{1,0:T(8,128)(2,1)} %copy-done.174, ...), custom_call_target="tpu_custom_call" | custom-call | flops 7208960 | bytes 4325376 | tf_op jit(solution)/shard_map/back_last/pallas_call | solution.py:650
  1302.7 13.3 skip_back.3
  1346.0 38.5 %gains.1 = (f32[4,2,136,128]{3,2,1,0:T(8,128)S(1)}, bf16[352,768]{1,0:T(8,128)(2,1)S(1)}) custom-call(f32[136,128]{1,0:T(8,128)S(1)} %pad_bitcast_fusion.refs_0_, bf16[352,768]{1,0:T(8,128)(2,1)S(1)} %fusion.50.refs_1_), custom_call_target="tpu_custom_call" | custom-call | tf_op jit(solution)/shard_map/gains/pallas_call | solution.py:812
  1401.0 48.9 %last.3 = (f32[256,1408]{1,0:T(8,128)S(1)}, bf16[1,2,176,704]{3,2,1,0:T(8,128)(2,1)S(1)}, bf16[352,704]{1,0:T(8,128)(2,1)S(1)}) custom-call(bf16[1024,768]{1,0:T(8,128)(2,1)} %get-tuple-element.510.refs_0_, bf16[1024,768]{1,0:T(8,128)(2,1)} %get-tuple-element.512.refs_1_, bf16[1408,768]{1,0:T(8,128)(2,1)} %bitcast.412, bf16[1408,768]{1,0:T(8,128)(2,1)} %bitcast.414, ...), custom_call_target="tpu_custom_call" | custom-call | flops 7208960 | bytes 4325376 | tf_op jit(solution)/shard_map/last/pallas_call | solution.py:650
  1463.1 8.1 collective-permute-done
  (777 shorter events, 233.9 us)
Async XLA Ops:
  7.2 203.8 %all-gather.13.cloned.1.call-start = ((), (), s32[]{:S(2)}) async-start(), calls=%async_computation.10 | async-start | bytes 4956160 | tf_op jit(solution)/shard_map/all_gather | solution.py:1071
  46.4 261.7 %all-gather.23.cloned.1.call-start = ((), (), s32[]{:S(2)}) async-start(), calls=%async_computation.21 | async-start | bytes 1548288 | tf_op jit(solution)/shard_map/all_gather | solution.py:1112
  50.8 97.7 %copy-start.1 = (f32[256,1408]{1,0:T(8,128)}, f32[256,1408]{1,0:T(8,128)S(1)}, u32[]{:S(2)}) copy-start(f32[256,1408]{1,0:T(8,128)S(1)} %convert_element_type.484.resid_ref) | copy-start | bytes 4325380
  52.0 95.5 %copy-start.205 = (bf16[2,256,1408]{2,1,0:T(8,128)(2,1)S(1)}, bf16[2,256,1408]{2,1,0:T(8,128)(2,1)}, u32[]{:S(2)}) copy-start(bf16[2,256,1408]{2,1,0:T(8,128)(2,1)} %param.18) | copy-start | bytes 4325380
  52.8 95.6 %copy-start.236 = (f32[2,2816]{1,0:T(2,128)S(1)}, f32[2,2816]{1,0:T(2,128)}, u32[]{:S(2)}) copy-start(f32[2,2816]{1,0:T(2,128)} %param.21) | copy-start | bytes 67588
  148.5 8.1 copy-start.216
  157.6 46.3 %copy-start.230 = (bf16[2,333,128]{2,0,1:T(2,128)(2,1)S(1)}, bf16[2,333,128]{2,0,1:T(2,128)(2,1)}, u32[]{:S(2)}) copy-start(bf16[2,333,128]{2,0,1:T(2,128)(2,1)} %param.20) | copy-start | bytes 511492
  157.6 44.3 %copy-start.141 = (f32[1,1408]{1,0:T(1,128)}, f32[1,1408]{1,0:T(1,128)S(1)}, u32[]{:S(2)}) copy-start(f32[1,1408]{1,0:T(1,128)S(1)} %get-tuple-element.496.refs_1_.refs_4_) | copy-start | bytes 16900
  157.6 81.6 %copy-start.143 = (f32[1,1408]{1,0:T(1,128)}, f32[1,1408]{1,0:T(1,128)S(1)}, u32[]{:S(2)}) copy-start(f32[1,1408]{1,0:T(1,128)S(1)} %get-tuple-element.495.refs_3_.refs_4_) | copy-start | bytes 16900
  204.6 105.9 %all-gather.15.cloned.1.call-start = ((), (), s32[]{:S(2)}) async-start(), calls=%async_computation.11 | async-start | bytes 1966080 | tf_op jit(solution)/shard_map/all_gather | solution.py:1071
  206.8 106.3 %all-gather.11.cloned.1.call-start = ((), (), s32[]{:S(2)}) async-start(), calls=%async_computation.9 | async-start | bytes 2703360 | tf_op jit(solution)/shard_map/all_gather | solution.py:1071
  209.3 246.6 %all-gather.25.cloned.1.call-start = ((), (), s32[]{:S(2)}) async-start(), calls=%async_computation.22 | async-start | bytes 8921088 | tf_op jit(solution)/shard_map/all_gather | solution.py:1159
  211.0 109.1 %copy-start.19 = (f32[88,1024]{1,0:T(8,128)}, f32[88,1024]{1,0:T(8,128)S(1)}, u32[]{:S(2)}) copy-start(f32[88,1024]{1,0:T(8,128)S(1)} %get-tuple-element.505.cos_ref) | copy-start | bytes 1081348
  211.0 612.7 %copy-start.17 = (f32[88,1024]{1,0:T(8,128)}, f32[88,1024]{1,0:T(8,128)S(1)}, u32[]{:S(2)}) copy-start(f32[88,1024]{1,0:T(8,128)S(1)} %get-tuple-element.504.sin_ref) | copy-start | bytes 1081348
  218.5 9.9 copy-start.58
  218.5 9.9 copy-start.59
  218.5 9.9 copy-start.60
  229.3 9.9 copy-start.153
  229.3 273.6 %all-gather.19.cloned.1.call-start = ((), (), s32[]{:S(2)}) async-start(), calls=%async_computation.13 | async-start | bytes 4956160 | tf_op jit(solution)/shard_map/all_gather | solution.py:1071
  239.2 60.4 %copy-start.193 = (bf16[1,1,352,176]{3,2,1,0:T(8,128)(2,1)S(1)}, bf16[1,1,352,176]{3,2,1,0:T(8,128)(2,1)}, u32[]{:S(2)}) copy-start(bf16[1,1,352,176]{3,2,1,0:T(8,128)(2,1)} %copy.257) | copy-start | bytes 371716
  239.2 60.4 %copy-start.194 = (bf16[1,1,352,176]{3,2,1,0:T(8,128)(2,1)S(1)}, bf16[1,1,352,176]{3,2,1,0:T(8,128)(2,1)}, u32[]{:S(2)}) copy-start(bf16[1,1,352,176]{3,2,1,0:T(8,128)(2,1)} %copy.258) | copy-start | bytes 371716
  239.2 60.4 %copy-start.195 = (bf16[1,176,352]{1,2,0:T(8,128)(2,1)S(1)}, bf16[1,176,352]{1,2,0:T(8,128)(2,1)}, u32[]{:S(2)}) copy-start(bf16[1,176,352]{1,2,0:T(8,128)(2,1)} %copy.259) | copy-start | bytes 371716
  305.3 278.2 %all-gather.21.cloned.1.call-start = ((), (), s32[]{:S(2)}) async-start(), calls=%async_computation.14 | async-start | bytes 1966080 | tf_op jit(solution)/shard_map/all_gather | solution.py:1071
  326.1 75.6 %copy-start.100 = (bf16[352,1024]{1,0:T(8,128)(2,1)}, bf16[352,1024]{1,0:T(8,128)(2,1)S(1)}, u32[]{:S(2)}) copy-start(bf16[352,1024]{1,0:T(8,128)(2,1)S(1)} %get-tuple-element.167.refs_0_) | copy-start | bytes 2162692
  326.1 75.6 %copy-start.181 = (bf16[2,2,352,768]{3,2,1,0:T(8,128)(2,1)S(1)}, bf16[2,2,352,768]{3,2,1,0:T(8,128)(2,1)}, u32[]{:S(2)}) copy-start(bf16[2,2,352,768]{3,2,1,0:T(8,128)(2,1)} %get-tuple-element.173) | copy-start | bytes 6488068
  458.3 7.9 copy-start.99
  458.3 7.9 copy-start.146
  458.3 40.5 %copy-start.211 = (bf16[1,1,256,176]{3,2,1,0:T(8,128)(2,1)S(1)}, bf16[1,1,256,176]{3,2,1,0:T(8,128)(2,1)}, u32[]{:S(2)}) copy-start(bf16[1,1,256,176]{3,2,1,0:T(8,128)(2,1)} %copy-done.210) | copy-start | bytes 270340
  458.3 40.5 %copy-start.213 = (bf16[1,1,256,176]{3,2,1,0:T(8,128)(2,1)S(1)}, bf16[1,1,256,176]{3,2,1,0:T(8,128)(2,1)}, u32[]{:S(2)}) copy-start(bf16[1,1,256,176]{3,2,1,0:T(8,128)(2,1)} %copy-done.212) | copy-start | bytes 270340
  466.2 34.0 %copy-start.2 = (f32[256,1408]{1,0:T(8,128)}, f32[256,1408]{1,0:T(8,128)S(1)}, u32[]{:S(2)}) copy-start(f32[256,1408]{1,0:T(8,128)S(1)} %get-tuple-element.180.refs_0_.refs_2_.refs_3_) | copy-start | bytes 4325380
  500.2 86.0 %all-gather.17.cloned.1.call-start = ((), (), s32[]{:S(2)}) async-start(), calls=%async_computation.12 | async-start | bytes 2703360 | tf_op jit(solution)/shard_map/all_gather | solution.py:1071
  502.8 479.3 %reduce-scatter.17.cloned.1.call-start = ((), (), s32[]{:S(2)}) async-start(), calls=%async_computation.17 | async-start | bytes 1966080 | tf_op jit(solution)/shard_map/reduce_scatter | solution.py:1219
  512.0 10.8 copy-start.65
  512.0 10.8 copy-start.66
  512.0 10.8 copy-start.67
  512.6 10.2 copy-start.96
  512.6 10.2 copy-start.98
  597.4 40.8 %copy-start.183 = (bf16[2,2,352,768]{3,2,1,0:T(8,128)(2,1)S(1)}, bf16[2,2,352,768]{3,2,1,0:T(8,128)(2,1)}, u32[]{:S(2)}) copy-start(bf16[2,2,352,768]{3,2,1,0:T(8,128)(2,1)} %get-tuple-element.196) | copy-start | bytes 6488068
  664.9 46.5 %copy-start.188 = (bf16[1408,704]{1,0:T(8,128)(2,1)S(1)}, bf16[1408,704]{1,0:T(8,128)(2,1)}, u32[]{:S(2)}) copy-start(bf16[1408,704]{1,0:T(8,128)(2,1)} %all-gather.17.cloned.1.call-done) | copy-start | bytes 5947396
  716.1 8.0 copy-start.218
  728.0 255.3 %reduce-scatter.15.cloned.1.call-start = ((), (), s32[]{:S(2)}) async-start(), calls=%async_computation.16 | async-start | bytes 2703360 | tf_op jit(solution)/shard_map/reduce_scatter | solution.py:1219
  743.2 241.4 %reduce-scatter.13.cloned.1.call-start = ((), (), s32[]{:S(2)}) async-start(), calls=%async_computation.15 | async-start | bytes 4956160 | tf_op jit(solution)/shard_map/reduce_scatter | solution.py:1219
  862.9 123.1 %reduce-scatter.25.cloned.1.call-start = ((), (), s32[]{:S(2)}) async-start(), calls=%async_computation.23 | async-start | bytes 5406720
  869.0 57.9 %copy-start.3 = (bf16[2,352,768]{2,1,0:T(8,128)(2,1)}, bf16[2,352,768]{2,1,0:T(8,128)(2,1)S(1)}, u32[]{:S(2)}) copy-start(bf16[2,352,768]{2,1,0:T(8,128)(2,1)S(1)} %fusion.34.refs_6_) | copy-start | bytes 3244036
  870.1 56.8 %copy-start.4 = (bf16[1,2,352,768]{3,2,1,0:T(8,128)(2,1)}, bf16[1,2,352,768]{3,2,1,0:T(8,128)(2,1)S(1)}, u32[]{:S(2)}) copy-start(bf16[1,2,352,768]{3,2,1,0:T(8,128)(2,1)S(1)} %add_convert_fusion.2) | copy-start | bytes 3244036
  870.1 41.0 %copy-start.8 = (bf16[256,1408]{1,0:T(8,128)(2,1)S(1)}, bf16[256,1408]{1,0:T(8,128)(2,1)}, u32[]{:S(2)}) copy-start(bf16[256,1408]{1,0:T(8,128)(2,1)} %get-tuple-element.392.skip_ref) | copy-start | bytes 2162692
  926.8 311.0 %reduce-scatter.21.cloned.1.call-start = ((), (), s32[]{:S(2)}) async-start(), calls=%async_computation.19 | async-start | bytes 1966080 | tf_op jit(solution)/shard_map/reduce_scatter | solution.py:1219
  926.9 33.8 %copy-start.204 = (bf16[1024,768]{1,0:T(8,128)(2,1)S(1)}, bf16[1024,768]{1,0:T(8,128)(2,1)}, u32[]{:S(2)}) copy-start(bf16[1024,768]{1,0:T(8,128)(2,1)} %get-tuple-element.508.refs_1_) | copy-start | bytes 4718596
  960.7 12.3 copy-start.150
  987.3 80.6 %copy-start.186 = (bf16[1408,704]{1,0:T(8,128)(2,1)S(1)}, bf16[1408,704]{1,0:T(8,128)(2,1)}, u32[]{:S(2)}) copy-start(bf16[1408,704]{1,0:T(8,128)(2,1)} %all-gather.11.cloned.1.call-done) | copy-start | bytes 5947396
  1072.3 8.9 copy-start.219
  1085.1 154.0 %reduce-scatter.19.cloned.1.call-start = ((), (), s32[]{:S(2)}) async-start(), calls=%async_computation.18 | async-start | bytes 2703360 | tf_op jit(solution)/shard_map/reduce_scatter | solution.py:1219
  1099.8 298.3 %reduce-scatter.23.cloned.1.call-start = ((), (), s32[]{:S(2)}) async-start(), calls=%async_computation.20 | async-start | bytes 4956160 | tf_op jit(solution)/shard_map/reduce_scatter | solution.py:1219
  1164.3 60.0 %copy-start.45 = (bf16[1,352,768]{2,1,0:T(8,128)(2,1)}, bf16[1,352,768]{2,1,0:T(8,128)(2,1)S(1)}, u32[]{:S(2)}) copy-start(bf16[1,352,768]{2,1,0:T(8,128)(2,1)S(1)} %get-tuple-element.245) | copy-start | bytes 1622020
  1164.3 60.0 %copy-start.47 = (bf16[1,352,768]{2,1,0:T(8,128)(2,1)}, bf16[1,352,768]{2,1,0:T(8,128)(2,1)S(1)}, u32[]{:S(2)}) copy-start(bf16[1,352,768]{2,1,0:T(8,128)(2,1)S(1)} %get-tuple-element.244) | copy-start | bytes 1622020
  1214.3 23.6 %all-to-all-start = ((bf16[8,333,128]{2,1,0:T(8,128)(2,1)}), bf16[8,333,128]{2,1,0:T(8,128)(2,1)}, u32[]{:S(2)}, u32[]{:S(2)}) async-start(bf16[8,333,128]{2,1,0:T(8,128)(2,1)} %bitcast.366), calls=%async_computation.3 | async-start | bytes 1376256 | tf_op jit(solution)/shard_map/all_to_all | solution.py:1336
  1218.9 180.8 %reduce-scatter.27.cloned.1.call-start = ((), (), s32[]{:S(2)}) async-start(), calls=%async_computation.24 | async-start | bytes 5406720
  1229.1 11.2 copy-start.142
  1241.3 60.0 %copy-start.6 = (bf16[256,1408]{1,0:T(8,128)(2,1)S(1)}, bf16[256,1408]{1,0:T(8,128)(2,1)}, u32[]{:S(2)}) copy-start(bf16[256,1408]{1,0:T(8,128)(2,1)} %copy-done.5) | copy-start | bytes 2162692
  1241.3 60.0 %copy-start.140 = (f32[1,2816]{1,0:T(1,128)S(1)}, f32[1,2816]{1,0:T(1,128)}, u32[]{:S(2)}) copy-start(f32[1,2816]{1,0:T(1,128)} %copy-done.139) | copy-start | bytes 33796
  1401.0 48.9 %copy-start.170 = (bf16[352,1408]{1,0:T(8,128)(2,1)S(1)}, bf16[352,1408]{1,0:T(8,128)(2,1)}, u32[]{:S(2)}) copy-start(bf16[352,1408]{1,0:T(8,128)(2,1)} %reduce-scatter.23.cloned.1.call-done) | copy-start | bytes 2973700
  1456.6 14.6 collective-permute-start
  1460.1 11.1 copy-start.162
  1460.1 12.1 copy-start.191
  (207 other events, 609.6 us)
Sparse Core Ops, SparseCore 0:
  46.5 50.7 all-gather.12
  204.7 22.7 all-gather.22
  230.0 38.7 all-gather.14
  271.0 41.7 all-gather.10
  316.3 99.9 all-gather.24
  418.0 56.9 all-gather.18
  500.3 29.5 all-gather.20
  532.3 50.3 all-gather.16
  728.1 29.2 reduce-scatter.16
  760.2 53.3 reduce-scatter.14
  863.0 58.9 reduce-scatter.12
  927.0 53.1 reduce-scatter.24
  1085.2 31.2 reduce-scatter.20
  1120.0 48.8 reduce-scatter.18
  1208.7 56.6 reduce-scatter.22
  1318.3 52.0 reduce-scatter.26

commit v4 on v3

--- a/solution.py
+++ b/solution.py
@@ -88,7 +88,8 @@
     )
 
 
-QUERY_CHUNK = 512
+QUERY_CHUNK = 1024
+BACK_CHUNK = 512
 
 
 def attention_kernel(
@@ -144,8 +145,8 @@
     grad_t = grad.T
     query_t = query_low.T
     query_grad = []
-    for start in range(0, query_low.shape[1], QUERY_CHUNK):
-        span = slice(start, start + QUERY_CHUNK)
+    for start in range(0, query_low.shape[1], BACK_CHUNK):
+        span = slice(start, start + BACK_CHUNK)
         scores = jnp.dot(keys_t, query_low[:, span], preferred_element_type=F32)
         probs = jnp.exp(scores * SCALE - logsum_ref[0, :, span])
         if count < keys_t.shape[0]:
@@ -1138,10 +1139,7 @@
         )
         if layer == 0:
             up_half, down_stack = others[:2], others[2]
-            text, cross_other, text_other, first_all = lax.optimization_barrier(
-                (text, cross_other, text_other, first_all)
-            )
-            text_own = own_text(text)
+            text_own = own_text(lax.optimization_barrier((text, cross_other))[0])
         else:
             cross_other, text_other = others
         cross_full.append(gather_both(cross_pack[layer], cross_other, [local] * 2))

time: 1490 us -> 1480 us (level)
  Pallas kernels: 1060 us -> 1040 us
    unnamed x548 -> x556, local copies, waits for them, and re-layouts: 82.2 us -> 87.1 us
  transfers between devices with their start and end apart: 18 -> 18, of which waited for: 2 -> 2; matrix products, arithmetic and copies ran while one was open for 17% -> 18% of each run, Pallas kernels for 53% -> 52%
where the time goes in v4:
time: 1480 us; the launch traced here: 1470 us
  Pallas kernels  1040 us (70%)
  local copies, waits for them, and re-layouts  166 us (11%)
  matrix products  146 us (10%)
  other arithmetic  79.3 us (5%)
  between operations  17.7 us (1%)
    pallas_call x16, Pallas kernels, token_call(): pl.pallas_call(functools.partial(token_kernel, sums, spreads, body, len(i...  852 us
    dot_general x40, matrix products, dot(): lax.dot_general(left, right, (((left_dim,), (right_dim,)), ((), ())), pre...  146 us
    unnamed x556, local copies, waits for them, and re-layouts  87.1 us
    pallas_call x4, Pallas kernels, attention_back(): pl.pallas_call(functools.partial(attention_back_kernel, count, turn), gri...  48.7 us
    pallas_call x4, Pallas kernels, local_call(): pl.pallas_call(body, out_shape=shapes, in_specs=[pl.BlockSpec(memory_spac...  40.6 us
    pallas_call x1, Pallas kernels, end_call(): pl.pallas_call(functools.partial(end_kernel, modes), out_shape=[jax.Shape...  38.7 us
    pallas_call x1, Pallas kernels, start_call(): pl.pallas_call(functools.partial(start_kernel, modes), out_shape=[jax.Sha...  31.6 us
  transfers between devices with their start and end apart: 18, of which 2 were waited for; matrix products, arithmetic and copies ran while one was open for 18% of the time, Pallas kernels for 52%

profile of v4, /device:TPU:0, one launch (start us, length us, event | category | flops | bytes accessed | tf_op | source)
XLA Modules:
  0.0 1470.3 jit_solution(18156621780441340594)
XLA Ops:
  11.2 31.6 %shift.1 = (f32[4,8,384]{2,1,0:T(8,128)S(1)}, f32[8,8,256]{2,1,0:T(8,128)S(1)}, bf16[352,704]{1,0:T(8,128)(2,1)S(1)}) custom-call(f32[4,8,384]{2,1,0:T(8,128)S(1)} %fusion.62.refs_0_, bf16[2,384,256]{2,1,0:T(8,128)(2,1)S(1)} %pad.20.refs_1_, bf16[352,704]{1,0:T(8,128)(2,1)S(1)} %pad_maximum_fusion.14.refs_2_), custom_call_target="tpu_custom_call" | custom-call | tf_op jit(solution)/shard_map/shift/pallas_call | solution.py:739
  53.2 94.6 %spread.2 = (bf16[4,256,1408]{2,1,0:T(8,128)(2,1)}, bf16[352,352]{1,0:T(8,128)(2,1)S(1)}, bf16[256,352]{1,0:T(8,128)(2,1)S(1)}, bf16[2,352,768]{2,1,0:T(8,128)(2,1)S(1)}, bf16[4,8,176,704]{3,2,1,0:T(8,128)(2,1)}) custom-call(f32[256,1408]{1,0:T(8,128)S(1)} %convert_element_type.483.refs_0_.refs_4_, bf16[352,352]{1,0:T(8,128)(2,1)S(1)} %pad_maximum_fusion.21.refs_1_, ...), custom_call_target="tpu_custom_call" | custom-call | flops 7208960 | bytes 4325376 | tf_op jit(solution)/shard_map/spread/pallas_call | solution.py:651
  156.1 7.0 skip.2
  166.3 44.1 %first.2 = (bf16[4,256,1408]{2,1,0:T(8,128)(2,1)}, bf16[2,352,768]{2,1,0:T(8,128)(2,1)S(1)}, bf16[2,352,768]{2,1,0:T(8,128)(2,1)S(1)}, bf16[2,352,768]{2,1,0:T(8,128)(2,1)S(1)}) custom-call(f32[256,1408]{1,0:T(8,128)} %copy-done, f32[1,1408]{1,0:T(1,128)S(1)} %get-tuple-element.490.refs_1_.refs_4_, f32[1,1408]{1,0:T(1,128)S(1)} %slice.566.refs_2_, ...), custom_call_target="tpu_custom_call" | custom-call | flops 7208960 | bytes 4325376 | tf_op jit(solution)/shard_map/first/pallas_call | solution.py:651
  214.8 6.9 fusion.91
  222.3 8.9 shard_map.288
  241.0 69.3 %middle.4 = (f32[256,1408]{1,0:T(8,128)}, bf16[4,256,1408]{2,1,0:T(8,128)(2,1)}, bf16[2,2,352,768]{3,2,1,0:T(8,128)(2,1)}, bf16[2,2,352,768]{3,2,1,0:T(8,128)(2,...) custom-call(bf16[352,1024]{1,0:T(8,128)(2,1)S(1)} %copy-done.112, ...), custom_call_target="tpu_custom_call" | custom-call | flops 7208960 | bytes 4325376 | tf_op jit(solution)/shard_map/middle/pallas_call | solution.py:651
  332.6 4.6 shard_map.289
  337.3 53.7 %middle.5 = (f32[256,1408]{1,0:T(8,128)}, bf16[4,256,1408]{2,1,0:T(8,128)(2,1)}, bf16[2,2,352,768]{3,2,1,0:T(8,128)(2,1)}, bf16[2,2,352,768]{3,2,1,0:T(8,128)(2,1)}, bf16[2,352,768]{2,1,0:T(8,128)(2,1)S(1)}) custom-call(bf16[352,1024]{1,0:T(8,128)(2,1)S(1)} %get-tuple-element.161.refs_0_, bf16[1408,352]{1,0:T(8,128)(2,1)S(1)} %get-tuple-element.375.refs_1_, ...), custom_call_target="tpu_custom_call" | custom-call | flops 7208960 | bytes 4325376 | tf_op jit(solution)/shard_map/middle/pallas_call | solution.py:651
  391.1 7.0 multiply_convert_fusion.2
  398.2 4.6 multiply_convert_fusion.3
  402.7 39.5 %last.2 = (f32[256,1408]{1,0:T(8,128)}, bf16[2,352,768]{2,1,0:T(8,128)(2,1)S(1)}, bf16[2,352,768]{2,1,0:T(8,128)(2,1)S(1)}, bf16[2,352,768]{2,1,0:T(8,128)(2,1)S(1)}) custom-call(bf16[1024,768]{1,0:T(8,128)(2,1)} %get-tuple-element.500.refs_0_, bf16[1024,768]{1,0:T(8,128)(2,1)} %get-tuple-element.502.refs_1_, bf16[1408,768]{1,0:T(8,128)(2,1)} %bitcast.424, ...), custom_call_target="tpu_custom_call" | custom-call | flops 7208960 | bytes 4325376 | tf_op jit(solution)/shard_map/last/pallas_call | solution.py:651
  447.7 6.8 skip.3
  455.6 30.1 %first.3 = (bf16[4,256,1408]{2,1,0:T(8,128)(2,1)S(1)}, bf16[352,352]{1,0:T(8,128)(2,1)S(1)}, bf16[256,352]{1,0:T(8,128)(2,1)S(1)}) custom-call(f32[256,1408]{1,0:T(8,128)S(1)} %get-tuple-element.174.refs_0_.refs_2_.refs_3_, f32[1,1408]{1,0:T(1,128)S(1)} %get-tuple-element.491.refs_1_.refs_4_, f32[1,1408]{1,0:T(1,128)S(1)} %copy-done.148, ...), custom_call_target="tpu_custom_call" | custom-call | flops 7208960 | bytes 4325376 | tf_op jit(solution)/shard_map/first/pallas_call | solution.py:651
  493.8 6.9 fusion.89
  501.7 9.0 shard_map.290
  510.8 56.9 %middle.6 = (f32[256,1408]{1,0:T(8,128)}, bf16[4,256,1408]{2,1,0:T(8,128)(2,1)}, bf16[2,2,352,768]{3,2,1,0:T(8,128)(2,1)}, bf16[2,2,352,768]{3,2,1,0:T(8,128)(2,...) custom-call(bf16[352,1024]{1,0:T(8,128)(2,1)S(1)} %get-tuple-element.178.refs_0_, ...), custom_call_target="tpu_custom_call" | custom-call | flops 7208960 | bytes 4325376 | tf_op jit(solution)/shard_map/middle/pallas_call | solution.py:651
  573.1 3.9 fusion.83.query_ref
  577.1 4.6 shard_map.291
  583.6 41.7 %middle.7 = (f32[256,1408]{1,0:T(8,128)S(1)}, bf16[4,256,1408]{2,1,0:T(8,128)(2,1)}, bf16[2,2,352,768]{3,2,1,0:T(8,128)(2,1)}, bf16[2,2,352,768]{3,2,1,0:T(8,128)(2,1)}) custom-call(bf16[352,1024]{1,0:T(8,128)(2,1)S(1)} %get-tuple-element.184.refs_0_, bf16[1408,352]{1,0:T(8,128)(2,1)S(1)} %get-tuple-element.377.refs_1_, ...), custom_call_target="tpu_custom_call" | custom-call | flops 7208960 | bytes 4325376 | tf_op jit(solution)/shard_map/middle/pallas_call | solution.py:651
  625.3 6.6 multiply_convert_fusion
  632.0 3.9 fusion.19.refs_1_
  635.9 3.9 convolution_convert_fusion.8
  639.8 4.2 multiply_convert_fusion.1
  644.0 4.1 fusion.13.refs_0_
  648.1 3.9 convolution_convert_fusion.9
  652.0 45.0 %back.4 = (f32[256,1408]{1,0:T(8,128)S(1)}, f32[1,1408]{1,0:T(1,128)S(1)}, bf16[4,256,1408]{2,1,0:T(8,128)(2,1)}, bf16[1,2,352,768]{3,2,1,0:T(8,128)(2,1)S(1)}, bf16[1,2,352,768]{3,2,1,0:T(8,128)(2,1)S(1)}) custom-call(bf16[1024,768]{1,0:T(8,128)(2,1)} %copy-done.204, bf16[1024,768]{1,0:T(8,128)(2,1)} %copy-done.203, bf16[1408,768]{1,0:T(8,128)(2,1)} %bitcast.420, ...), custom_call_target="tpu_custom_call" | custom-call | flops 7208960 | bytes 4325376 | tf_op jit(solution)/shard_map/back/pallas_call | solution.py:651
  698.1 4.5 convolution_convert_fusion.21.grad_ref
  702.7 7.7 shard_map.292
  723.3 6.2 convolution_convert_fusion.6
  734.9 5.7 convolution_convert_fusion.7
  740.6 62.9 %back.5 = (f32[256,1408]{1,0:T(8,128)}, f32[1,1408]{1,0:T(1,128)S(1)}, bf16[4,256,1408]{2,1,0:T(8,128)(2,1)}, bf16[1,352,768]{2,1,0:T(8,128)(2,1)S(1)}, bf16[1,3...) custom-call(bf16[352,1024]{1,0:T(8,128)(2,1)S(1)} %copy-done.115, ...), custom_call_target="tpu_custom_call" | custom-call | flops 7208960 | bytes 4325376 | tf_op jit(solution)/shard_map/back/pallas_call | solution.py:651
  803.6 5.2 convolution_convert_fusion.20.grad_ref
  808.8 16.7 %shard_map.293 = (bf16[352,1024]{1,0:T(8,128)(2,1)S(1)}, bf16[352,1024]{1,0:T(8,128)(2,1)S(1)}, bf16[352,1024]{1,0:T(8,128)(2,1)S(1)}) custom-call(f32[352,1024]{1,0:T(8,128)S(1)} %copy-done.68, f32[352,1024]{1,0:T(8,128)} %copy-done.66, f32[352,1024]{1,0:T(8,128)} %copy-done.65, f32[4,1,1024]{2,1,0:T(1,128)S(1)} %get-tuple-element.196.logsum_ref, ...), custom_call_target="tpu_custom_call" | custom-call | flops 3690987520 | bytes 5767168 | tf_op jit(solution)/shard_map/pallas_call | solution.py:209
  831.7 4.0 convolution_convert_fusion.1
  835.7 3.7 fusion.96
  839.4 8.5 concatenate.93
  848.2 4.0 slice.734.refs_1_
  855.8 38.4 %back_last.2 = (f32[256,1408]{1,0:T(8,128)S(1)}, f32[1,1408]{1,0:T(1,128)S(1)}, f32[1,1408]{1,0:T(1,128)S(1)}, bf16[1,352,768]{2,1,0:T(8,128)(2,1)S(1)}, bf16[1,...) custom-call(bf16[1056,1024]{1,0:T(8,128)(2,1)} %copy-done.177, bf16[1408,1056]{1,0:T(8,128)(2,1)} %slice.734.refs_1_, ...), custom_call_target="tpu_custom_call" | custom-call | flops 7208960 | bytes 4325376 | tf_op jit(solution)/shard_map/back_last/pallas_call | solution.py:651
  896.7 13.5 skip_back.2
  914.3 32.5 %spread.3 = (bf16[4,256,1408]{2,1,0:T(8,128)(2,1)S(1)}, bf16[352,768]{1,0:T(8,128)(2,1)S(1)}) custom-call(f32[256,1408]{1,0:T(8,128)S(1)} %copy-done.13, bf16[352,768]{1,0:T(8,128)(2,1)S(1)} %fusion.48.refs_1_), custom_call_target="tpu_custom_call" | custom-call | flops 7208960 | bytes 4325376 | tf_op jit(solution)/shard_map/spread/pallas_call | solution.py:651
  946.9 3.9 convolution_convert_fusion.2
  951.4 3.9 fusion.31.refs_1_
  955.3 3.8 convolution_convert_fusion.4
  959.2 4.1 fusion.25.refs_0_
  964.4 3.8 convolution_convert_fusion.5
  973.3 79.3 %back.6 = (f32[256,1408]{1,0:T(8,128)}, f32[1,1408]{1,0:T(1,128)S(1)}, bf16[4,256,1408]{2,1,0:T(8,128)(2,1)}, bf16[1,2,352,768]{3,2,1,0:T(8,128)(2,1)S(1)}, bf16...) custom-call(bf16[1024,768]{1,0:T(8,128)(2,1)} %copy-done.202, ...), custom_call_target="tpu_custom_call" | custom-call | flops 7208960 | bytes 4325376 | tf_op jit(solution)/shard_map/back/pallas_call | solution.py:651
  1055.9 3.9 convolution_convert_fusion.19.grad_ref
  1059.9 7.8 shard_map.294
  1072.7 6.2 convolution_convert_fusion.3
  1092.2 58.5 %back.7 = (f32[256,1408]{1,0:T(8,128)}, f32[1,1408]{1,0:T(1,128)S(1)}, bf16[4,256,1408]{2,1,0:T(8,128)(2,1)}, bf16[1,352,768]{2,1,0:T(8,128)(2,1)S(1)}, bf16[1,3...) custom-call(bf16[352,1024]{1,0:T(8,128)(2,1)S(1)} %copy-done.110, ...), custom_call_target="tpu_custom_call" | custom-call | flops 7208960 | bytes 4325376 | tf_op jit(solution)/shard_map/back/pallas_call | solution.py:651
  1151.7 5.0 convolution_convert_fusion.18.grad_ref
  1156.7 16.6 %shard_map.295 = (bf16[352,1024]{1,0:T(8,128)(2,1)S(1)}, bf16[352,1024]{1,0:T(8,128)(2,1)S(1)}, bf16[352,1024]{1,0:T(8,128)(2,1)S(1)}) custom-call(f32[352,1024]{1,0:T(8,128)S(1)} %copy-done.61, f32[352,1024]{1,0:T(8,128)} %copy-done.59, f32[352,1024]{1,0:T(8,128)} %copy-done.58, f32[4,1,1024]{2,1,0:T(1,128)S(1)} %copy-done.156, ...), custom_call_target="tpu_custom_call" | custom-call | flops 3690987520 | bytes 5767168 | tf_op jit(solution)/shard_map/pallas_call | solution.py:209
  1179.1 4.0 convolution_convert_fusion
  1183.2 4.0 fusion.95
  1187.1 8.8 concatenate.104
  1201.7 4.6 all-to-all-start
  1208.2 4.0 slice.706.refs_1_
  1219.7 5.6 all-to-all-done
  1228.7 56.2 %back_last.3 = (f32[256,1408]{1,0:T(8,128)}, f32[1,1408]{1,0:T(1,128)S(1)}, f32[1,1408]{1,0:T(1,128)S(1)}, bf16[1,352,768]{2,1,0:T(8,128)(2,1)S(1)}, bf16[1,352,...) custom-call(bf16[1056,1024]{1,0:T(8,128)(2,1)} %copy-done.176, ...), custom_call_target="tpu_custom_call" | custom-call | flops 7208960 | bytes 4325376 | tf_op jit(solution)/shard_map/back_last/pallas_call | solution.py:651
  1290.1 13.3 skip_back.3
  1333.9 38.7 %gains.1 = (f32[4,2,136,128]{3,2,1,0:T(8,128)S(1)}, bf16[352,768]{1,0:T(8,128)(2,1)S(1)}) custom-call(f32[136,128]{1,0:T(8,128)S(1)} %pad_bitcast_fusion.refs_0_, bf16[352,768]{1,0:T(8,128)(2,1)S(1)} %fusion.50.refs_1_), custom_call_target="tpu_custom_call" | custom-call | tf_op jit(solution)/shard_map/gains/pallas_call | solution.py:813
  1389.0 49.0 %last.3 = (f32[256,1408]{1,0:T(8,128)S(1)}, bf16[1,2,176,704]{3,2,1,0:T(8,128)(2,1)S(1)}, bf16[352,704]{1,0:T(8,128)(2,1)S(1)}) custom-call(bf16[1024,768]{1,0:T(8,128)(2,1)} %get-tuple-element.504.refs_0_, bf16[1024,768]{1,0:T(8,128)(2,1)} %get-tuple-element.506.refs_1_, bf16[1408,768]{1,0:T(8,128)(2,1)} %bitcast.412, bf16[1408,768]{1,0:T(8,128)(2,1)} %bitcast.414, ...), custom_call_target="tpu_custom_call" | custom-call | flops 7208960 | bytes 4325376 | tf_op jit(solution)/shard_map/last/pallas_call | solution.py:651
  1451.1 8.1 collective-permute-done
  (785 shorter events, 242.6 us)
Async XLA Ops:
  7.2 207.5 %all-gather.13.cloned.1.call-start = ((), (), s32[]{:S(2)}) async-start(), calls=%async_computation.10 | async-start | bytes 4956160 | tf_op jit(solution)/shard_map/all_gather | solution.py:1072
  46.4 274.2 %all-gather.23.cloned.1.call-start = ((), (), s32[]{:S(2)}) async-start(), calls=%async_computation.21 | async-start | bytes 1548288 | tf_op jit(solution)/shard_map/all_gather | solution.py:1113
  52.4 95.5 %copy-start.228 = (bf16[2,333,128]{2,0,1:T(2,128)(2,1)S(1)}, bf16[2,333,128]{2,0,1:T(2,128)(2,1)}, u32[]{:S(2)}) copy-start(bf16[2,333,128]{2,0,1:T(2,128)(2,1)} %param.20) | copy-start | bytes 511492
  148.6 174.4 %all-gather.15.cloned.1.call-start = ((), (), s32[]{:S(2)}) async-start(), calls=%async_computation.11 | async-start | bytes 1966080 | tf_op jit(solution)/shard_map/all_gather | solution.py:1072
  150.9 174.9 %all-gather.11.cloned.1.call-start = ((), (), s32[]{:S(2)}) async-start(), calls=%async_computation.9 | async-start | bytes 2703360 | tf_op jit(solution)/shard_map/all_gather | solution.py:1072
  152.4 292.9 %all-gather.25.cloned.1.call-start = ((), (), s32[]{:S(2)}) async-start(), calls=%async_computation.22 | async-start | bytes 8921088 | tf_op jit(solution)/shard_map/all_gather | solution.py:1157
  155.0 8.1 copy-start.1
  156.1 9.3 copy-start.217
  166.2 47.1 %copy-start.143 = (f32[1,1408]{1,0:T(1,128)}, f32[1,1408]{1,0:T(1,128)S(1)}, u32[]{:S(2)}) copy-start(f32[1,1408]{1,0:T(1,128)S(1)} %get-tuple-element.490.refs_1_.refs_4_) | copy-start | bytes 16900
  166.3 74.7 %copy-start.145 = (f32[1,1408]{1,0:T(1,128)}, f32[1,1408]{1,0:T(1,128)S(1)}, u32[]{:S(2)}) copy-start(f32[1,1408]{1,0:T(1,128)S(1)} %get-tuple-element.489.refs_3_.refs_4_) | copy-start | bytes 16900
  214.7 117.9 %copy-start.19 = (f32[88,1024]{1,0:T(8,128)}, f32[88,1024]{1,0:T(8,128)S(1)}, u32[]{:S(2)}) copy-start(f32[88,1024]{1,0:T(8,128)S(1)} %get-tuple-element.499.cos_ref) | copy-start | bytes 1081348
  214.7 594.1 %copy-start.17 = (f32[88,1024]{1,0:T(8,128)}, f32[88,1024]{1,0:T(8,128)S(1)}, u32[]{:S(2)}) copy-start(f32[88,1024]{1,0:T(8,128)S(1)} %get-tuple-element.498.sin_ref) | copy-start | bytes 1081348
  222.2 8.9 copy-start.58
  222.3 8.9 copy-start.59
  222.3 8.9 copy-start.60
  222.3 10.1 copy-start.221
  232.1 8.9 copy-start.155
  232.1 260.0 %all-gather.19.cloned.1.call-start = ((), (), s32[]{:S(2)}) async-start(), calls=%async_computation.13 | async-start | bytes 4956160 | tf_op jit(solution)/shard_map/all_gather | solution.py:1072
  232.5 8.5 copy-start.99
  241.0 69.4 %copy-start.195 = (bf16[1,1,352,176]{3,2,1,0:T(8,128)(2,1)S(1)}, bf16[1,1,352,176]{3,2,1,0:T(8,128)(2,1)}, u32[]{:S(2)}) copy-start(bf16[1,1,352,176]{3,2,1,0:T(8,128)(2,1)} %copy.257) | copy-start | bytes 371716
  241.0 69.4 %copy-start.196 = (bf16[1,1,352,176]{3,2,1,0:T(8,128)(2,1)S(1)}, bf16[1,1,352,176]{3,2,1,0:T(8,128)(2,1)}, u32[]{:S(2)}) copy-start(bf16[1,1,352,176]{3,2,1,0:T(8,128)(2,1)} %copy.258) | copy-start | bytes 371716
  241.0 69.4 %copy-start.197 = (bf16[1,176,352]{1,2,0:T(8,128)(2,1)S(1)}, bf16[1,176,352]{1,2,0:T(8,128)(2,1)}, u32[]{:S(2)}) copy-start(bf16[1,176,352]{1,2,0:T(8,128)(2,1)} %copy.259) | copy-start | bytes 371716
  315.0 255.6 %all-gather.21.cloned.1.call-start = ((), (), s32[]{:S(2)}) async-start(), calls=%async_computation.14 | async-start | bytes 1966080 | tf_op jit(solution)/shard_map/all_gather | solution.py:1072
  337.3 53.8 %copy-start.102 = (bf16[352,1024]{1,0:T(8,128)(2,1)}, bf16[352,1024]{1,0:T(8,128)(2,1)S(1)}, u32[]{:S(2)}) copy-start(bf16[352,1024]{1,0:T(8,128)(2,1)S(1)} %get-tuple-element.161.refs_0_) | copy-start | bytes 2162692
  337.3 53.8 %copy-start.153 = (f32[4,1,1024]{2,1,0:T(1,128)}, f32[4,1,1024]{2,1,0:T(1,128)S(1)}, u32[]{:S(2)}) copy-start(f32[4,1,1024]{2,1,0:T(1,128)S(1)} %get-tuple-element.195.logsum_ref) | copy-start | bytes 49156
  337.3 53.7 %copy-start.183 = (bf16[2,2,352,768]{3,2,1,0:T(8,128)(2,1)S(1)}, bf16[2,2,352,768]{3,2,1,0:T(8,128)(2,1)}, u32[]{:S(2)}) copy-start(bf16[2,2,352,768]{3,2,1,0:T(8,128)(2,1)} %get-tuple-element.167) | copy-start | bytes 6488068
  447.7 40.3 %copy-start.212 = (bf16[1,1,256,176]{3,2,1,0:T(8,128)(2,1)S(1)}, bf16[1,1,256,176]{3,2,1,0:T(8,128)(2,1)}, u32[]{:S(2)}) copy-start(bf16[1,1,256,176]{3,2,1,0:T(8,128)(2,1)} %copy-done.211) | copy-start | bytes 270340
  447.7 40.3 %copy-start.214 = (bf16[1,1,256,176]{3,2,1,0:T(8,128)(2,1)S(1)}, bf16[1,1,256,176]{3,2,1,0:T(8,128)(2,1)}, u32[]{:S(2)}) copy-start(bf16[1,1,256,176]{3,2,1,0:T(8,128)(2,1)} %copy-done.213) | copy-start | bytes 270340
  455.6 33.7 %copy-start.2 = (f32[256,1408]{1,0:T(8,128)}, f32[256,1408]{1,0:T(8,128)S(1)}, u32[]{:S(2)}) copy-start(f32[256,1408]{1,0:T(8,128)S(1)} %get-tuple-element.174.refs_0_.refs_2_.refs_3_) | copy-start | bytes 4325380
  489.4 83.7 %all-gather.17.cloned.1.call-start = ((), (), s32[]{:S(2)}) async-start(), calls=%async_computation.12 | async-start | bytes 2703360 | tf_op jit(solution)/shard_map/all_gather | solution.py:1072
  492.0 476.2 %reduce-scatter.17.cloned.1.call-start = ((), (), s32[]{:S(2)}) async-start(), calls=%async_computation.17 | async-start | bytes 1966080 | tf_op jit(solution)/shard_map/reduce_scatter | solution.py:1217
  501.4 9.4 copy-start.65
  501.4 9.4 copy-start.66
  501.4 9.4 copy-start.67
  501.7 9.1 copy-start.95
  501.7 9.1 copy-start.97
  510.8 59.8 %copy-start.218 = (bf16[42,8,8,128]{3,1,2,0:T(8,128)(2,1)S(1)}, bf16[42,8,8,128]{3,1,2,0:T(8,128)(2,1)}, u32[]{:S(2)}) copy-start(bf16[42,8,8,128]{3,1,2,0:T(8,128)(2,1)} %copy.267) | copy-start | bytes 2064388
  583.6 41.7 %copy-start.185 = (bf16[2,2,352,768]{3,2,1,0:T(8,128)(2,1)S(1)}, bf16[2,2,352,768]{3,2,1,0:T(8,128)(2,1)}, u32[]{:S(2)}) copy-start(bf16[2,2,352,768]{3,2,1,0:T(8,128)(2,1)} %get-tuple-element.190) | copy-start | bytes 6488068
  652.0 46.2 %copy-start.190 = (bf16[1408,704]{1,0:T(8,128)(2,1)S(1)}, bf16[1408,704]{1,0:T(8,128)(2,1)}, u32[]{:S(2)}) copy-start(bf16[1408,704]{1,0:T(8,128)(2,1)} %all-gather.17.cloned.1.call-done) | copy-start | bytes 5947396
  714.4 255.0 %reduce-scatter.15.cloned.1.call-start = ((), (), s32[]{:S(2)}) async-start(), calls=%async_computation.16 | async-start | bytes 2703360 | tf_op jit(solution)/shard_map/reduce_scatter | solution.py:1217
  729.5 241.1 %reduce-scatter.13.cloned.1.call-start = ((), (), s32[]{:S(2)}) async-start(), calls=%async_computation.15 | async-start | bytes 4956160 | tf_op jit(solution)/shard_map/reduce_scatter | solution.py:1217
  848.0 124.1 %reduce-scatter.25.cloned.1.call-start = ((), (), s32[]{:S(2)}) async-start(), calls=%async_computation.23 | async-start | bytes 5406720
  853.8 58.8 %copy-start.3 = (bf16[2,352,768]{2,1,0:T(8,128)(2,1)}, bf16[2,352,768]{2,1,0:T(8,128)(2,1)S(1)}, u32[]{:S(2)}) copy-start(bf16[2,352,768]{2,1,0:T(8,128)(2,1)S(1)} %fusion.34.refs_6_) | copy-start | bytes 3244036
  855.8 56.8 %copy-start.4 = (bf16[1,2,352,768]{3,2,1,0:T(8,128)(2,1)}, bf16[1,2,352,768]{3,2,1,0:T(8,128)(2,1)S(1)}, u32[]{:S(2)}) copy-start(bf16[1,2,352,768]{3,2,1,0:T(8,128)(2,1)S(1)} %add_convert_fusion.2) | copy-start | bytes 3244036
  855.8 40.8 %copy-start.8 = (bf16[256,1408]{1,0:T(8,128)(2,1)S(1)}, bf16[256,1408]{1,0:T(8,128)(2,1)}, u32[]{:S(2)}) copy-start(bf16[256,1408]{1,0:T(8,128)(2,1)} %get-tuple-element.386.skip_ref) | copy-start | bytes 2162692
  912.5 312.7 %reduce-scatter.21.cloned.1.call-start = ((), (), s32[]{:S(2)}) async-start(), calls=%async_computation.19 | async-start | bytes 1966080 | tf_op jit(solution)/shard_map/reduce_scatter | solution.py:1217
  912.6 34.2 %copy-start.205 = (bf16[1024,768]{1,0:T(8,128)(2,1)S(1)}, bf16[1024,768]{1,0:T(8,128)(2,1)}, u32[]{:S(2)}) copy-start(bf16[1024,768]{1,0:T(8,128)(2,1)} %get-tuple-element.502.refs_1_) | copy-start | bytes 4718596
  946.8 12.3 copy-start.152
  973.3 82.5 %copy-start.188 = (bf16[1408,704]{1,0:T(8,128)(2,1)S(1)}, bf16[1408,704]{1,0:T(8,128)(2,1)}, u32[]{:S(2)}) copy-start(bf16[1408,704]{1,0:T(8,128)(2,1)} %all-gather.11.cloned.1.call-done) | copy-start | bytes 5947396
  1059.9 8.8 copy-start.220
  1072.6 153.8 %reduce-scatter.19.cloned.1.call-start = ((), (), s32[]{:S(2)}) async-start(), calls=%async_computation.18 | async-start | bytes 2703360 | tf_op jit(solution)/shard_map/reduce_scatter | solution.py:1217
  1087.3 298.8 %reduce-scatter.23.cloned.1.call-start = ((), (), s32[]{:S(2)}) async-start(), calls=%async_computation.20 | async-start | bytes 4956160 | tf_op jit(solution)/shard_map/reduce_scatter | solution.py:1217
  1151.7 63.0 %copy-start.45 = (bf16[1,352,768]{2,1,0:T(8,128)(2,1)}, bf16[1,352,768]{2,1,0:T(8,128)(2,1)S(1)}, u32[]{:S(2)}) copy-start(bf16[1,352,768]{2,1,0:T(8,128)(2,1)S(1)} %get-tuple-element.239) | copy-start | bytes 1622020
  1151.7 63.0 %copy-start.47 = (bf16[1,352,768]{2,1,0:T(8,128)(2,1)}, bf16[1,352,768]{2,1,0:T(8,128)(2,1)S(1)}, u32[]{:S(2)}) copy-start(bf16[1,352,768]{2,1,0:T(8,128)(2,1)S(1)} %get-tuple-element.238) | copy-start | bytes 1622020
  1201.7 23.6 %all-to-all-start = ((bf16[8,333,128]{2,1,0:T(8,128)(2,1)}), bf16[8,333,128]{2,1,0:T(8,128)(2,1)}, u32[]{:S(2)}, u32[]{:S(2)}) async-start(bf16[8,333,128]{2,1,0:T(8,128)(2,1)} %bitcast.366), calls=%async_computation.3 | async-start | bytes 1376256 | tf_op jit(solution)/shard_map/all_to_all | solution.py:1334
  1206.3 181.4 %reduce-scatter.27.cloned.1.call-start = ((), (), s32[]{:S(2)}) async-start(), calls=%async_computation.24 | async-start | bytes 5406720
  1219.4 8.2 copy-start.144
  1228.7 60.1 %copy-start.6 = (bf16[256,1408]{1,0:T(8,128)(2,1)S(1)}, bf16[256,1408]{1,0:T(8,128)(2,1)}, u32[]{:S(2)}) copy-start(bf16[256,1408]{1,0:T(8,128)(2,1)} %copy-done.5) | copy-start | bytes 2162692
  1228.7 60.1 %copy-start.142 = (f32[1,2816]{1,0:T(1,128)S(1)}, f32[1,2816]{1,0:T(1,128)}, u32[]{:S(2)}) copy-start(f32[1,2816]{1,0:T(1,128)} %copy-done.141) | copy-start | bytes 33796
  1333.6 41.9 %copy-start.233 = (bf16[8,352]{1,0:T(8,128)(2,1)S(1)}, bf16[8,352]{1,0:T(8,128)(2,1)}, u32[]{:S(2)}) copy-start(bf16[8,352]{1,0:T(8,128)(2,1)} %convert_element_type.574) | copy-start | bytes 16900
  1389.0 49.0 %copy-start.172 = (bf16[352,1408]{1,0:T(8,128)(2,1)S(1)}, bf16[352,1408]{1,0:T(8,128)(2,1)}, u32[]{:S(2)}) copy-start(bf16[352,1408]{1,0:T(8,128)(2,1)} %reduce-scatter.23.cloned.1.call-done) | copy-start | bytes 2973700
  1444.8 14.5 collective-permute-start
  1448.1 11.1 copy-start.164
  1448.1 12.1 copy-start.193
  (211 other events, 645.6 us)
Sparse Core Ops, SparseCore 0:
  46.5 50.7 all-gather.12
  148.7 32.0 all-gather.22
  183.3 30.1 all-gather.14
  215.8 37.9 all-gather.10
  257.2 87.9 all-gather.24
  346.8 60.0 all-gather.18
  489.5 30.5 all-gather.20
  522.6 48.8 all-gather.16
  714.5 30.0 reduce-scatter.16
  747.5 53.3 reduce-scatter.14
  848.1 61.2 reduce-scatter.12
  912.7 53.4 reduce-scatter.24
  1072.7 31.0 reduce-scatter.20
  1107.2 49.4 reduce-scatter.18
  1196.1 56.6 reduce-scatter.22
  1305.8 52.0 reduce-scatter.26

commit v5 on v4

--- a/solution.py
+++ b/solution.py
@@ -1334,10 +1334,6 @@
             blocks = lax.all_to_all(
                 blocks, ("lat", "chip", "core"), split_axis=0, concat_axis=0, tiled=True
             )
-            both, blocks = lax.optimization_barrier((both, blocks))
-            text_out = jnp.sum(
-                blocks.astype(F32).reshape((LATENTS, ranks) + blocks.shape[1:]), axis=1
-            )
             riders += [swap(cross_sum[1]), swap(text_sum[1])]
         grad_one, gain_self, shift_own, *others = back_last_tokens(
             (True, [both], [weight[:, : 3 * wide]]),
@@ -1346,6 +1342,11 @@
             attn_gain[layer, 0:1],
             riders,
         )
+        if layer == 0:
+            grad_one, blocks = lax.optimization_barrier((grad_one, blocks))
+            text_out = jnp.sum(
+                blocks.astype(F32).reshape((LATENTS, ranks) + blocks.shape[1:]), axis=1
+            )
         down_sum = added_two(downs, others[:2])
         up_grad = up_mine + others[2].astype(F32)
         early = others[3:]

time: 1480 us -> 1470 us (level)
    unnamed x556 -> x544, local copies, waits for them, and re-layouts: 87.1 us -> 87.3 us
  transfers between devices with their start and end apart: 18 -> 18, of which waited for: 2 -> 1; matrix products, arithmetic and copies ran while one was open for 18% -> 18% of each run, Pallas kernels for 52% -> 53%
where the time goes in v5:
time: 1470 us; the launch traced here: 1460 us
  Pallas kernels  1040 us (71%)
  local copies, waits for them, and re-layouts  165 us (11%)
  matrix products  146 us (10%)
  other arithmetic  77.3 us (5%)
  between operations  17.7 us (1%)
    pallas_call x16, Pallas kernels, token_call(): pl.pallas_call(functools.partial(token_kernel, sums, spreads, body, len(i...  854 us
    dot_general x40, matrix products, dot(): lax.dot_general(left, right, (((left_dim,), (right_dim,)), ((), ())), pre...  146 us
    unnamed x544, local copies, waits for them, and re-layouts  87.3 us
    pallas_call x4, Pallas kernels, attention_back(): pl.pallas_call(functools.partial(attention_back_kernel, count, turn), gri...  48.8 us
    pallas_call x4, Pallas kernels, local_call(): pl.pallas_call(body, out_shape=shapes, in_specs=[pl.BlockSpec(memory_spac...  40.6 us
    pallas_call x1, Pallas kernels, end_call(): pl.pallas_call(functools.partial(end_kernel, modes), out_shape=[jax.Shape...  38.4 us
    pallas_call x1, Pallas kernels, start_call(): pl.pallas_call(functools.partial(start_kernel, modes), out_shape=[jax.Sha...  31.6 us
  transfers between devices with their start and end apart: 18, of which 1 were waited for; matrix products, arithmetic and copies ran while one was open for 18% of the time, Pallas kernels for 53%

profile of v5, /device:TPU:0, one launch (start us, length us, event | category | flops | bytes accessed | tf_op | source)
XLA Modules:
  0.0 1464.7 jit_solution(14197196294939964891)
XLA Ops:
  11.3 31.6 %shift.1 = (f32[4,8,384]{2,1,0:T(8,128)S(1)}, f32[8,8,256]{2,1,0:T(8,128)S(1)}, bf16[352,704]{1,0:T(8,128)(2,1)S(1)}) custom-call(f32[4,8,384]{2,1,0:T(8,128)S(1)} %fusion.62.refs_0_, bf16[2,384,256]{2,1,0:T(8,128)(2,1)S(1)} %pad.20.refs_1_, bf16[352,704]{1,0:T(8,128)(2,1)S(1)} %pad_maximum_fusion.14.refs_2_), custom_call_target="tpu_custom_call" | custom-call | tf_op jit(solution)/shard_map/shift/pallas_call | solution.py:739
  53.3 94.6 %spread.2 = (bf16[4,256,1408]{2,1,0:T(8,128)(2,1)}, bf16[352,352]{1,0:T(8,128)(2,1)S(1)}, bf16[256,352]{1,0:T(8,128)(2,1)S(1)}, bf16[2,352,768]{2,1,0:T(8,128)(2,1)S(1)}, bf16[4,8,176,704]{3,2,1,0:T(8,128)(2,1)}) custom-call(f32[256,1408]{1,0:T(8,128)S(1)} %convert_element_type.483.refs_0_.refs_4_, bf16[352,352]{1,0:T(8,128)(2,1)S(1)} %pad_maximum_fusion.21.refs_1_, ...), custom_call_target="tpu_custom_call" | custom-call | flops 7208960 | bytes 4325376 | tf_op jit(solution)/shard_map/spread/pallas_call | solution.py:651
  156.1 7.0 skip.2
  166.3 44.1 %first.2 = (bf16[4,256,1408]{2,1,0:T(8,128)(2,1)}, bf16[2,352,768]{2,1,0:T(8,128)(2,1)S(1)}, bf16[2,352,768]{2,1,0:T(8,128)(2,1)S(1)}, bf16[2,352,768]{2,1,0:T(8,128)(2,1)S(1)}) custom-call(f32[256,1408]{1,0:T(8,128)} %copy-done, f32[1,1408]{1,0:T(1,128)S(1)} %get-tuple-element.490.refs_1_.refs_4_, f32[1,1408]{1,0:T(1,128)S(1)} %slice.566.refs_2_, ...), custom_call_target="tpu_custom_call" | custom-call | flops 7208960 | bytes 4325376 | tf_op jit(solution)/shard_map/first/pallas_call | solution.py:651
  214.8 6.9 fusion.91
  222.3 8.9 shard_map.288
  241.1 69.4 %middle.4 = (f32[256,1408]{1,0:T(8,128)}, bf16[4,256,1408]{2,1,0:T(8,128)(2,1)}, bf16[2,2,352,768]{3,2,1,0:T(8,128)(2,1)}, bf16[2,2,352,768]{3,2,1,0:T(8,128)(2,...) custom-call(bf16[352,1024]{1,0:T(8,128)(2,1)S(1)} %copy-done.112, ...), custom_call_target="tpu_custom_call" | custom-call | flops 7208960 | bytes 4325376 | tf_op jit(solution)/shard_map/middle/pallas_call | solution.py:651
  332.7 4.6 shard_map.289
  337.4 53.7 %middle.5 = (f32[256,1408]{1,0:T(8,128)}, bf16[4,256,1408]{2,1,0:T(8,128)(2,1)}, bf16[2,2,352,768]{3,2,1,0:T(8,128)(2,1)}, bf16[2,2,352,768]{3,2,1,0:T(8,128)(2,1)}, bf16[2,352,768]{2,1,0:T(8,128)(2,1)S(1)}) custom-call(bf16[352,1024]{1,0:T(8,128)(2,1)S(1)} %get-tuple-element.161.refs_0_, bf16[1408,352]{1,0:T(8,128)(2,1)S(1)} %get-tuple-element.375.refs_1_, ...), custom_call_target="tpu_custom_call" | custom-call | flops 7208960 | bytes 4325376 | tf_op jit(solution)/shard_map/middle/pallas_call | solution.py:651
  391.2 7.0 multiply_convert_fusion.2
  398.2 4.6 multiply_convert_fusion.3
  402.8 39.5 %last.2 = (f32[256,1408]{1,0:T(8,128)}, bf16[2,352,768]{2,1,0:T(8,128)(2,1)S(1)}, bf16[2,352,768]{2,1,0:T(8,128)(2,1)S(1)}, bf16[2,352,768]{2,1,0:T(8,128)(2,1)S(1)}) custom-call(bf16[1024,768]{1,0:T(8,128)(2,1)} %get-tuple-element.500.refs_0_, bf16[1024,768]{1,0:T(8,128)(2,1)} %get-tuple-element.502.refs_1_, bf16[1408,768]{1,0:T(8,128)(2,1)} %bitcast.424, ...), custom_call_target="tpu_custom_call" | custom-call | flops 7208960 | bytes 4325376 | tf_op jit(solution)/shard_map/last/pallas_call | solution.py:651
  447.8 6.8 skip.3
  455.7 30.1 %first.3 = (bf16[4,256,1408]{2,1,0:T(8,128)(2,1)S(1)}, bf16[352,352]{1,0:T(8,128)(2,1)S(1)}, bf16[256,352]{1,0:T(8,128)(2,1)S(1)}) custom-call(f32[256,1408]{1,0:T(8,128)S(1)} %get-tuple-element.174.refs_0_.refs_2_.refs_3_, f32[1,1408]{1,0:T(1,128)S(1)} %get-tuple-element.491.refs_1_.refs_4_, f32[1,1408]{1,0:T(1,128)S(1)} %copy-done.147, ...), custom_call_target="tpu_custom_call" | custom-call | flops 7208960 | bytes 4325376 | tf_op jit(solution)/shard_map/first/pallas_call | solution.py:651
  493.9 6.9 fusion.89
  501.8 9.0 shard_map.290
  510.9 56.9 %middle.6 = (f32[256,1408]{1,0:T(8,128)}, bf16[4,256,1408]{2,1,0:T(8,128)(2,1)}, bf16[2,2,352,768]{3,2,1,0:T(8,128)(2,1)}, bf16[2,2,352,768]{3,2,1,0:T(8,128)(2,...) custom-call(bf16[352,1024]{1,0:T(8,128)(2,1)S(1)} %get-tuple-element.178.refs_0_, ...), custom_call_target="tpu_custom_call" | custom-call | flops 7208960 | bytes 4325376 | tf_op jit(solution)/shard_map/middle/pallas_call | solution.py:651
  573.2 3.9 fusion.83.query_ref
  577.1 4.6 shard_map.291
  583.6 41.7 %middle.7 = (f32[256,1408]{1,0:T(8,128)S(1)}, bf16[4,256,1408]{2,1,0:T(8,128)(2,1)}, bf16[2,2,352,768]{3,2,1,0:T(8,128)(2,1)}, bf16[2,2,352,768]{3,2,1,0:T(8,128)(2,1)}) custom-call(bf16[352,1024]{1,0:T(8,128)(2,1)S(1)} %get-tuple-element.184.refs_0_, bf16[1408,352]{1,0:T(8,128)(2,1)S(1)} %get-tuple-element.377.refs_1_, ...), custom_call_target="tpu_custom_call" | custom-call | flops 7208960 | bytes 4325376 | tf_op jit(solution)/shard_map/middle/pallas_call | solution.py:651
  625.3 6.6 multiply_convert_fusion
  632.0 3.9 fusion.19.refs_1_
  635.9 3.9 convolution_convert_fusion.8
  639.8 4.2 multiply_convert_fusion.1
  644.0 4.1 fusion.13.refs_0_
  648.1 3.9 convolution_convert_fusion.9
  651.9 45.0 %back.4 = (f32[256,1408]{1,0:T(8,128)S(1)}, f32[1,1408]{1,0:T(1,128)S(1)}, bf16[4,256,1408]{2,1,0:T(8,128)(2,1)}, bf16[1,2,352,768]{3,2,1,0:T(8,128)(2,1)S(1)}, bf16[1,2,352,768]{3,2,1,0:T(8,128)(2,1)S(1)}) custom-call(bf16[1024,768]{1,0:T(8,128)(2,1)} %copy-done.203, bf16[1024,768]{1,0:T(8,128)(2,1)} %copy-done.202, bf16[1408,768]{1,0:T(8,128)(2,1)} %bitcast.420, ...), custom_call_target="tpu_custom_call" | custom-call | flops 7208960 | bytes 4325376 | tf_op jit(solution)/shard_map/back/pallas_call | solution.py:651
  698.1 4.5 convolution_convert_fusion.21.grad_ref
  702.7 7.7 shard_map.292
  714.5 3.7 convolution_convert_fusion.13
  723.3 6.2 convolution_convert_fusion.6
  734.9 5.7 convolution_convert_fusion.7
  740.6 62.9 %back.5 = (f32[256,1408]{1,0:T(8,128)}, f32[1,1408]{1,0:T(1,128)S(1)}, bf16[4,256,1408]{2,1,0:T(8,128)(2,1)}, bf16[1,352,768]{2,1,0:T(8,128)(2,1)S(1)}, bf16[1,3...) custom-call(bf16[352,1024]{1,0:T(8,128)(2,1)S(1)} %copy-done.115, ...), custom_call_target="tpu_custom_call" | custom-call | flops 7208960 | bytes 4325376 | tf_op jit(solution)/shard_map/back/pallas_call | solution.py:651
  803.6 5.2 convolution_convert_fusion.20.grad_ref
  808.9 16.7 %shard_map.293 = (bf16[352,1024]{1,0:T(8,128)(2,1)S(1)}, bf16[352,1024]{1,0:T(8,128)(2,1)S(1)}, bf16[352,1024]{1,0:T(8,128)(2,1)S(1)}) custom-call(f32[352,1024]{1,0:T(8,128)S(1)} %copy-done.68, f32[352,1024]{1,0:T(8,128)} %copy-done.66, f32[352,1024]{1,0:T(8,128)} %copy-done.65, f32[4,1,1024]{2,1,0:T(1,128)S(1)} %get-tuple-element.196.logsum_ref, ...), custom_call_target="tpu_custom_call" | custom-call | flops 3690987520 | bytes 5767168 | tf_op jit(solution)/shard_map/pallas_call | solution.py:209
  831.7 4.0 convolution_convert_fusion.1
  835.7 3.7 fusion.96
  839.5 8.5 concatenate.93
  848.3 4.0 slice.734.refs_1_
  855.9 38.5 %back_last.2 = (f32[256,1408]{1,0:T(8,128)S(1)}, f32[1,1408]{1,0:T(1,128)S(1)}, f32[1,1408]{1,0:T(1,128)S(1)}, bf16[1,352,768]{2,1,0:T(8,128)(2,1)S(1)}, bf16[1,...) custom-call(bf16[1056,1024]{1,0:T(8,128)(2,1)} %copy-done.176, bf16[1408,1056]{1,0:T(8,128)(2,1)} %slice.734.refs_1_, ...), custom_call_target="tpu_custom_call" | custom-call | flops 7208960 | bytes 4325376 | tf_op jit(solution)/shard_map/back_last/pallas_call | solution.py:651
  896.7 13.6 skip_back.2
  914.4 32.5 %spread.3 = (bf16[4,256,1408]{2,1,0:T(8,128)(2,1)S(1)}, bf16[352,768]{1,0:T(8,128)(2,1)S(1)}) custom-call(f32[256,1408]{1,0:T(8,128)S(1)} %copy-done.13, bf16[352,768]{1,0:T(8,128)(2,1)S(1)} %fusion.48.refs_1_), custom_call_target="tpu_custom_call" | custom-call | flops 7208960 | bytes 4325376 | tf_op jit(solution)/shard_map/spread/pallas_call | solution.py:651
  947.0 3.9 convolution_convert_fusion.2
  951.5 3.9 fusion.31.refs_1_
  955.4 3.8 convolution_convert_fusion.4
  959.3 4.1 fusion.25.refs_0_
  964.5 3.8 convolution_convert_fusion.5
  973.4 79.3 %back.6 = (f32[256,1408]{1,0:T(8,128)}, f32[1,1408]{1,0:T(1,128)S(1)}, bf16[4,256,1408]{2,1,0:T(8,128)(2,1)}, bf16[1,2,352,768]{3,2,1,0:T(8,128)(2,1)S(1)}, bf16...) custom-call(bf16[1024,768]{1,0:T(8,128)(2,1)} %copy-done.201, ...), custom_call_target="tpu_custom_call" | custom-call | flops 7208960 | bytes 4325376 | tf_op jit(solution)/shard_map/back/pallas_call | solution.py:651
  1056.0 3.9 convolution_convert_fusion.19.grad_ref
  1060.0 7.8 shard_map.294
  1072.8 6.2 convolution_convert_fusion.3
  1092.3 58.4 %back.7 = (f32[256,1408]{1,0:T(8,128)}, f32[1,1408]{1,0:T(1,128)S(1)}, bf16[4,256,1408]{2,1,0:T(8,128)(2,1)}, bf16[1,352,768]{2,1,0:T(8,128)(2,1)S(1)}, bf16[1,3...) custom-call(bf16[352,1024]{1,0:T(8,128)(2,1)S(1)} %copy-done.110, ...), custom_call_target="tpu_custom_call" | custom-call | flops 7208960 | bytes 4325376 | tf_op jit(solution)/shard_map/back/pallas_call | solution.py:651
  1151.7 5.0 convolution_convert_fusion.18.grad_ref
  1156.8 16.6 %shard_map.295 = (bf16[352,1024]{1,0:T(8,128)(2,1)S(1)}, bf16[352,1024]{1,0:T(8,128)(2,1)S(1)}, bf16[352,1024]{1,0:T(8,128)(2,1)S(1)}) custom-call(f32[352,1024]{1,0:T(8,128)S(1)} %copy-done.61, f32[352,1024]{1,0:T(8,128)} %copy-done.59, f32[352,1024]{1,0:T(8,128)} %copy-done.58, f32[4,1,1024]{2,1,0:T(1,128)S(1)} %copy-done.155, ...), custom_call_target="tpu_custom_call" | custom-call | flops 3690987520 | bytes 5767168 | tf_op jit(solution)/shard_map/pallas_call | solution.py:209
  1179.2 4.0 convolution_convert_fusion
  1183.2 3.9 fusion.95
  1187.1 8.8 concatenate.104
  1196.8 3.9 slice.706.refs_1_
  1205.5 4.6 all-to-all-start
  1219.4 57.7 %back_last.3 = (f32[256,1408]{1,0:T(8,128)}, f32[1,1408]{1,0:T(1,128)S(1)}, f32[1,1408]{1,0:T(1,128)S(1)}, bf16[1,352,768]{2,1,0:T(8,128)(2,1)S(1)}, bf16[1,352,...) custom-call(bf16[1056,1024]{1,0:T(8,128)(2,1)} %copy-done.175, ...), custom_call_target="tpu_custom_call" | custom-call | flops 7208960 | bytes 4325376 | tf_op jit(solution)/shard_map/back_last/pallas_call | solution.py:651
  1283.4 13.2 skip_back.3
  1324.5 38.4 %gains.1 = (f32[4,2,136,128]{3,2,1,0:T(8,128)S(1)}, bf16[352,768]{1,0:T(8,128)(2,1)S(1)}) custom-call(f32[136,128]{1,0:T(8,128)S(1)} %pad_bitcast_fusion.refs_0_, bf16[352,768]{1,0:T(8,128)(2,1)S(1)} %fusion.50.refs_1_), custom_call_target="tpu_custom_call" | custom-call | tf_op jit(solution)/shard_map/gains/pallas_call | solution.py:813
  1381.6 50.1 %last.3 = (f32[256,1408]{1,0:T(8,128)S(1)}, bf16[1,2,176,704]{3,2,1,0:T(8,128)(2,1)S(1)}, bf16[352,704]{1,0:T(8,128)(2,1)S(1)}) custom-call(bf16[1024,768]{1,0:T(8,128)(2,1)} %get-tuple-element.504.refs_0_, bf16[1024,768]{1,0:T(8,128)(2,1)} %get-tuple-element.506.refs_1_, bf16[1408,768]{1,0:T(8,128)(2,1)} %bitcast.412, bf16[1408,768]{1,0:T(8,128)(2,1)} %bitcast.414, ...), custom_call_target="tpu_custom_call" | custom-call | flops 7208960 | bytes 4325376 | tf_op jit(solution)/shard_map/last/pallas_call | solution.py:651
  1443.7 9.9 collective-permute-done
  (773 shorter events, 235.1 us)
Async XLA Ops:
  7.2 207.6 %all-gather.13.cloned.1.call-start = ((), (), s32[]{:S(2)}) async-start(), calls=%async_computation.10 | async-start | bytes 4956160 | tf_op jit(solution)/shard_map/all_gather | solution.py:1072
  46.4 274.2 %all-gather.23.cloned.1.call-start = ((), (), s32[]{:S(2)}) async-start(), calls=%async_computation.21 | async-start | bytes 1548288 | tf_op jit(solution)/shard_map/all_gather | solution.py:1113
  52.4 95.5 %copy-start.227 = (bf16[2,333,128]{2,0,1:T(2,128)(2,1)S(1)}, bf16[2,333,128]{2,0,1:T(2,128)(2,1)}, u32[]{:S(2)}) copy-start(bf16[2,333,128]{2,0,1:T(2,128)(2,1)} %param.20) | copy-start | bytes 511492
  148.7 174.4 %all-gather.15.cloned.1.call-start = ((), (), s32[]{:S(2)}) async-start(), calls=%async_computation.11 | async-start | bytes 1966080 | tf_op jit(solution)/shard_map/all_gather | solution.py:1072
  150.9 174.9 %all-gather.11.cloned.1.call-start = ((), (), s32[]{:S(2)}) async-start(), calls=%async_computation.9 | async-start | bytes 2703360 | tf_op jit(solution)/shard_map/all_gather | solution.py:1072
  152.4 292.9 %all-gather.25.cloned.1.call-start = ((), (), s32[]{:S(2)}) async-start(), calls=%async_computation.22 | async-start | bytes 8921088 | tf_op jit(solution)/shard_map/all_gather | solution.py:1157
  155.1 8.1 copy-start.1
  156.1 9.3 copy-start.216
  166.3 47.1 %copy-start.142 = (f32[1,1408]{1,0:T(1,128)}, f32[1,1408]{1,0:T(1,128)S(1)}, u32[]{:S(2)}) copy-start(f32[1,1408]{1,0:T(1,128)S(1)} %get-tuple-element.490.refs_1_.refs_4_) | copy-start | bytes 16900
  166.3 74.7 %copy-start.144 = (f32[1,1408]{1,0:T(1,128)}, f32[1,1408]{1,0:T(1,128)S(1)}, u32[]{:S(2)}) copy-start(f32[1,1408]{1,0:T(1,128)S(1)} %get-tuple-element.489.refs_3_.refs_4_) | copy-start | bytes 16900
  214.8 117.9 %copy-start.19 = (f32[88,1024]{1,0:T(8,128)}, f32[88,1024]{1,0:T(8,128)S(1)}, u32[]{:S(2)}) copy-start(f32[88,1024]{1,0:T(8,128)S(1)} %get-tuple-element.499.cos_ref) | copy-start | bytes 1081348
  214.8 594.1 %copy-start.17 = (f32[88,1024]{1,0:T(8,128)}, f32[88,1024]{1,0:T(8,128)S(1)}, u32[]{:S(2)}) copy-start(f32[88,1024]{1,0:T(8,128)S(1)} %get-tuple-element.498.sin_ref) | copy-start | bytes 1081348
  222.3 8.9 copy-start.58
  222.3 8.9 copy-start.59
  222.3 8.9 copy-start.60
  222.3 10.1 copy-start.220
  232.1 8.9 copy-start.154
  232.1 260.0 %all-gather.19.cloned.1.call-start = ((), (), s32[]{:S(2)}) async-start(), calls=%async_computation.13 | async-start | bytes 4956160 | tf_op jit(solution)/shard_map/all_gather | solution.py:1072
  232.6 8.5 copy-start.99
  241.0 69.4 %copy-start.194 = (bf16[1,1,352,176]{3,2,1,0:T(8,128)(2,1)S(1)}, bf16[1,1,352,176]{3,2,1,0:T(8,128)(2,1)}, u32[]{:S(2)}) copy-start(bf16[1,1,352,176]{3,2,1,0:T(8,128)(2,1)} %copy.257) | copy-start | bytes 371716
  241.0 69.4 %copy-start.195 = (bf16[1,1,352,176]{3,2,1,0:T(8,128)(2,1)S(1)}, bf16[1,1,352,176]{3,2,1,0:T(8,128)(2,1)}, u32[]{:S(2)}) copy-start(bf16[1,1,352,176]{3,2,1,0:T(8,128)(2,1)} %copy.258) | copy-start | bytes 371716
  241.0 69.4 %copy-start.196 = (bf16[1,176,352]{1,2,0:T(8,128)(2,1)S(1)}, bf16[1,176,352]{1,2,0:T(8,128)(2,1)}, u32[]{:S(2)}) copy-start(bf16[1,176,352]{1,2,0:T(8,128)(2,1)} %copy.259) | copy-start | bytes 371716
  315.0 255.6 %all-gather.21.cloned.1.call-start = ((), (), s32[]{:S(2)}) async-start(), calls=%async_computation.14 | async-start | bytes 1966080 | tf_op jit(solution)/shard_map/all_gather | solution.py:1072
  337.3 53.8 %copy-start.102 = (bf16[352,1024]{1,0:T(8,128)(2,1)}, bf16[352,1024]{1,0:T(8,128)(2,1)S(1)}, u32[]{:S(2)}) copy-start(bf16[352,1024]{1,0:T(8,128)(2,1)S(1)} %get-tuple-element.161.refs_0_) | copy-start | bytes 2162692
  337.3 53.8 %copy-start.152 = (f32[4,1,1024]{2,1,0:T(1,128)}, f32[4,1,1024]{2,1,0:T(1,128)S(1)}, u32[]{:S(2)}) copy-start(f32[4,1,1024]{2,1,0:T(1,128)S(1)} %get-tuple-element.195.logsum_ref) | copy-start | bytes 49156
  337.4 53.8 %copy-start.182 = (bf16[2,2,352,768]{3,2,1,0:T(8,128)(2,1)S(1)}, bf16[2,2,352,768]{3,2,1,0:T(8,128)(2,1)}, u32[]{:S(2)}) copy-start(bf16[2,2,352,768]{3,2,1,0:T(8,128)(2,1)} %get-tuple-element.167) | copy-start | bytes 6488068
  447.8 7.9 copy-start.101
  447.8 7.9 copy-start.147
  447.8 40.3 %copy-start.211 = (bf16[1,1,256,176]{3,2,1,0:T(8,128)(2,1)S(1)}, bf16[1,1,256,176]{3,2,1,0:T(8,128)(2,1)}, u32[]{:S(2)}) copy-start(bf16[1,1,256,176]{3,2,1,0:T(8,128)(2,1)} %copy-done.210) | copy-start | bytes 270340
  447.8 40.3 %copy-start.213 = (bf16[1,1,256,176]{3,2,1,0:T(8,128)(2,1)S(1)}, bf16[1,1,256,176]{3,2,1,0:T(8,128)(2,1)}, u32[]{:S(2)}) copy-start(bf16[1,1,256,176]{3,2,1,0:T(8,128)(2,1)} %copy-done.212) | copy-start | bytes 270340
  455.7 33.7 %copy-start.2 = (f32[256,1408]{1,0:T(8,128)}, f32[256,1408]{1,0:T(8,128)S(1)}, u32[]{:S(2)}) copy-start(f32[256,1408]{1,0:T(8,128)S(1)} %get-tuple-element.174.refs_0_.refs_2_.refs_3_) | copy-start | bytes 4325380
  489.5 83.7 %all-gather.17.cloned.1.call-start = ((), (), s32[]{:S(2)}) async-start(), calls=%async_computation.12 | async-start | bytes 2703360 | tf_op jit(solution)/shard_map/all_gather | solution.py:1072
  492.1 476.3 %reduce-scatter.17.cloned.1.call-start = ((), (), s32[]{:S(2)}) async-start(), calls=%async_computation.17 | async-start | bytes 1966080 | tf_op jit(solution)/shard_map/reduce_scatter | solution.py:1217
  501.4 9.4 copy-start.65
  501.5 9.4 copy-start.66
  501.5 9.4 copy-start.67
  501.8 9.1 copy-start.95
  501.8 9.1 copy-start.97
  510.9 59.7 %copy-start.217 = (bf16[42,8,8,128]{3,1,2,0:T(8,128)(2,1)S(1)}, bf16[42,8,8,128]{3,1,2,0:T(8,128)(2,1)}, u32[]{:S(2)}) copy-start(bf16[42,8,8,128]{3,1,2,0:T(8,128)(2,1)} %copy.267) | copy-start | bytes 2064388
  583.6 41.7 %copy-start.184 = (bf16[2,2,352,768]{3,2,1,0:T(8,128)(2,1)S(1)}, bf16[2,2,352,768]{3,2,1,0:T(8,128)(2,1)}, u32[]{:S(2)}) copy-start(bf16[2,2,352,768]{3,2,1,0:T(8,128)(2,1)} %get-tuple-element.190) | copy-start | bytes 6488068
  651.9 46.2 %copy-start.189 = (bf16[1408,704]{1,0:T(8,128)(2,1)S(1)}, bf16[1408,704]{1,0:T(8,128)(2,1)}, u32[]{:S(2)}) copy-start(bf16[1408,704]{1,0:T(8,128)(2,1)} %all-gather.17.cloned.1.call-done) | copy-start | bytes 5947396
  702.7 7.8 copy-start.218
  714.4 255.1 %reduce-scatter.15.cloned.1.call-start = ((), (), s32[]{:S(2)}) async-start(), calls=%async_computation.16 | async-start | bytes 2703360 | tf_op jit(solution)/shard_map/reduce_scatter | solution.py:1217
  729.5 241.2 %reduce-scatter.13.cloned.1.call-start = ((), (), s32[]{:S(2)}) async-start(), calls=%async_computation.15 | async-start | bytes 4956160 | tf_op jit(solution)/shard_map/reduce_scatter | solution.py:1217
  848.0 124.2 %reduce-scatter.25.cloned.1.call-start = ((), (), s32[]{:S(2)}) async-start(), calls=%async_computation.23 | async-start | bytes 5406720
  853.8 58.9 %copy-start.3 = (bf16[2,352,768]{2,1,0:T(8,128)(2,1)}, bf16[2,352,768]{2,1,0:T(8,128)(2,1)S(1)}, u32[]{:S(2)}) copy-start(bf16[2,352,768]{2,1,0:T(8,128)(2,1)S(1)} %fusion.34.refs_6_) | copy-start | bytes 3244036
  855.8 56.9 %copy-start.4 = (bf16[1,2,352,768]{3,2,1,0:T(8,128)(2,1)}, bf16[1,2,352,768]{3,2,1,0:T(8,128)(2,1)S(1)}, u32[]{:S(2)}) copy-start(bf16[1,2,352,768]{3,2,1,0:T(8,128)(2,1)S(1)} %add_convert_fusion.2) | copy-start | bytes 3244036
  855.8 40.9 %copy-start.8 = (bf16[256,1408]{1,0:T(8,128)(2,1)S(1)}, bf16[256,1408]{1,0:T(8,128)(2,1)}, u32[]{:S(2)}) copy-start(bf16[256,1408]{1,0:T(8,128)(2,1)} %get-tuple-element.386.skip_ref) | copy-start | bytes 2162692
  912.6 303.2 %reduce-scatter.21.cloned.1.call-start = ((), (), s32[]{:S(2)}) async-start(), calls=%async_computation.19 | async-start | bytes 1966080 | tf_op jit(solution)/shard_map/reduce_scatter | solution.py:1217
  912.7 34.2 %copy-start.204 = (bf16[1024,768]{1,0:T(8,128)(2,1)S(1)}, bf16[1024,768]{1,0:T(8,128)(2,1)}, u32[]{:S(2)}) copy-start(bf16[1024,768]{1,0:T(8,128)(2,1)} %get-tuple-element.502.refs_1_) | copy-start | bytes 4718596
  946.9 12.3 copy-start.151
  973.4 82.5 %copy-start.187 = (bf16[1408,704]{1,0:T(8,128)(2,1)S(1)}, bf16[1408,704]{1,0:T(8,128)(2,1)}, u32[]{:S(2)}) copy-start(bf16[1408,704]{1,0:T(8,128)(2,1)} %all-gather.11.cloned.1.call-done) | copy-start | bytes 5947396
  1060.0 8.8 copy-start.219
  1072.7 144.3 %reduce-scatter.19.cloned.1.call-start = ((), (), s32[]{:S(2)}) async-start(), calls=%async_computation.18 | async-start | bytes 2703360 | tf_op jit(solution)/shard_map/reduce_scatter | solution.py:1217
  1087.5 291.2 %reduce-scatter.23.cloned.1.call-start = ((), (), s32[]{:S(2)}) async-start(), calls=%async_computation.20 | async-start | bytes 4956160 | tf_op jit(solution)/shard_map/reduce_scatter | solution.py:1217
  1151.7 58.8 %copy-start.45 = (bf16[1,352,768]{2,1,0:T(8,128)(2,1)}, bf16[1,352,768]{2,1,0:T(8,128)(2,1)S(1)}, u32[]{:S(2)}) copy-start(bf16[1,352,768]{2,1,0:T(8,128)(2,1)S(1)} %get-tuple-element.236) | copy-start | bytes 1622020
  1151.7 58.8 %copy-start.47 = (bf16[1,352,768]{2,1,0:T(8,128)(2,1)}, bf16[1,352,768]{2,1,0:T(8,128)(2,1)S(1)}, u32[]{:S(2)}) copy-start(bf16[1,352,768]{2,1,0:T(8,128)(2,1)S(1)} %get-tuple-element.235) | copy-start | bytes 1622020
  1205.5 75.5 %all-to-all-start = ((bf16[8,333,128]{2,1,0:T(8,128)(2,1)}), bf16[8,333,128]{2,1,0:T(8,128)(2,1)}, u32[]{:S(2)}, u32[]{:S(2)}) async-start(bf16[8,333,128]{2,1,0:T(8,128)(2,1)} %bitcast.366), calls=%async_computation.5 | async-start | bytes 1376256 | tf_op jit(solution)/shard_map/all_to_all | solution.py:1334
  1210.1 170.2 %reduce-scatter.27.cloned.1.call-start = ((), (), s32[]{:S(2)}) async-start(), calls=%async_computation.24 | async-start | bytes 5406720
  1219.4 61.6 %copy-start.141 = (f32[1,2816]{1,0:T(1,128)S(1)}, f32[1,2816]{1,0:T(1,128)}, u32[]{:S(2)}) copy-start(f32[1,2816]{1,0:T(1,128)} %copy-done.140) | copy-start | bytes 33796
  1381.6 50.1 %copy-start.171 = (bf16[352,1408]{1,0:T(8,128)(2,1)S(1)}, bf16[352,1408]{1,0:T(8,128)(2,1)}, u32[]{:S(2)}) copy-start(bf16[352,1408]{1,0:T(8,128)(2,1)} %reduce-scatter.23.cloned.1.call-done) | copy-start | bytes 2973700
  1438.4 15.2 %collective-permute-start = (bf16[176,704]{1,0:T(8,128)(2,1)}, bf16[176,704]{1,0:T(8,128)(2,1)}, u32[]{:S(2)}, u32[]{:S(2)}) collective-permute-start(bf16[176,704]{1,0:T(8,128)(2,1)} %fusion.55), channel_id=1, source_target_pairs={{0,4},{4,0},{1,5},{5,1},{2,6},{6,2},{3,7},{7,3},{8,12},{12,8},{9,1... | collective-permute-start | bytes 743432 | tf_op jit(solution)/shard_map/ppermute | solution.py:1388
  1440.7 12.9 copy-start.163
  1440.7 13.9 copy-start.192
  (205 other events, 593.0 us)
Sparse Core Ops, SparseCore 0:
  46.6 50.7 all-gather.12
  148.8 32.0 all-gather.22
  183.3 30.1 all-gather.14
  215.8 37.9 all-gather.10
  257.2 88.0 all-gather.24
  347.0 60.0 all-gather.18
  489.6 30.5 all-gather.20
  522.6 48.8 all-gather.16
  714.5 30.0 reduce-scatter.16
  747.5 53.3 reduce-scatter.14
  848.1 61.3 reduce-scatter.12
  912.7 53.4 reduce-scatter.24
  1072.9 30.8 reduce-scatter.20
  1107.2 49.3 reduce-scatter.18
  1196.1 59.8 reduce-scatter.22
  1299.0 52.9 reduce-scatter.26
